TPU v7x, 32 devices: a whole 2x2x4 slice. The times are simulated.
32 devices in a mesh: ctx: 8 (over z, core), exp: 4 (over y, x).
Axes of the slice: x: 2, y: 2, z: 4, core: 2. Of those that a mesh axis runs over, the one named last changes fastest.
Arguments:
- tokens: bfloat16 [6144, 2048], P(('ctx', 'exp')), may hold values from -6 to 6
- expert_ids: int32 [6144, 1], P(('ctx', 'exp')), may hold values from 0 to 1; in each aligned block of 192 rows (0 to 191, 192 to 383, ...) at most 144 rows name the same one
- damping: bfloat16 [6144], P(('ctx', 'exp')), may hold values from 0 to 0.5, as said below
- in_weight: bfloat16 [4, 2048, 2, 1024], P('exp', 'ctx'), may hold values from -0.125 to 0.125
- out_weight: bfloat16 [4, 1024, 2048], P('exp', None, 'ctx'), may hold values from -0.125 to 0.125
- w_bc: bfloat16 [2048, 256], replicated, may hold values from -0.125 to 0.125
- w_dt: bfloat16 [32, 2048], replicated, may hold values from -0.125 to 0.125
- rate: float32 [32], P('exp'), may hold values from 0 to 3, as said below
- dt_bias: float32 [32], P('exp'), may hold values from -5.5 to -3.5
- d_skip: float32 [32], P('exp'), may hold values from 0.5 to 2
- gain: float32 [2048], P('exp'), may hold values from 0.25 to 1.75
- conv_weight: float32 [4, 2048], P(None, 'exp'), may hold values from -3 to 3
Outputs:
- mixed: bfloat16 [6144, 2048], P(('ctx', 'exp'))
Inputs may be any that keep to these rules, and one draw needn't show every extreme that they name: `expert_ids`: among the 192 tokens of one device at most 144 name the same expert, and in every draw some device has an expert named by exactly 144 of its tokens. `damping`: Nonnegative. `rate`: Positive.
All inputs are finite; a program needn't handle non-finite values.
Results may differ from a plain program's by a relative error of at most 0.012.
Values may be sent and summed in bfloat16 or wider, within the bound.
No kernel may reach another device: no remote copies, remote signals or barrier semaphores. Data moves between devices by JAX's collectives and lax.ppermute only.
A program may use at most 128 MiB of HBM per device.

v0:
```python
import functools

import jax
import jax.numpy as jnp
from jax import lax
from jax.experimental import pallas as pl
from jax.experimental.pallas import tpu as pltpu
from jax.sharding import PartitionSpec as P

both = ("ctx", "exp")
extra = 128
halo = 16
dt_lane, reach_lane = 16, 32
highest = lax.Precision.HIGHEST
f32, bf16 = jnp.float32, jnp.bfloat16


def params(mib):
    return pltpu.CompilerParams(vmem_limit_bytes=mib << 20)


def vmem(*shape):
    return pl.BlockSpec(shape, lambda *_: (0,) * len(shape), pipeline_mode=pl.Buffered(1))


def shift(array, move):
    groups = lax.axis_size("exp")
    pairs = []
    for c in range(lax.axis_size("ctx")):
        for e in range(groups):
            to = move(c // 2, c % 2, e)
            if to is not None:
                pairs.append((c * groups + e, (2 * to[0] + to[1]) * groups + to[2]))
    return lax.ppermute(array, both, pairs)


def line_gather(own, depth):
    if depth == 1:
        return [own], []
    first = shift(own, lambda z, k, e: ((z + 1) % depth, k, e))
    last = shift(own, lambda z, k, e: ((z - 1) % depth, k, e)) if depth > 2 else None
    ups, downs = [], []
    up, down = first, last
    for s in range(2, depth - 1):
        up = shift(up, lambda z, k, e: (z + 1, k, e) if s - 1 <= z < depth - 1 else None)
        down = shift(down, lambda z, k, e: (z - 1, k, e) if 0 < z <= depth - s else None)
        ups.append(up)
        downs.append(down)
    middle = [(ups[s - 2], downs[depth - s - 2]) for s in range(2, depth - 1)]
    return [own, first] + ([last] if depth > 2 else []), middle


def maps_kernel(heads, width, x_ref, w_ref, bias_ref, rate_ref, maps_ref, cols_ref, rows_ref, total):
    length = x_ref.shape[0]

    @pl.when(pl.program_id(0) == 0)
    def _():
        total[...] = jnp.zeros_like(total)

    found = jnp.dot(x_ref[:, :width], w_ref[...], preferred_element_type=f32).astype(bf16)
    state2 = maps_ref.shape[1]
    maps_ref[...] = found[:, :state2]
    raw = found[:, state2:].astype(f32) + bias_ref[...]
    steps = jnp.maximum(raw, 0.0) + jnp.log1p(jnp.exp(-jnp.abs(raw)))
    damping = x_ref[:, width : width + extra].astype(f32)[:, 1:2]
    logs = -(rate_ref[...] * steps + damping)
    row = lax.broadcasted_iota(jnp.int32, (length, length), 0)
    col = lax.broadcasted_iota(jnp.int32, (length, length), 1)
    lower = (row >= col).astype(f32)
    climb = jnp.dot(lower, logs, precision=highest, preferred_element_type=f32)
    lane = lax.broadcasted_iota(jnp.int32, climb.shape, 1)
    reach = climb + total[...]
    packed = jnp.where(lane < dt_lane, climb, jnp.where(lane < reach_lane, steps, reach))
    cols_ref[...] = packed
    rows_ref[...] = jnp.transpose(packed)[: rows_ref.shape[0]]
    total[...] = reach[length - 1 : length]


def maps(tokens, w_maps, bias, rate, heads, state2, length):
    count, width = tokens.shape[0], w_maps.shape[0]
    return pl.pallas_call(
        functools.partial(maps_kernel, heads, width),
        grid=(count // length,),
        in_specs=[
            pl.BlockSpec((length, tokens.shape[1]), lambda b: (b, 0)),
            vmem(*w_maps.shape),
            vmem(1, 128),
            vmem(1, 128),
        ],
        out_specs=[
            pl.BlockSpec((length, state2), lambda b: (b, 0)),
            pl.BlockSpec((length, 128), lambda b: (b, 0)),
            pl.BlockSpec((reach_lane, length), lambda b: (0, b)),
        ],
        out_shape=[
            jax.ShapeDtypeStruct((count, state2), bf16),
            jax.ShapeDtypeStruct((count, 128), f32),
            jax.ShapeDtypeStruct((reach_lane, count), f32),
        ],
        scratch_shapes=[pltpu.VMEM((1, 128), f32)],
        compiler_params=params(32),
        name="maps",
    )(tokens, w_maps, bias, rate)


def scan_kernel(
    first_head, head, experts, depth, width, near, middle, pos_ref, x_ref, edge_ref, *refs
):
    slots = refs[: near + 2 * middle]
    maps_ref, cols_ref, rows_ref, taps_ref, skip_ref = refs[near + 2 * middle :][:5]
    y_ref, gate_ref, final_ref, whole, seen, state = refs[near + 2 * middle + 5 :]
    length, channels = y_ref.shape
    taps = taps_ref.shape[0]
    width_state = maps_ref.shape[1] // 2
    step, z = pl.program_id(0), pos_ref[0]
    depth_rows = width // depth

    def place(ref, distance):
        rows = pl.ds(pl.multiple_of(lax.rem(z - distance + depth, depth) * depth_rows, 128), depth_rows)
        for e in range(experts):
            whole[e, rows, :] = ref[e * depth_rows : (e + 1) * depth_rows, :]

    def project(tokens):
        chosen = tokens[:, width : width + extra].astype(f32)[:, 0:1]
        total = jnp.dot(tokens[:, :width], whole[0], preferred_element_type=f32)
        for e in range(1, experts):
            other = jnp.dot(tokens[:, :width], whole[e], preferred_element_type=f32)
            total = jnp.where(chosen == e, other, total)
        total = total.astype(bf16)
        return total[:, :channels], total[:, channels:]

    @pl.when(step == 0)
    def _():
        for at, distance in zip(range(near), (0, 1, depth - 1)):
            place(slots[at], distance)
        for at in range(middle):
            distance = at + 2

            @pl.when(z >= distance)
            def _():
                place(slots[near + 2 * at], distance)

            @pl.when(z < distance)
            def _():
                place(slots[near + 2 * at + 1], distance)

        before, _ = project(edge_ref[...])
        seen[0:8, :] = before[halo - 8 :].astype(f32)
        state[...] = jnp.zeros_like(state)

    inner, gate = project(x_ref[...])
    gate_ref[...] = gate
    seen[8:, :] = inner.astype(f32)
    mixed = jnp.zeros((length, channels), f32)
    for tap in range(taps):
        mixed = mixed + taps_ref[tap : tap + 1, :] * seen[pl.ds(8 - (taps - 1) + tap, length), :]
    seen[0:8, :] = seen[pl.ds(length, 8), :]
    values = mixed / (1.0 + jnp.exp(-mixed))

    keys, queries = maps_ref[:, :width_state], maps_ref[:, width_state:]
    gram = lax.dot_general(queries, keys, (((1,), (1,)), ((), ())), preferred_element_type=f32)
    row = lax.broadcasted_iota(jnp.int32, (length, length), 0)
    col = lax.broadcasted_iota(jnp.int32, (length, length), 1)
    lower = row >= col
    gram = jnp.where(lower, gram, 0.0)
    lane = lax.broadcasted_iota(jnp.int32, (1, channels), 1)
    rounded = values.astype(bf16)
    inside, growth, ends, decay = [], 0.0, 0.0, 0.0
    reached = 0.0
    for j in range(channels // head):
        at = first_head + j
        mine = lane // head == j
        climb, size = cols_ref[:, at : at + 1], cols_ref[:, dt_lane + at : dt_lane + at + 1]
        climb_row, size_row = rows_ref[at : at + 1, :], rows_ref[dt_lane + at : dt_lane + at + 1, :]
        spread = jnp.exp(jnp.where(lower, climb - climb_row, 0.0)) * gram * size_row
        inside.append(
            jnp.dot(
                spread.astype(bf16), rounded[:, j * head : (j + 1) * head], preferred_element_type=f32
            )
        )
        last = climb[length - 1 : length]
        growth = jnp.where(mine, jnp.exp(climb), growth)
        ends = jnp.where(mine, jnp.exp(last - climb) * size, ends)
        decay = jnp.where(mine, jnp.exp(last), decay)
        reach = cols_ref[length - 1 : length, reach_lane + at : reach_lane + at + 1]
        reached = jnp.where(mine, reach, reached)
    inside = inside[0] if len(inside) == 1 else jnp.concatenate(inside, axis=1)
    carried = jnp.dot(queries, state[...].astype(bf16), preferred_element_type=f32)
    y_ref[...] = inside + growth * carried + skip_ref[...] * values
    fresh = lax.dot_general(
        keys, (ends * values).astype(bf16), (((0,), (0,)), ((), ())), preferred_element_type=f32
    )
    state[...] = decay * state[...] + fresh

    @pl.when(step == pl.num_programs(0) - 1)
    def _():
        final_ref[:width_state, :] = state[...]
        final_ref[width_state:, :] = jnp.broadcast_to(reached, (8, channels))


def scan(z, tokens, edge, slots, middle, found, taps, skip, first_head, head, experts, depth, width, length):
    maps_all, cols, rows = found
    count, channels = tokens.shape[0], taps.shape[1]
    width_state = maps_all.shape[1] // 2
    flat = list(slots) + [part for pair in middle for part in pair]
    block = lambda *shape: pl.BlockSpec(shape, lambda b, _: (b, 0))
    return pl.pallas_call(
        functools.partial(
            scan_kernel, first_head, head, experts, depth, width, len(slots), len(middle)
        ),
        grid_spec=pltpu.PrefetchScalarGridSpec(
            num_scalar_prefetch=1,
            grid=(count // length,),
            in_specs=[block(length, tokens.shape[1]), vmem(*edge.shape)]
            + [vmem(*part.shape) for part in flat]
            + [
                block(length, maps_all.shape[1]),
                block(length, 128),
                pl.BlockSpec((rows.shape[0], length), lambda b, _: (0, b)),
                vmem(*taps.shape),
                vmem(*skip.shape),
            ],
            out_specs=[
                block(length, channels),
                block(length, channels),
                pl.BlockSpec((width_state + 8, channels), lambda b, _: (0, 0)),
            ],
            scratch_shapes=[
                pltpu.VMEM((experts, width, 2 * channels), bf16),
                pltpu.VMEM((8 + length, channels), f32),
                pltpu.VMEM((width_state, channels), f32),
            ],
        ),
        out_shape=[
            jax.ShapeDtypeStruct((count, channels), f32),
            jax.ShapeDtypeStruct((count, channels), bf16),
            jax.ShapeDtypeStruct((width_state + 8, channels), f32),
        ],
        compiler_params=params(48),
        name="scan",
    )(z, tokens, edge, *flat, maps_all, cols, rows, taps, skip)


def norm_kernel(chunks, before, head, heads, pos_ref, maps_ref, cols_ref, gain_ref, *refs):
    ys, gates = refs[:chunks], refs[chunks : 2 * chunks]
    finals = refs[2 * chunks : 2 * chunks + chunks * before]
    out_ref, entering = refs[2 * chunks + chunks * before :]
    width_state = maps_ref.shape[1] // 2
    channels = out_ref.shape[1]
    each = channels // chunks

    @pl.when(pl.program_id(0) == 0)
    def _():
        for q in range(chunks):
            total = jnp.zeros((width_state, each), f32)
            logs = jnp.zeros((1, each), f32)
            for s in range(before):
                ref = finals[q * before + s]
                total = total + jnp.exp(logs) * ref[:width_state, :]
                logs = logs + ref[width_state : width_state + 1, :]
            entering[:, q * each : (q + 1) * each] = total.astype(bf16)

    lane = lax.broadcasted_iota(jnp.int32, (1, channels), 1)
    growth = 0.0
    for j in range(heads):
        reach = cols_ref[:, reach_lane + j : reach_lane + j + 1]
        growth = jnp.where(lane // head == j, jnp.exp(reach), growth)
    queries = maps_ref[:, width_state:]
    carried = growth * jnp.dot(queries, entering[...], preferred_element_type=f32)
    join = lambda parts: parts[0][...] if chunks == 1 else jnp.concatenate([p[...] for p in parts], axis=1)
    gate = join(gates).astype(f32)
    gated = (join(ys) + carried) * (gate / (1.0 + jnp.exp(-gate)))
    row = lax.broadcasted_iota(jnp.int32, (channels, channels), 0) // head
    col = lax.broadcasted_iota(jnp.int32, (channels, channels), 1) // head
    same = (row == col).astype(f32)
    square = jnp.dot(gated * gated, same, precision=highest, preferred_element_type=f32) * (1.0 / head)
    out_ref[...] = (gated * lax.rsqrt(square + 1e-05) * gain_ref[...]).astype(bf16)


def norm(part, found, gain, ys, gates, finals, head, length):
    maps_all, cols, _ = found
    count, channels = maps_all.shape[0] // 2, gain.shape[1]
    chunks, before = len(ys), len(finals[0])
    steps = count // length
    block = lambda *shape: pl.BlockSpec(shape, lambda b, at: (at[0] * steps + b, 0))
    flat = [array for group in finals for array in group]
    return pl.pallas_call(
        functools.partial(norm_kernel, chunks, before, head, channels // head),
        grid_spec=pltpu.PrefetchScalarGridSpec(
            num_scalar_prefetch=1,
            grid=(steps,),
            in_specs=[block(length, maps_all.shape[1]), block(length, 128), vmem(*gain.shape)]
            + [block(length, channels // chunks)] * (2 * chunks)
            + [vmem(*array.shape) for array in flat],
            out_specs=pl.BlockSpec((length, channels), lambda b, _: (b, 0)),
            scratch_shapes=[pltpu.VMEM((maps_all.shape[1] // 2, channels), bf16)],
        ),
        out_shape=jax.ShapeDtypeStruct((count, channels), bf16),
        compiler_params=params(32),
        name="norm",
    )(part, maps_all, cols, gain, *ys, *gates, *flat)


def out_kernel(experts, groups, pos_ref, ids_ref, mine_ref, other_ref, w_mine_ref, w_other_ref, *outs):
    group, width = pos_ref[0], mine_ref.shape[0] // groups
    chunk = w_mine_ref.shape[2]
    for s in range(groups):
        rows = pl.ds(pl.multiple_of(jnp.bitwise_xor(group, s) * width, 64), width)
        chosen = ids_ref[rows, :].astype(f32)[:, 0:1]
        mine, other = mine_ref[rows, :], other_ref[rows, :]
        zero = jnp.zeros_like(mine)
        for k in range(2):
            total = jnp.zeros((width, chunk), f32)
            for e in range(experts):
                total += jnp.dot(jnp.where(chosen == e, mine, zero), w_mine_ref[2 * e + k], preferred_element_type=f32)
                total += jnp.dot(jnp.where(chosen == e, other, zero), w_other_ref[2 * e + k], preferred_element_type=f32)
            outs[s][:, k * chunk : (k + 1) * chunk] = total.astype(bf16)


def project_out(group, ids, mine, other, w_mine, w_other, groups):
    experts, chunk = w_mine.shape[0] // 2, w_mine.shape[2]
    rows = mine.shape[0] // groups
    whole = pl.BlockSpec(memory_space=pltpu.VMEM)
    return pl.pallas_call(
        functools.partial(out_kernel, experts, groups),
        in_specs=[pl.BlockSpec(memory_space=pltpu.SMEM)] + [whole] * 5,
        out_specs=[whole] * groups,
        out_shape=[jax.ShapeDtypeStruct((rows, 2 * chunk), bf16)] * groups,
        compiler_params=params(48),
        name="project_out",
    )(group, ids, mine, other, w_mine, w_other)


def sum_kernel(depth, groups, pos_ref, *refs):
    out_ref = refs[-1]
    for s in range(depth):
        parts = refs[s * groups : (s + 1) * groups]
        total = parts[0][...].astype(f32)
        for part in parts[1:]:
            total = total + part[...].astype(f32)
        wide = total.shape[1]
        at = pl.multiple_of(lax.rem(pos_ref[0] - s + depth, depth) * wide, 128)
        out_ref[:, pl.ds(at, wide)] = total.astype(bf16)


def add_up(z, parts, depth, groups):
    rows, wide = parts[0].shape
    whole = pl.BlockSpec(memory_space=pltpu.VMEM)
    return pl.pallas_call(
        functools.partial(sum_kernel, depth, groups),
        in_specs=[pl.BlockSpec(memory_space=pltpu.SMEM)] + [whole] * len(parts),
        out_specs=whole,
        out_shape=jax.ShapeDtypeStruct((rows, depth * wide), bf16),
        compiler_params=params(48),
        name="add_up",
    )(z, *parts)


def spread_pieces(piece_of, groups):
    index = 2 * (lax.axis_index("exp") // 2) + lax.axis_index("ctx") % 2
    return [
        shift(
            piece_of(jnp.bitwise_xor(index, r)),
            lambda z, k, e: (z, e % 2, (2 * (e // 2) + k) ^ r),
        )
        for r in range(groups)
    ]


def arrange(blocks, group):
    stacked = jnp.zeros((len(blocks),) + blocks[0].shape, blocks[0].dtype)
    for r, block in enumerate(blocks):
        stacked = lax.dynamic_update_index_in_dim(stacked, block, jnp.bitwise_xor(group, r), 0)
    return stacked


def on_device(
    tokens, expert_ids, damping, in_weight, out_weight, w_bc, w_dt, rate, dt_bias, d_skip, gain, conv_weight
):
    groups, parts = lax.axis_size("exp"), lax.axis_size("ctx")
    depth, experts = parts // 2, groups // 2
    group, core, z = lax.axis_index("exp"), lax.axis_index("ctx") % 2, lax.axis_index("ctx") // 2
    rows, width = tokens.shape
    half = in_weight.shape[3]
    piece = half // groups
    heads = rate.shape[0] // 2
    head = piece // heads
    chunks = 2 if piece % 256 == 0 else 1
    channels = piece // chunks
    count = 2 * groups * rows
    length = 256 if count % 512 == 0 else 128
    scalar = lambda v: jnp.reshape(v, (1,)).astype(jnp.int32)
    z_at, group_at = scalar(z), scalar(group)
    depth_weight = in_weight.shape[1]

    flat = in_weight[0].reshape(depth_weight, 2 * half)
    in_slots = []
    for q in range(chunks):

        def piece_of(p):
            at = p * piece + q * channels
            return jnp.concatenate(
                [lax.dynamic_slice(flat, (0, j * half + at), (depth_weight, channels)) for j in range(2)],
                axis=1,
            )

        shard = arrange(spread_pieces(piece_of, groups), group)
        shard = shard.reshape(groups * depth_weight, 2 * channels)
        in_slots.append(line_gather(shard, depth))

    added = jnp.concatenate(
        [expert_ids.astype(bf16), damping[:, None], jnp.zeros((rows, extra - 2), bf16)], axis=1
    )
    wide = jnp.concatenate([tokens, added], axis=1)
    own = [wide] + [shift(wide, lambda z, k, e: (z, k, e ^ s)) for s in range(1, groups)]
    swapped = [shift(block, lambda z, k, e: (z, 1 - k, e)) for block in own]
    plane = jnp.zeros((count, width + extra), bf16)
    for where, blocks in ((core, own), (1 - core, swapped)):
        for s, block in enumerate(blocks):
            at = (where * groups + jnp.bitwise_xor(group, s)) * rows
            plane = lax.dynamic_update_slice(plane, block, (at, 0))
    edge = shift(plane[count - halo :], lambda z, k, e: (z + 1, k, e) if z + 1 < depth else None)

    local = lambda vector: lax.dynamic_slice_in_dim(vector, core * heads, heads, 0)
    lanes = lambda vector: jnp.concatenate(
        [jnp.pad(local(vector), (0, dt_lane - heads))] * (128 // dt_lane)
    )[None, :]
    picked = lax.dynamic_slice_in_dim(w_dt, (2 * group + core) * heads, heads, 0)
    picked = jnp.concatenate([jnp.pad(picked, ((0, dt_lane - heads), (0, 0)))] * (128 // dt_lane), axis=0)
    w_maps = jnp.concatenate([w_bc, picked.T], axis=1)
    found = maps(plane, w_maps, lanes(dt_bias), lanes(rate), heads, w_bc.shape[1], length)

    half_taps = lax.dynamic_slice_in_dim(conv_weight, core * piece, piece, 1)
    half_gain = lax.dynamic_slice_in_dim(gain, core * piece, piece, 0)[None, :]
    half_skip = jnp.repeat(local(d_skip), head)[None, :]
    ys, gates, finals = [], [], []
    for q in range(chunks):
        span = slice(q * channels, (q + 1) * channels)
        y, gate, final = scan(
            z_at, plane, edge, *in_slots[q], found, half_taps[:, span], half_skip[:, span],
            q * channels // head, head, experts, depth, width, length,
        )
        ys.append(y)
        gates.append(gate)
        finals.append(
            [
                shift(final, lambda z, k, e: (z + s, k, e) if z + s < depth else None)
                for s in range(1, depth)
            ]
        )

    out_flat = out_weight[0]
    out_blocks = spread_pieces(
        lambda p: lax.dynamic_slice_in_dim(out_flat, p * piece, piece, 0), groups
    )
    near, middle = line_gather(arrange(out_blocks, group), depth)
    ordered = near[:2] + [
        jnp.where(z >= s + 2, up, down) for s, (up, down) in enumerate(middle)
    ] + near[2:]
    other_half = [shift(array, lambda z, k, e: (z, 1 - k, e)) for array in ordered]

    theirs = norm(scalar(1 - core), found, half_gain, ys, gates, finals, head, length)
    other = shift(theirs, lambda z, k, e: (z, 1 - k, e))
    mine = norm(scalar(core), found, half_gain, ys, gates, finals, head, length)

    ids = lax.dynamic_slice(plane, (core * groups * rows, width), (groups * rows, extra))
    blocks = []
    for s in range(depth):
        results = project_out(group_at, ids, mine, other, ordered[s], other_half[s], groups)
        blocks += [results[0]] + [
            shift(results[r], lambda z, k, e: (z, k, e ^ r)) for r in range(1, groups)
        ]
    return add_up(z_at, blocks, depth, groups)


def solution(mesh):
    placed = (
        P(("ctx", "exp"), None),
        P(("ctx", "exp"), None),
        P(("ctx", "exp")),
        P("exp", "ctx", None, None),
        P("exp", None, "ctx"),
        P(),
        P(),
        P("exp"),
        P("exp"),
        P("exp"),
        P("exp"),
        P(None, "exp"),
    )
    return jax.shard_map(
        on_device, mesh=mesh, in_specs=placed, out_specs=P(("ctx", "exp"), None), check_vma=False
    )
```

profile of v0, /device:TPU:16, one launch (start us, length us, event | category | flops | bytes accessed | tf_op | source)
XLA Modules:
  0.0 273.7 jit_solution(1476873007640620129)
XLA Ops:
  1.7 2.0 concatenate.39
  3.6 1.5 collective-permute-start
  5.1 1.5 collective-permute-start.1
  7.1 1.5 copy.19
  10.3 2.1 collective-permute-start.8
  14.9 5.3 %concatenate.40 = bf16[128,2048]{0,1:T(8,128)(2,1)S(1)} concatenate(bf16[16,2048]{0,1:T(8,128)(2,1)S(1)} %pad.11, bf16[16,2048]{0,1:T(8,128)(2,1)S(1)} %pad.11, bf16[16,2048]{0,1:T(8,128)(2,1)S(1)} %pad.11, bf16[16,2048]{0,1:T(8,128)(2,1)S(1)} %pad.11, bf16[16,2048]{0,1:T(8,128)(2,1)S(1)} %pad.11, bf16[16,2048]{0,1:T(8,128)(2,1)S(1)} %pad.11, bf16[16,2048]{0,1:T(8,128)(2,1)S(1)} %pad.11, ...), dimensions={0} | concatenate | bytes 1048576 | tf_op jit(solution)/shard_map/concatenate | solution.py:429
  20.5 3.2 %broadcast_in_dim.58 = bf16[1536,2176]{1,0:T(8,128)(2,1)} broadcast(bf16[]{:T(256)} %constant.114.clone.1), dimensions={} | broadcast | bytes 6684674 | tf_op jit(solution)/shard_map/broadcast_in_dim | solution.py:417
  23.6 2.1 constant_dynamic-update-slice_fusion.7
  25.8 1.4 pad_maximum_fusion.w_ref
  30.3 1.6 collective-permute-start.10
  32.0 12.1 %collective-permute-done.9 = bf16[256,256]{1,0:T(8,128)(2,1)} collective-permute-done((bf16[256,256]{1,0:T(8,128)(2,1)}, bf16[256,256]{1,0:T(8,128)(2,1)}, u32[]{:S(2)}, u32[]{:S(2)}) %collective-permute-start.9) | collective-permute-done | bytes 131104 | tf_op jit(solution)/shard_map/ppermute | solution.py:34
  44.1 9.8 %collective-permute-start.17 = (bf16[256,256]{1,0:T(8,128)(2,1)S(1)}, bf16[256,256]{1,0:T(8,128)(2,1)S(1)}, u32[]{:S(2)}, u32[]{:S(2)}) collective-permute-start(bf16[256,256]{1,0:T(8,128)(2,1)S(1)} %pad_maximum_fusion.6), channel_id=1, source_target_pairs={{0,1},{1,5},{2,3},{3,7},{4,0},{5,4},{6,2},{7,6},{8,9},{9,13},{10,1... | collective-permute-start | bytes 393224 | tf_op jit(solution)/shard_map/ppermute | solution.py:34
  54.7 1.6 collective-permute-done.17
  56.4 2.4 collective-permute-start.11
  58.8 1.6 collective-permute-start.18
  60.4 5.2 %collective-permute-done.18 = bf16[256,256]{1,0:T(8,128)(2,1)S(1)} collective-permute-done((bf16[256,256]{1,0:T(8,128)(2,1)S(1)}, bf16[256,256]{1,0:T(8,128)(2,1)S(1)}, u32[]{:S(2)}, u32[]{:S(2)}) %collective-permute-start.18) | collective-permute-done | bytes 131104 | tf_op jit(solution)/shard_map/ppermute | solution.py:34
  66.3 4.6 %collective-permute-done.19 = bf16[256,256]{1,0:T(8,128)(2,1)S(1)} collective-permute-done((bf16[256,256]{1,0:T(8,128)(2,1)S(1)}, bf16[256,256]{1,0:T(8,128)(2,1)S(1)}, u32[]{:S(2)}, u32[]{:S(2)}) %collective-permute-start.19) | collective-permute-done | bytes 131104 | tf_op jit(solution)/shard_map/ppermute | solution.py:34
  73.8 3.1 %collective-permute-start.34 = (bf16[256,256]{1,0:T(8,128)(2,1)S(1)}, bf16[256,256]{1,0:T(8,128)(2,1)S(1)}, u32[]{:S(2)}, u32[]{:S(2)}) collective-permute-start(bf16[256,256]{1,0:T(8,128)(2,1)S(1)} %get-tuple-element.71), channel_id=1, source_target_pairs={{0,3},{1,7},{2,1},{3,5},{4,2},{5,6},{6,0},{7,4},{8,11},{9,15},{10,... | collective-permute-start | bytes 393224 | tf_op jit(solution)/shard_map/ppermute | solution.py:34
  77.5 1.6 collective-permute-start.12
  79.8 1.4 collective-permute-done.34
  82.2 2.1 constant_dynamic-update-slice_fusion.6
  84.3 18.7 %collective-permute-done.12.refs_1_ = bf16[1024,256]{1,0:T(8,128)(2,1)S(1)} collective-permute-done((bf16[1024,256]{1,0:T(8,128)(2,1)S(1)}, bf16[1024,256]{1,0:T(8,128)(2,1)S(1)}, u32[]{:S(2)}, u32[]{:S(2)}) %collective-permute-start.12) | collective-permute-done | bytes 524320 | tf_op jit(solution)/shard_map/ppermute | solution.py:34
  103.0 1.7 collective-permute-start.20
  105.0 2.1 constant_dynamic-update-slice_fusion.5
  107.7 2.1 constant_dynamic-update-slice_fusion.4
  109.8 15.4 %collective-permute-done.20.refs_1_ = bf16[1024,256]{1,0:T(8,128)(2,1)S(1)} collective-permute-done((bf16[1024,256]{1,0:T(8,128)(2,1)S(1)}, bf16[1024,256]{1,0:T(8,128)(2,1)S(1)}, u32[]{:S(2)}, u32[]{:S(2)}) %collective-permute-start.20) | collective-permute-done | bytes 524320 | tf_op jit(solution)/shard_map/ppermute | solution.py:34
  125.2 2.6 collective-permute-start.39
  128.8 1.4 collective-permute-start.45
  131.2 2.5 collective-permute-start.14
  134.7 14.3 %collective-permute-done.39.w_mine_ref = bf16[4,256,256]{2,1,0:T(8,128)(2,1)} collective-permute-done((bf16[4,256,256]{2,1,0:T(8,128)(2,1)}, bf16[4,256,256]{2,1,0:T(8,128)(2,1)}, u32[]{:S(2)}, u32[]{:S(2)}) %collective-permute-start.39) | collective-permute-done | bytes 524320 | tf_op jit(solution)/shard_map/ppermute | solution.py:34
  149.0 1.3 collective-permute-start.15
  150.4 3.8 %collective-permute-start.22 = (bf16[1024,256]{1,0:T(8,128)(2,1)S(1)}, bf16[1024,256]{1,0:T(8,128)(2,1)S(1)}, u32[]{:S(2)}, u32[]{:S(2)}) collective-permute-start(bf16[1024,256]{1,0:T(8,128)(2,1)S(1)} %collective-permute-done.20.refs_1_), channel_id=1, source_target_pairs={{8,16},{9,17},{10,18},{11,19},{12,20},{13,21},{14,22},{15,23},{16,... | collective-permute-start | bytes 1572872 | tf_op jit(solution)/shard_map/ppermute | solution.py:34
  154.1 2.1 collective-permute-start.23
  157.3 2.9 %collective-permute-done.14.refs_3_ = bf16[1024,256]{1,0:T(8,128)(2,1)S(1)} collective-permute-done((bf16[1024,256]{1,0:T(8,128)(2,1)S(1)}, bf16[1024,256]{1,0:T(8,128)(2,1)S(1)}, u32[]{:S(2)}, u32[]{:S(2)}) %collective-permute-start.14) | collective-permute-done | bytes 524320 | tf_op jit(solution)/shard_map/ppermute | solution.py:34
  160.2 4.4 %collective-permute-start.44 = (bf16[4,256,256]{2,1,0:T(8,128)(2,1)}, bf16[4,256,256]{2,1,0:T(8,128)(2,1)}, u32[]{:S(2)}, u32[]{:S(2)}) collective-permute-start(bf16[4,256,256]{2,1,0:T(8,128)(2,1)} %collective-permute-done.39.w_mine_ref), channel_id=1, source_target_pairs={{8,16},{9,17},{10,18},{11,19},{12,20},{13,21},{14,22},{15,23},{16,... | collective-permute-start | bytes 1572872 | tf_op jit(solution)/shard_map/ppermute | solution.py:34
  164.6 3.1 %collective-permute-start.46 = (bf16[4,256,256]{2,1,0:T(8,128)(2,1)}, bf16[4,256,256]{2,1,0:T(8,128)(2,1)}, u32[]{:S(2)}, u32[]{:S(2)}) collective-permute-start(bf16[4,256,256]{2,1,0:T(8,128)(2,1)} %collective-permute-done.45.w_mine_ref), channel_id=1, source_target_pairs={{8,0},{9,1},{10,2},{11,3},{12,4},{13,5},{14,6},{15,7},{16,8},{17,9... | collective-permute-start | bytes 1572872 | tf_op jit(solution)/shard_map/ppermute | solution.py:34
  169.5 1.9 collective-permute-start.7
  171.4 9.9 %maps.1 = (bf16[1536,256]{1,0:T(8,128)(2,1)S(1)}, f32[1536,128]{1,0:T(8,128)S(1)}, f32[32,1536]{1,0:T(8,128)S(1)}) custom-call(bf16[1536,2176]{1,0:T(8,128)(2,1)} %constant_dynamic-update-slice_fusion.x_ref, bf16[2048,384]{1,0:T(8,128)(2,1)S(1)} %pad_maximum_fusion.w_ref, f32[1,128]{1,0:T(1,128)S(1)} %bitcast.53, f32[1,128]{1,0:T(1,128)S(1)} %bitcast.54), custom_call_target="tpu_custom_call" | custom-call | tf_op jit(solution)/shard_map/maps/pallas_call | solution.py:81
  181.3 2.1 collective-permute-done.7.edge_ref
  183.4 8.8 %scan.2 = (f32[1536,128]{1,0:T(8,128)S(1)}, bf16[1536,128]{1,0:T(8,128)(2,1)S(1)}, f32[136,128]{1,0:T(8,128)S(1)}) custom-call(s32[1]{0:T(128)} %bitcast.pos_ref, bf16[1536,2176]{1,0:T(8,128)(2,1)} %constant_dynamic-update-slice_fusion.x_ref, bf16[16,2176]{1,0:T(8,128)(2,1)S(1)} %collective-permute-done.7.edge_ref, bf16[1024,256]{1,0:T(8,128)(2,1)S(1)} %bitcast.47, ...), custom_call_target="tpu_custom_call" | custom-call | tf_op jit(solution)/shard_map/scan/pallas_call | solution.py:207
  192.2 3.6 %collective-permute-start.24 = (f32[136,128]{1,0:T(8,128)S(1)}, f32[136,128]{1,0:T(8,128)S(1)}, u32[]{:S(2)}, u32[]{:S(2)}) collective-permute-start(f32[136,128]{1,0:T(8,128)S(1)} %get-tuple-element.37), channel_id=1, source_target_pairs={{0,8},{1,9},{2,10},{3,11},{4,12},{5,13},{6,14},{7,15},{8,16},{9,17... | collective-permute-start | bytes 208904 | tf_op jit(solution)/shard_map/ppermute | solution.py:34
  195.9 1.3 collective-permute-start.25
  197.8 9.4 %scan.3 = (f32[1536,128]{1,0:T(8,128)S(1)}, bf16[1536,128]{1,0:T(8,128)(2,1)S(1)}, f32[136,128]{1,0:T(8,128)}) custom-call(s32[1]{0:T(128)} %bitcast.pos_ref, bf16[1536,2176]{1,0:T(8,128)(2,1)} %constant_dynamic-update-slice_fusion.x_ref, bf16[16,2176]{1,0:T(8,128)(2,1)S(1)} %collective-permute-done.7.edge_ref, bf16[1024,256]{1,0:T(8,128)(2,1)S(1)} %bitcast.50, ...), custom_call_target="tpu_custom_call" | custom-call | tf_op jit(solution)/shard_map/scan/pallas_call | solution.py:207
  208.1 1.9 collective-permute-start.27
  210.1 1.3 collective-permute-start.28
  212.8 1.9 collective-permute-done.27.refs_7_
  214.7 3.4 %collective-permute-done.28.refs_8_ = f32[136,128]{1,0:T(8,128)} collective-permute-done((f32[136,128]{1,0:T(8,128)}, f32[136,128]{1,0:T(8,128)}, u32[]{:S(2)}, u32[]{:S(2)}) %collective-permute-start.28) | collective-permute-done | bytes 69664 | tf_op jit(solution)/shard_map/ppermute | solution.py:34
  219.3 3.6 %norm.3 = bf16[768,256]{1,0:T(8,128)(2,1)} custom-call(s32[1]{0:T(128)} %bitcast.17.pos_ref, bf16[1536,256]{1,0:T(8,128)(2,1)S(1)} %get-tuple-element.30.refs_5_.maps_ref, f32[1536,128]{1,0:T(8,128)S(1)} %get-tuple-element.31.refs_6_.cols_ref, f32[1,256]{1,0:T(1,128)S(1)} %bitcast.51, f32[1536,128]{1,0:T(8,128)S(1)} %get-tuple-element.33.refs_0_, ...), custom_call_target="tpu_custom_call" | custom-call | tf_op jit(solution)/shard_map/norm/pallas_call | solution.py:287
  230.0 2.9 %norm.2.mine_ref = bf16[768,256]{1,0:T(8,128)(2,1)S(1)} custom-call(s32[1]{0:T(128)} %bitcast.2.pos_ref, bf16[1536,256]{1,0:T(8,128)(2,1)S(1)} %get-tuple-element.30.refs_5_.maps_ref, f32[1536,128]{1,0:T(8,128)S(1)} %get-tuple-element.31.refs_6_.cols_ref, f32[1,256]{1,0:T(1,128)S(1)} %bitcast.52, f32[1536,128]{1,0:T(8,128)S(1)} %get-tuple-element.33.refs_0_, ...), custom_call_target="tpu_custom_call" | custom-call | tf_op jit(solution)/shard_map/norm/pallas_call | solution.py:287
  232.9 2.3 project_out.4
  236.6 2.1 collective-permute-start.38
  238.8 2.2 project_out.5
  241.6 2.1 project_out.6
  244.6 2.1 collective-permute-start.43
  246.8 1.9 collective-permute-start.48
  248.7 2.2 project_out.7
  250.9 1.5 collective-permute-start.49
  252.6 3.2 %collective-permute-done.42.refs_6_ = bf16[192,512]{1,0:T(8,128)(2,1)S(1)} collective-permute-done((bf16[192,512]{1,0:T(8,128)(2,1)S(1)}, bf16[192,512]{1,0:T(8,128)(2,1)S(1)}, u32[]{:S(2)}, u32[]{:S(2)}) %collective-permute-start.42) | collective-permute-done | bytes 196640 | tf_op jit(solution)/shard_map/ppermute | solution.py:34
  255.8 1.5 collective-permute-start.52
  257.3 1.3 collective-permute-start.53
  258.6 1.3 collective-permute-done.48.refs_9_
  260.7 3.5 %collective-permute-done.49.refs_10_ = bf16[192,512]{1,0:T(8,128)(2,1)S(1)} collective-permute-done((bf16[192,512]{1,0:T(8,128)(2,1)S(1)}, bf16[192,512]{1,0:T(8,128)(2,1)S(1)}, u32[]{:S(2)}, u32[]{:S(2)}) %collective-permute-start.49) | collective-permute-done | bytes 196640 | tf_op jit(solution)/shard_map/ppermute | solution.py:34
  264.9 3.5 %collective-permute-done.52.refs_13_ = bf16[192,512]{1,0:T(8,128)(2,1)S(1)} collective-permute-done((bf16[192,512]{1,0:T(8,128)(2,1)S(1)}, bf16[192,512]{1,0:T(8,128)(2,1)S(1)}, u32[]{:S(2)}, u32[]{:S(2)}) %collective-permute-start.52) | collective-permute-done | bytes 196640 | tf_op jit(solution)/shard_map/ppermute | solution.py:34
  269.0 3.5 %collective-permute-done.54.refs_15_ = bf16[192,512]{1,0:T(8,128)(2,1)S(1)} collective-permute-done((bf16[192,512]{1,0:T(8,128)(2,1)S(1)}, bf16[192,512]{1,0:T(8,128)(2,1)S(1)}, u32[]{:S(2)}, u32[]{:S(2)}) %collective-permute-start.54) | collective-permute-done | bytes 196640 | tf_op jit(solution)/shard_map/ppermute | solution.py:34
  (148 shorter events, 40.6 us)
Async XLA Ops:
  0.0 14.4 %copy-start = (bf16[32,2048]{1,0:T(8,128)(2,1)S(1)}, bf16[32,2048]{1,0:T(8,128)(2,1)}, u32[]{:S(2)}) copy-start(bf16[32,2048]{1,0:T(8,128)(2,1)} %param.18) | copy-start | bytes 393220
  0.0 20.2 %copy-start.13 = (f32[8]{0:T(128)S(1)}, f32[8]{0:T(128)}, u32[]{:S(2)}) copy-start(f32[8]{0:T(128)} %param.21) | copy-start | bytes 100
  3.6 78.6 %collective-permute-start = (bf16[192,2176]{1,0:T(8,128)(2,1)}, bf16[192,2176]{1,0:T(8,128)(2,1)}, u32[]{:S(2)}, u32[]{:S(2)}) collective-permute-start(bf16[192,2176]{1,0:T(8,128)(2,1)} %concatenate.39), channel_id=1, source_target_pairs={{0,1},{1,0},{2,3},{3,2},{4,5},{5,4},{6,7},{7,6},{8,9},{9,8},{10,11... | collective-permute-start | bytes 2506760 | tf_op jit(solution)/shard_map/ppermute | solution.py:34
  5.1 99.9 %collective-permute-start.1 = (bf16[192,2176]{1,0:T(8,128)(2,1)}, bf16[192,2176]{1,0:T(8,128)(2,1)}, u32[]{:S(2)}, u32[]{:S(2)}) collective-permute-start(bf16[192,2176]{1,0:T(8,128)(2,1)} %concatenate.39), channel_id=1, source_target_pairs={{0,2},{1,3},{2,0},{3,1},{4,6},{5,7},{6,4},{7,5},{8,10},{9,11},{10,... | collective-permute-start | bytes 2506760 | tf_op jit(solution)/shard_map/ppermute | solution.py:34
  6.7 100.5 %collective-permute-start.2 = (bf16[192,2176]{1,0:T(8,128)(2,1)}, bf16[192,2176]{1,0:T(8,128)(2,1)}, u32[]{:S(2)}, u32[]{:S(2)}) collective-permute-start(bf16[192,2176]{1,0:T(8,128)(2,1)} %concatenate.39), channel_id=1, source_target_pairs={{0,3},{1,2},{2,1},{3,0},{4,7},{5,6},{6,5},{7,4},{8,11},{9,10},{10,... | collective-permute-start | bytes 2506760 | tf_op jit(solution)/shard_map/ppermute | solution.py:34
  10.3 18.3 %collective-permute-start.8 = (bf16[256,256]{1,0:T(8,128)(2,1)}, bf16[256,256]{1,0:T(8,128)(2,1)}, u32[]{:S(2)}, u32[]{:S(2)}) collective-permute-start(bf16[256,256]{1,0:T(8,128)(2,1)} %pad_maximum_fusion.1), channel_id=1, source_target_pairs={{0,0},{1,4},{2,2},{3,6},{4,1},{5,5},{6,3},{7,7},{8,8},{9,12},{10,1... | collective-permute-start | bytes 393224 | tf_op jit(solution)/shard_map/ppermute | solution.py:34
  13.1 30.9 %collective-permute-start.9 = (bf16[256,256]{1,0:T(8,128)(2,1)}, bf16[256,256]{1,0:T(8,128)(2,1)}, u32[]{:S(2)}, u32[]{:S(2)}) collective-permute-start(bf16[256,256]{1,0:T(8,128)(2,1)} %pad_maximum_fusion.2), channel_id=1, source_target_pairs={{0,1},{1,5},{2,3},{3,7},{4,0},{5,4},{6,2},{7,6},{8,9},{9,13},{10,1... | collective-permute-start | bytes 393224 | tf_op jit(solution)/shard_map/ppermute | solution.py:34
  20.2 8.2 %copy-start.15 = (f32[8]{0:T(128)S(1)}, f32[8]{0:T(128)}, u32[]{:S(2)}) copy-start(f32[8]{0:T(128)} %param.19) | copy-start | bytes 100
  20.2 8.4 %copy-start.10 = (bf16[1,1024,256]{2,1,0:T(8,128)(2,1)S(1)}, bf16[1,1024,256]{2,1,0:T(8,128)(2,1)}, u32[]{:S(2)}) copy-start(bf16[1,1024,256]{2,1,0:T(8,128)(2,1)} %param.16) | copy-start | bytes 1572868
  28.7 1.6 collective-permute-start.16
  30.3 28.4 %collective-permute-start.10 = (bf16[256,256]{1,0:T(8,128)(2,1)S(1)}, bf16[256,256]{1,0:T(8,128)(2,1)S(1)}, u32[]{:S(2)}, u32[]{:S(2)}) collective-permute-start(bf16[256,256]{1,0:T(8,128)(2,1)S(1)} %pad_maximum_fusion.3), channel_id=1, source_target_pairs={{0,2},{1,6},{2,0},{3,4},{4,3},{5,7},{6,1},{7,5},{8,10},{9,14},{10,... | collective-permute-start | bytes 393224 | tf_op jit(solution)/shard_map/ppermute | solution.py:34
  44.1 12.3 %collective-permute-start.17 = (bf16[256,256]{1,0:T(8,128)(2,1)S(1)}, bf16[256,256]{1,0:T(8,128)(2,1)S(1)}, u32[]{:S(2)}, u32[]{:S(2)}) collective-permute-start(bf16[256,256]{1,0:T(8,128)(2,1)S(1)} %pad_maximum_fusion.6), channel_id=1, source_target_pairs={{0,1},{1,5},{2,3},{3,7},{4,0},{5,4},{6,2},{7,6},{8,9},{9,13},{10,1... | collective-permute-start | bytes 393224 | tf_op jit(solution)/shard_map/ppermute | solution.py:34
  56.4 9.3 %collective-permute-start.11 = (bf16[256,256]{1,0:T(8,128)(2,1)S(1)}, bf16[256,256]{1,0:T(8,128)(2,1)S(1)}, u32[]{:S(2)}, u32[]{:S(2)}) collective-permute-start(bf16[256,256]{1,0:T(8,128)(2,1)S(1)} %pad_maximum_fusion.4), channel_id=1, source_target_pairs={{0,3},{1,7},{2,1},{3,5},{4,2},{5,6},{6,0},{7,4},{8,11},{9,15},{10,... | collective-permute-start | bytes 393224 | tf_op jit(solution)/shard_map/ppermute | solution.py:34
  58.8 6.8 %collective-permute-start.18 = (bf16[256,256]{1,0:T(8,128)(2,1)S(1)}, bf16[256,256]{1,0:T(8,128)(2,1)S(1)}, u32[]{:S(2)}, u32[]{:S(2)}) collective-permute-start(bf16[256,256]{1,0:T(8,128)(2,1)S(1)} %pad_maximum_fusion.7), channel_id=1, source_target_pairs={{0,2},{1,6},{2,0},{3,4},{4,3},{5,7},{6,1},{7,5},{8,10},{9,14},{10,... | collective-permute-start | bytes 393224 | tf_op jit(solution)/shard_map/ppermute | solution.py:34
  65.6 5.3 %collective-permute-start.19 = (bf16[256,256]{1,0:T(8,128)(2,1)S(1)}, bf16[256,256]{1,0:T(8,128)(2,1)S(1)}, u32[]{:S(2)}, u32[]{:S(2)}) collective-permute-start(bf16[256,256]{1,0:T(8,128)(2,1)S(1)} %pad_maximum_fusion.8), channel_id=1, source_target_pairs={{0,3},{1,7},{2,1},{3,5},{4,2},{5,6},{6,0},{7,4},{8,11},{9,15},{10,... | collective-permute-start | bytes 393224 | tf_op jit(solution)/shard_map/ppermute | solution.py:34
  65.6 5.6 %collective-permute-start.31 = (bf16[256,256]{1,0:T(8,128)(2,1)S(1)}, bf16[256,256]{1,0:T(8,128)(2,1)S(1)}, u32[]{:S(2)}, u32[]{:S(2)}) collective-permute-start(bf16[256,256]{1,0:T(8,128)(2,1)S(1)} %get-tuple-element.73), channel_id=1, source_target_pairs={{0,0},{1,4},{2,2},{3,6},{4,1},{5,5},{6,3},{7,7},{8,8},{9,12},{10,1... | collective-permute-start | bytes 393224 | tf_op jit(solution)/shard_map/ppermute | solution.py:34
  70.9 2.9 %collective-permute-start.32 = (bf16[256,256]{1,0:T(8,128)(2,1)S(1)}, bf16[256,256]{1,0:T(8,128)(2,1)S(1)}, u32[]{:S(2)}, u32[]{:S(2)}) collective-permute-start(bf16[256,256]{1,0:T(8,128)(2,1)S(1)} %get-tuple-element.72), channel_id=1, source_target_pairs={{0,1},{1,5},{2,3},{3,7},{4,0},{5,4},{6,2},{7,6},{8,9},{9,13},{10,1... | collective-permute-start | bytes 393224 | tf_op jit(solution)/shard_map/ppermute | solution.py:34
  71.3 100.1 %copy-start.11 = (f32[4,512]{1,0:T(4,128)S(1)}, f32[4,512]{1,0:T(4,128)}, u32[]{:S(2)}) copy-start(f32[4,512]{1,0:T(4,128)} %param.23) | copy-start | bytes 24580
  71.3 6.2 %collective-permute-start.33 = (bf16[256,256]{1,0:T(8,128)(2,1)S(1)}, bf16[256,256]{1,0:T(8,128)(2,1)S(1)}, u32[]{:S(2)}, u32[]{:S(2)}) collective-permute-start(bf16[256,256]{1,0:T(8,128)(2,1)S(1)} %get-tuple-element.74), channel_id=1, source_target_pairs={{0,2},{1,6},{2,0},{3,4},{4,3},{5,7},{6,1},{7,5},{8,10},{9,14},{10,... | collective-permute-start | bytes 393224 | tf_op jit(solution)/shard_map/ppermute | solution.py:34
  73.8 7.3 %collective-permute-start.34 = (bf16[256,256]{1,0:T(8,128)(2,1)S(1)}, bf16[256,256]{1,0:T(8,128)(2,1)S(1)}, u32[]{:S(2)}, u32[]{:S(2)}) collective-permute-start(bf16[256,256]{1,0:T(8,128)(2,1)S(1)} %get-tuple-element.71), channel_id=1, source_target_pairs={{0,3},{1,7},{2,1},{3,5},{4,2},{5,6},{6,0},{7,4},{8,11},{9,15},{10,... | collective-permute-start | bytes 393224 | tf_op jit(solution)/shard_map/ppermute | solution.py:34
  77.5 25.5 %collective-permute-start.12 = (bf16[1024,256]{1,0:T(8,128)(2,1)S(1)}, bf16[1024,256]{1,0:T(8,128)(2,1)S(1)}, u32[]{:S(2)}, u32[]{:S(2)}) collective-permute-start(bf16[1024,256]{1,0:T(8,128)(2,1)S(1)} %bitcast.45), channel_id=1, source_target_pairs={{0,8},{1,9},{2,10},{3,11},{4,12},{5,13},{6,14},{7,15},{8,16},{9,17... | collective-permute-start | bytes 1572872 | tf_op jit(solution)/shard_map/ppermute | solution.py:34
  81.1 23.6 %collective-permute-start.13 = (bf16[1024,256]{1,0:T(8,128)(2,1)S(1)}, bf16[1024,256]{1,0:T(8,128)(2,1)S(1)}, u32[]{:S(2)}, u32[]{:S(2)}) collective-permute-start(bf16[1024,256]{1,0:T(8,128)(2,1)S(1)} %bitcast.46), channel_id=1, source_target_pairs={{0,24},{1,25},{2,26},{3,27},{4,28},{5,29},{6,30},{7,31},{8,0},{9,1... | collective-permute-start | bytes 1572872 | tf_op jit(solution)/shard_map/ppermute | solution.py:34
  82.2 48.0 %collective-permute-start.3 = (bf16[192,2176]{1,0:T(8,128)(2,1)}, bf16[192,2176]{1,0:T(8,128)(2,1)S(1)}, u32[]{:S(2)}, u32[]{:S(2)}) collective-permute-start(bf16[192,2176]{1,0:T(8,128)(2,1)} %concatenate.39), channel_id=1, source_target_pairs={{0,4},{1,5},{2,6},{3,7},{4,0},{5,1},{6,2},{7,3},{8,12},{9,13},{10,... | collective-permute-start | bytes 2506760 | tf_op jit(solution)/shard_map/ppermute | solution.py:34
  103.0 22.2 %collective-permute-start.20 = (bf16[1024,256]{1,0:T(8,128)(2,1)S(1)}, bf16[1024,256]{1,0:T(8,128)(2,1)S(1)}, u32[]{:S(2)}, u32[]{:S(2)}) collective-permute-start(bf16[1024,256]{1,0:T(8,128)(2,1)S(1)} %bitcast.48), channel_id=1, source_target_pairs={{0,8},{1,9},{2,10},{3,11},{4,12},{5,13},{6,14},{7,15},{8,16},{9,17... | collective-permute-start | bytes 1572872 | tf_op jit(solution)/shard_map/ppermute | solution.py:34
  104.7 24.1 %collective-permute-start.21 = (bf16[1024,256]{1,0:T(8,128)(2,1)S(1)}, bf16[1024,256]{1,0:T(8,128)(2,1)S(1)}, u32[]{:S(2)}, u32[]{:S(2)}) collective-permute-start(bf16[1024,256]{1,0:T(8,128)(2,1)S(1)} %bitcast.49), channel_id=1, source_target_pairs={{0,24},{1,25},{2,26},{3,27},{4,28},{5,29},{6,30},{7,31},{8,0},{9,1... | collective-permute-start | bytes 1572872 | tf_op jit(solution)/shard_map/ppermute | solution.py:34
  105.0 26.2 %collective-permute-start.4 = (bf16[192,2176]{1,0:T(8,128)(2,1)}, bf16[192,2176]{1,0:T(8,128)(2,1)S(1)}, u32[]{:S(2)}, u32[]{:S(2)}) collective-permute-start(bf16[192,2176]{1,0:T(8,128)(2,1)} %collective-permute-done), channel_id=1, source_target_pairs={{0,4},{1,5},{2,6},{3,7},{4,0},{5,1},{6,2},{7,3},{8,12},{9,13},{10,... | collective-permute-start | bytes 2506760 | tf_op jit(solution)/shard_map/ppermute | solution.py:34
  107.2 47.0 %collective-permute-start.5 = (bf16[192,2176]{1,0:T(8,128)(2,1)}, bf16[192,2176]{1,0:T(8,128)(2,1)S(1)}, u32[]{:S(2)}, u32[]{:S(2)}) collective-permute-start(bf16[192,2176]{1,0:T(8,128)(2,1)} %collective-permute-done.1), channel_id=1, source_target_pairs={{0,4},{1,5},{2,6},{3,7},{4,0},{5,1},{6,2},{7,3},{8,12},{9,13},{10,... | collective-permute-start | bytes 2506760 | tf_op jit(solution)/shard_map/ppermute | solution.py:34
  125.2 23.9 %collective-permute-start.39 = (bf16[4,256,256]{2,1,0:T(8,128)(2,1)}, bf16[4,256,256]{2,1,0:T(8,128)(2,1)}, u32[]{:S(2)}, u32[]{:S(2)}) collective-permute-start(bf16[4,256,256]{2,1,0:T(8,128)(2,1)} %bitcast_dynamic-update-slice_fusion.w_mine_ref), channel_id=1, source_target_pairs={{0,8},{1,9},{2,10},{3,11},{4,12},{5,13},{6,14},{7,15},{8,16},{9,17... | collective-permute-start | bytes 1572872 | tf_op jit(solution)/shard_map/ppermute | solution.py:34
  128.8 21.5 %collective-permute-start.45 = (bf16[4,256,256]{2,1,0:T(8,128)(2,1)}, bf16[4,256,256]{2,1,0:T(8,128)(2,1)}, u32[]{:S(2)}, u32[]{:S(2)}) collective-permute-start(bf16[4,256,256]{2,1,0:T(8,128)(2,1)} %bitcast_dynamic-update-slice_fusion.w_mine_ref), channel_id=1, source_target_pairs={{0,24},{1,25},{2,26},{3,27},{4,28},{5,29},{6,30},{7,31},{8,0},{9,1... | collective-permute-start | bytes 1572872 | tf_op jit(solution)/shard_map/ppermute | solution.py:34
  130.2 34.4 %collective-permute-start.6 = (bf16[192,2176]{1,0:T(8,128)(2,1)}, bf16[192,2176]{1,0:T(8,128)(2,1)S(1)}, u32[]{:S(2)}, u32[]{:S(2)}) collective-permute-start(bf16[192,2176]{1,0:T(8,128)(2,1)} %collective-permute-done.2), channel_id=1, source_target_pairs={{0,4},{1,5},{2,6},{3,7},{4,0},{5,1},{6,2},{7,3},{8,12},{9,13},{10,... | collective-permute-start | bytes 2506760 | tf_op jit(solution)/shard_map/ppermute | solution.py:34
  131.2 29.0 %collective-permute-start.14 = (bf16[1024,256]{1,0:T(8,128)(2,1)S(1)}, bf16[1024,256]{1,0:T(8,128)(2,1)S(1)}, u32[]{:S(2)}, u32[]{:S(2)}) collective-permute-start(bf16[1024,256]{1,0:T(8,128)(2,1)S(1)} %collective-permute-done.12.refs_1_), channel_id=1, source_target_pairs={{8,16},{9,17},{10,18},{11,19},{12,20},{13,21},{14,22},{15,23},{16,... | collective-permute-start | bytes 1572872 | tf_op jit(solution)/shard_map/ppermute | solution.py:34
  149.0 20.4 %collective-permute-start.15 = (bf16[1024,256]{1,0:T(8,128)(2,1)S(1)}, bf16[1024,256]{1,0:T(8,128)(2,1)S(1)}, u32[]{:S(2)}, u32[]{:S(2)}) collective-permute-start(bf16[1024,256]{1,0:T(8,128)(2,1)S(1)} %collective-permute-done.13.refs_2_), channel_id=1, source_target_pairs={{8,0},{9,1},{10,2},{11,3},{12,4},{13,5},{14,6},{15,7},{16,8},{17,9... | collective-permute-start | bytes 1572872 | tf_op jit(solution)/shard_map/ppermute | solution.py:34
  150.4 45.5 %collective-permute-start.22 = (bf16[1024,256]{1,0:T(8,128)(2,1)S(1)}, bf16[1024,256]{1,0:T(8,128)(2,1)S(1)}, u32[]{:S(2)}, u32[]{:S(2)}) collective-permute-start(bf16[1024,256]{1,0:T(8,128)(2,1)S(1)} %collective-permute-done.20.refs_1_), channel_id=1, source_target_pairs={{8,16},{9,17},{10,18},{11,19},{12,20},{13,21},{14,22},{15,23},{16,... | collective-permute-start | bytes 1572872 | tf_op jit(solution)/shard_map/ppermute | solution.py:34
  154.1 43.0 %collective-permute-start.23 = (bf16[1024,256]{1,0:T(8,128)(2,1)S(1)}, bf16[1024,256]{1,0:T(8,128)(2,1)S(1)}, u32[]{:S(2)}, u32[]{:S(2)}) collective-permute-start(bf16[1024,256]{1,0:T(8,128)(2,1)S(1)} %collective-permute-done.21.refs_2_), channel_id=1, source_target_pairs={{8,0},{9,1},{10,2},{11,3},{12,4},{13,5},{14,6},{15,7},{16,8},{17,9... | collective-permute-start | bytes 1572872 | tf_op jit(solution)/shard_map/ppermute | solution.py:34
  160.2 63.2 %collective-permute-start.44 = (bf16[4,256,256]{2,1,0:T(8,128)(2,1)}, bf16[4,256,256]{2,1,0:T(8,128)(2,1)}, u32[]{:S(2)}, u32[]{:S(2)}) collective-permute-start(bf16[4,256,256]{2,1,0:T(8,128)(2,1)} %collective-permute-done.39.w_mine_ref), channel_id=1, source_target_pairs={{8,16},{9,17},{10,18},{11,19},{12,20},{13,21},{14,22},{15,23},{16,... | collective-permute-start | bytes 1572872 | tf_op jit(solution)/shard_map/ppermute | solution.py:34
  164.6 58.8 %collective-permute-start.46 = (bf16[4,256,256]{2,1,0:T(8,128)(2,1)}, bf16[4,256,256]{2,1,0:T(8,128)(2,1)}, u32[]{:S(2)}, u32[]{:S(2)}) collective-permute-start(bf16[4,256,256]{2,1,0:T(8,128)(2,1)} %collective-permute-done.45.w_mine_ref), channel_id=1, source_target_pairs={{8,0},{9,1},{10,2},{11,3},{12,4},{13,5},{14,6},{15,7},{16,8},{17,9... | collective-permute-start | bytes 1572872 | tf_op jit(solution)/shard_map/ppermute | solution.py:34
  169.5 13.9 %collective-permute-start.7 = (bf16[16,2176]{1,0:T(8,128)(2,1)S(1)}, bf16[16,2176]{1,0:T(8,128)(2,1)S(1)}, u32[]{:S(2)}, u32[]{:S(2)}) collective-permute-start(bf16[16,2176]{1,0:T(8,128)(2,1)S(1)} %slice.20), channel_id=1, source_target_pairs={{0,8},{1,9},{2,10},{3,11},{4,12},{5,13},{6,14},{7,15},{8,16},{9,17... | collective-permute-start | bytes 208904 | tf_op jit(solution)/shard_map/ppermute | solution.py:34
  192.2 25.9 %copy-start.4 = (bf16[1536,128]{1,0:T(8,128)(2,1)}, bf16[1536,128]{1,0:T(8,128)(2,1)S(1)}, u32[]{:S(2)}) copy-start(bf16[1536,128]{1,0:T(8,128)(2,1)S(1)} %get-tuple-element.35.refs_2_) | copy-start | bytes 1179652
  192.2 20.5 %copy-start.12 = (f32[512]{0:T(512)S(1)}, f32[512]{0:T(512)}, u32[]{:S(2)}) copy-start(f32[512]{0:T(512)} %param.22) | copy-start | bytes 6148
  192.2 15.9 %collective-permute-start.24 = (f32[136,128]{1,0:T(8,128)S(1)}, f32[136,128]{1,0:T(8,128)S(1)}, u32[]{:S(2)}, u32[]{:S(2)}) collective-permute-start(f32[136,128]{1,0:T(8,128)S(1)} %get-tuple-element.37), channel_id=1, source_target_pairs={{0,8},{1,9},{2,10},{3,11},{4,12},{5,13},{6,14},{7,15},{8,16},{9,17... | collective-permute-start | bytes 208904 | tf_op jit(solution)/shard_map/ppermute | solution.py:34
  195.9 14.2 %collective-permute-start.25 = (f32[136,128]{1,0:T(8,128)S(1)}, f32[136,128]{1,0:T(8,128)S(1)}, u32[]{:S(2)}, u32[]{:S(2)}) collective-permute-start(f32[136,128]{1,0:T(8,128)S(1)} %get-tuple-element.37), channel_id=1, source_target_pairs={{0,16},{1,17},{2,18},{3,19},{4,20},{5,21},{6,22},{7,23},{8,24},{9,... | collective-permute-start | bytes 208904 | tf_op jit(solution)/shard_map/ppermute | solution.py:34
  197.2 14.2 %collective-permute-start.26 = (f32[136,128]{1,0:T(8,128)S(1)}, f32[136,128]{1,0:T(8,128)S(1)}, u32[]{:S(2)}, u32[]{:S(2)}) collective-permute-start(f32[136,128]{1,0:T(8,128)S(1)} %get-tuple-element.37), channel_id=1, source_target_pairs={{0,24},{1,25},{2,26},{3,27},{4,28},{5,29},{6,30},{7,31}} | collective-permute-start | bytes 208904 | tf_op jit(solution)/shard_map/ppermute | solution.py:34
  208.1 15.2 %copy-start.6 = (bf16[1536,128]{1,0:T(8,128)(2,1)}, bf16[1536,128]{1,0:T(8,128)(2,1)S(1)}, u32[]{:S(2)}) copy-start(bf16[1536,128]{1,0:T(8,128)(2,1)S(1)} %get-tuple-element.36.refs_3_) | copy-start | bytes 1179652
  208.1 6.5 %collective-permute-start.27 = (f32[136,128]{1,0:T(8,128)}, f32[136,128]{1,0:T(8,128)}, u32[]{:S(2)}, u32[]{:S(2)}) collective-permute-start(f32[136,128]{1,0:T(8,128)} %get-tuple-element.38), channel_id=1, source_target_pairs={{0,8},{1,9},{2,10},{3,11},{4,12},{5,13},{6,14},{7,15},{8,16},{9,17... | collective-permute-start | bytes 208904 | tf_op jit(solution)/shard_map/ppermute | solution.py:34
  210.1 8.0 %collective-permute-start.28 = (f32[136,128]{1,0:T(8,128)}, f32[136,128]{1,0:T(8,128)}, u32[]{:S(2)}, u32[]{:S(2)}) collective-permute-start(f32[136,128]{1,0:T(8,128)} %get-tuple-element.38), channel_id=1, source_target_pairs={{0,16},{1,17},{2,18},{3,19},{4,20},{5,21},{6,22},{7,23},{8,24},{9,... | collective-permute-start | bytes 208904 | tf_op jit(solution)/shard_map/ppermute | solution.py:34
  211.4 12.0 %copy-start.8 = (f32[136,128]{1,0:T(8,128)}, f32[136,128]{1,0:T(8,128)S(1)}, u32[]{:S(2)}) copy-start(f32[136,128]{1,0:T(8,128)S(1)} %collective-permute-done.26.refs_6_) | copy-start | bytes 208900
  211.4 6.7 %collective-permute-start.29 = (f32[136,128]{1,0:T(8,128)}, f32[136,128]{1,0:T(8,128)}, u32[]{:S(2)}, u32[]{:S(2)}) collective-permute-start(f32[136,128]{1,0:T(8,128)} %get-tuple-element.38), channel_id=1, source_target_pairs={{0,24},{1,25},{2,26},{3,27},{4,28},{5,29},{6,30},{7,31}} | collective-permute-start | bytes 208904 | tf_op jit(solution)/shard_map/ppermute | solution.py:34
  214.7 18.3 %collective-permute-start.35 = (bf16[4,256,256]{2,1,0:T(8,128)(2,1)}, bf16[4,256,256]{2,1,0:T(8,128)(2,1)}, u32[]{:S(2)}, u32[]{:S(2)}) collective-permute-start(bf16[4,256,256]{2,1,0:T(8,128)(2,1)} %bitcast_dynamic-update-slice_fusion.w_mine_ref), channel_id=1, source_target_pairs={{0,4},{1,5},{2,6},{3,7},{4,0},{5,1},{6,2},{7,3},{8,12},{9,13},{10,... | collective-permute-start | bytes 1572872 | tf_op jit(solution)/shard_map/ppermute | solution.py:34
  218.1 18.5 %collective-permute-start.40 = (bf16[4,256,256]{2,1,0:T(8,128)(2,1)}, bf16[4,256,256]{2,1,0:T(8,128)(2,1)}, u32[]{:S(2)}, u32[]{:S(2)}) collective-permute-start(bf16[4,256,256]{2,1,0:T(8,128)(2,1)} %collective-permute-done.39.w_mine_ref), channel_id=1, source_target_pairs={{0,4},{1,5},{2,6},{3,7},{4,0},{5,1},{6,2},{7,3},{8,12},{9,13},{10,... | collective-permute-start | bytes 1572872 | tf_op jit(solution)/shard_map/ppermute | solution.py:34
  222.8 10.1 %collective-permute-start.30 = (bf16[768,256]{1,0:T(8,128)(2,1)}, bf16[768,256]{1,0:T(8,128)(2,1)S(1)}, u32[]{:S(2)}, u32[]{:S(2)}) collective-permute-start(bf16[768,256]{1,0:T(8,128)(2,1)} %norm.3), channel_id=1, source_target_pairs={{0,4},{1,5},{2,6},{3,7},{4,0},{5,1},{6,2},{7,3},{8,12},{9,13},{10,... | collective-permute-start | bytes 1179656 | tf_op jit(solution)/shard_map/ppermute | solution.py:34
  224.5 16.5 %collective-permute-start.47 = (bf16[4,256,256]{2,1,0:T(8,128)(2,1)S(1)}, bf16[4,256,256]{2,1,0:T(8,128)(2,1)}, u32[]{:S(2)}, u32[]{:S(2)}) collective-permute-start(bf16[4,256,256]{2,1,0:T(8,128)(2,1)S(1)} %broadcast_select_fusion.w_mine_ref), channel_id=1, source_target_pairs={{0,4},{1,5},{2,6},{3,7},{4,0},{5,1},{6,2},{7,3},{8,12},{9,13},{10,... | collective-permute-start | bytes 1572872 | tf_op jit(solution)/shard_map/ppermute | solution.py:34
  224.6 19.1 %collective-permute-start.51 = (bf16[4,256,256]{2,1,0:T(8,128)(2,1)}, bf16[4,256,256]{2,1,0:T(8,128)(2,1)}, u32[]{:S(2)}, u32[]{:S(2)}) collective-permute-start(bf16[4,256,256]{2,1,0:T(8,128)(2,1)} %collective-permute-done.45.w_mine_ref), channel_id=1, source_target_pairs={{0,4},{1,5},{2,6},{3,7},{4,0},{5,1},{6,2},{7,3},{8,12},{9,13},{10,... | collective-permute-start | bytes 1572872 | tf_op jit(solution)/shard_map/ppermute | solution.py:34
  235.2 9.4 %collective-permute-start.36 = (bf16[192,512]{1,0:T(8,128)(2,1)S(1)}, bf16[192,512]{1,0:T(8,128)(2,1)S(1)}, u32[]{:S(2)}, u32[]{:S(2)}) collective-permute-start(bf16[192,512]{1,0:T(8,128)(2,1)S(1)} %get-tuple-element.40), channel_id=1, source_target_pairs={{0,1},{1,0},{2,3},{3,2},{4,5},{5,4},{6,7},{7,6},{8,9},{9,8},{10,11... | collective-permute-start | bytes 589832 | tf_op jit(solution)/shard_map/ppermute | solution.py:34
  235.7 11.0 %collective-permute-start.37 = (bf16[192,512]{1,0:T(8,128)(2,1)S(1)}, bf16[192,512]{1,0:T(8,128)(2,1)S(1)}, u32[]{:S(2)}, u32[]{:S(2)}) collective-permute-start(bf16[192,512]{1,0:T(8,128)(2,1)S(1)} %get-tuple-element.41), channel_id=1, source_target_pairs={{0,2},{1,3},{2,0},{3,1},{4,6},{5,7},{6,4},{7,5},{8,10},{9,11},{10,... | collective-permute-start | bytes 589832 | tf_op jit(solution)/shard_map/ppermute | solution.py:34
  236.6 14.3 %collective-permute-start.38 = (bf16[192,512]{1,0:T(8,128)(2,1)S(1)}, bf16[192,512]{1,0:T(8,128)(2,1)S(1)}, u32[]{:S(2)}, u32[]{:S(2)}) collective-permute-start(bf16[192,512]{1,0:T(8,128)(2,1)S(1)} %get-tuple-element.42), channel_id=1, source_target_pairs={{0,3},{1,2},{2,1},{3,0},{4,7},{5,6},{6,5},{7,4},{8,11},{9,10},{10,... | collective-permute-start | bytes 589832 | tf_op jit(solution)/shard_map/ppermute | solution.py:34
  241.0 11.4 %collective-permute-start.41 = (bf16[192,512]{1,0:T(8,128)(2,1)S(1)}, bf16[192,512]{1,0:T(8,128)(2,1)S(1)}, u32[]{:S(2)}, u32[]{:S(2)}) collective-permute-start(bf16[192,512]{1,0:T(8,128)(2,1)S(1)} %get-tuple-element.44), channel_id=1, source_target_pairs={{0,1},{1,0},{2,3},{3,2},{4,5},{5,4},{6,7},{7,6},{8,9},{9,8},{10,11... | collective-permute-start | bytes 589832 | tf_op jit(solution)/shard_map/ppermute | solution.py:34
  243.7 12.1 %collective-permute-start.42 = (bf16[192,512]{1,0:T(8,128)(2,1)S(1)}, bf16[192,512]{1,0:T(8,128)(2,1)S(1)}, u32[]{:S(2)}, u32[]{:S(2)}) collective-permute-start(bf16[192,512]{1,0:T(8,128)(2,1)S(1)} %get-tuple-element.45), channel_id=1, source_target_pairs={{0,2},{1,3},{2,0},{3,1},{4,6},{5,7},{6,4},{7,5},{8,10},{9,11},{10,... | collective-permute-start | bytes 589832 | tf_op jit(solution)/shard_map/ppermute | solution.py:34
  244.6 12.7 %collective-permute-start.43 = (bf16[192,512]{1,0:T(8,128)(2,1)S(1)}, bf16[192,512]{1,0:T(8,128)(2,1)S(1)}, u32[]{:S(2)}, u32[]{:S(2)}) collective-permute-start(bf16[192,512]{1,0:T(8,128)(2,1)S(1)} %get-tuple-element.46), channel_id=1, source_target_pairs={{0,3},{1,2},{2,1},{3,0},{4,7},{5,6},{6,5},{7,4},{8,11},{9,10},{10,... | collective-permute-start | bytes 589832 | tf_op jit(solution)/shard_map/ppermute | solution.py:34
  246.8 13.2 %collective-permute-start.48 = (bf16[192,512]{1,0:T(8,128)(2,1)S(1)}, bf16[192,512]{1,0:T(8,128)(2,1)S(1)}, u32[]{:S(2)}, u32[]{:S(2)}) collective-permute-start(bf16[192,512]{1,0:T(8,128)(2,1)S(1)} %get-tuple-element.48), channel_id=1, source_target_pairs={{0,1},{1,0},{2,3},{3,2},{4,5},{5,4},{6,7},{7,6},{8,9},{9,8},{10,11... | collective-permute-start | bytes 589832 | tf_op jit(solution)/shard_map/ppermute | solution.py:34
  250.9 13.2 %collective-permute-start.49 = (bf16[192,512]{1,0:T(8,128)(2,1)S(1)}, bf16[192,512]{1,0:T(8,128)(2,1)S(1)}, u32[]{:S(2)}, u32[]{:S(2)}) collective-permute-start(bf16[192,512]{1,0:T(8,128)(2,1)S(1)} %get-tuple-element.49), channel_id=1, source_target_pairs={{0,2},{1,3},{2,0},{3,1},{4,6},{5,7},{6,4},{7,5},{8,10},{9,11},{10,... | collective-permute-start | bytes 589832 | tf_op jit(solution)/shard_map/ppermute | solution.py:34
  252.4 12.5 %collective-permute-start.50 = (bf16[192,512]{1,0:T(8,128)(2,1)S(1)}, bf16[192,512]{1,0:T(8,128)(2,1)S(1)}, u32[]{:S(2)}, u32[]{:S(2)}) collective-permute-start(bf16[192,512]{1,0:T(8,128)(2,1)S(1)} %get-tuple-element.50), channel_id=1, source_target_pairs={{0,3},{1,2},{2,1},{3,0},{4,7},{5,6},{6,5},{7,4},{8,11},{9,10},{10,... | collective-permute-start | bytes 589832 | tf_op jit(solution)/shard_map/ppermute | solution.py:34
  255.8 12.6 %collective-permute-start.52 = (bf16[192,512]{1,0:T(8,128)(2,1)S(1)}, bf16[192,512]{1,0:T(8,128)(2,1)S(1)}, u32[]{:S(2)}, u32[]{:S(2)}) collective-permute-start(bf16[192,512]{1,0:T(8,128)(2,1)S(1)} %get-tuple-element.52), channel_id=1, source_target_pairs={{0,1},{1,0},{2,3},{3,2},{4,5},{5,4},{6,7},{7,6},{8,9},{9,8},{10,11... | collective-permute-start | bytes 589832 | tf_op jit(solution)/shard_map/ppermute | solution.py:34
  257.3 11.6 %collective-permute-start.53 = (bf16[192,512]{1,0:T(8,128)(2,1)S(1)}, bf16[192,512]{1,0:T(8,128)(2,1)S(1)}, u32[]{:S(2)}, u32[]{:S(2)}) collective-permute-start(bf16[192,512]{1,0:T(8,128)(2,1)S(1)} %get-tuple-element.53), channel_id=1, source_target_pairs={{0,2},{1,3},{2,0},{3,1},{4,6},{5,7},{6,4},{7,5},{8,10},{9,11},{10,... | collective-permute-start | bytes 589832 | tf_op jit(solution)/shard_map/ppermute | solution.py:34
  259.9 12.5 %collective-permute-start.54 = (bf16[192,512]{1,0:T(8,128)(2,1)S(1)}, bf16[192,512]{1,0:T(8,128)(2,1)S(1)}, u32[]{:S(2)}, u32[]{:S(2)}) collective-permute-start(bf16[192,512]{1,0:T(8,128)(2,1)S(1)} %get-tuple-element.54), channel_id=1, source_target_pairs={{0,3},{1,2},{2,1},{3,0},{4,7},{5,6},{6,5},{7,4},{8,11},{9,10},{10,... | collective-permute-start | bytes 589832 | tf_op jit(solution)/shard_map/ppermute | solution.py:34
  (7 other events, 14.1 us)
where the time goes:
time: 278 us; the launch traced here: 274 us
  waiting for transfers between devices  101 us (36%)
  starting transfers between devices  81.1 us (29%)
  Pallas kernels  44.7 us (16%)
  local copies, waits for them, and re-layouts  40.7 us (15%)
  other arithmetic  5.48 us (2%)
    ppermute x55, waiting for transfers between devices, shift(): return lax.ppermute(array, both, pairs)  101 us
    ppermute x55, starting transfers between devices, shift(): return lax.ppermute(array, both, pairs)  81.1 us
    pallas_call x2, Pallas kernels, scan(): pl.pallas_call(functools.partial(scan_kernel, first_head, head, experts,...  18.2 us
    dynamic_update_slice x8, local copies, waits for them, and re-layouts, on_device(): plane = lax.dynamic_update_slice(plane, block, (at, 0))  12.4 us
    pallas_call x1, Pallas kernels, maps(): pl.pallas_call(functools.partial(maps_kernel, heads, width), grid=(count...  9.86 us
    pallas_call x4, Pallas kernels, project_out(): pl.pallas_call(functools.partial(out_kernel, experts, groups), in_specs=[...  8.82 us
    unnamed x34, local copies, waits for them, and re-layouts  7.86 us
    pallas_call x2, Pallas kernels, norm(): pl.pallas_call(functools.partial(norm_kernel, chunks, before, head, chann...  6.49 us
  transfers between devices with their start and end apart: 55, of which 20 were waited for; matrix products, arithmetic and copies ran while one was open for 13% of the time, Pallas kernels for 16%

commit v1 on v0

--- a/solution.py
+++ b/solution.py
@@ -34,20 +34,33 @@
     return lax.ppermute(array, both, pairs)
 
 
-def line_gather(own, depth):
-    if depth == 1:
-        return [own], []
-    first = shift(own, lambda z, k, e: ((z + 1) % depth, k, e))
-    last = shift(own, lambda z, k, e: ((z - 1) % depth, k, e)) if depth > 2 else None
+def line_near(own, depth):
+    return (
+        shift(own, lambda z, k, e: ((z + 1) % depth, k, e)),
+        shift(own, lambda z, k, e: ((z - 1) % depth, k, e)),
+    )
+
+
+def step_up(array, s, depth):
+    return shift(array, lambda z, k, e: (z + 1, k, e) if s - 1 <= z < depth - 1 else None)
+
+
+def step_down(array, s, depth):
+    return shift(array, lambda z, k, e: (z - 1, k, e) if 0 < z <= depth - s else None)
+
+
+def line_far(near, depth):
     ups, downs = [], []
-    up, down = first, last
+    up, down = near
     for s in range(2, depth - 1):
-        up = shift(up, lambda z, k, e: (z + 1, k, e) if s - 1 <= z < depth - 1 else None)
-        down = shift(down, lambda z, k, e: (z - 1, k, e) if 0 < z <= depth - s else None)
+        up, down = step_up(up, s, depth), step_down(down, s, depth)
         ups.append(up)
         downs.append(down)
-    middle = [(ups[s - 2], downs[depth - s - 2]) for s in range(2, depth - 1)]
-    return [own, first] + ([last] if depth > 2 else []), middle
+    return paired(ups, downs)
+
+
+def paired(ups, downs):
+    return list(zip(ups, downs[::-1]))
 
 
 def maps_kernel(heads, width, x_ref, w_ref, bias_ref, rate_ref, maps_ref, cols_ref, rows_ref, total):
@@ -108,7 +121,8 @@
 ):
     slots = refs[: near + 2 * middle]
     maps_ref, cols_ref, rows_ref, taps_ref, skip_ref = refs[near + 2 * middle :][:5]
-    y_ref, gate_ref, final_ref, whole, seen, state = refs[near + 2 * middle + 5 :]
+    earlier = refs[near + 2 * middle + 5 : -6]
+    y_ref, gate_ref, final_ref, whole, seen, state = refs[-6:]
     length, channels = y_ref.shape
     taps = taps_ref.shape[0]
     width_state = maps_ref.shape[1] // 2
@@ -194,16 +208,25 @@
 
     @pl.when(step == pl.num_programs(0) - 1)
     def _():
-        final_ref[:width_state, :] = state[...]
-        final_ref[width_state:, :] = jnp.broadcast_to(reached, (8, channels))
-
-
-def scan(z, tokens, edge, slots, middle, found, taps, skip, first_head, head, experts, depth, width, length):
+        here = slice(first_head * head, first_head * head + channels)
+        for ref in earlier:
+            final_ref[:, : first_head * head] = ref[...]
+        final_ref[:width_state, here] = state[...].astype(bf16)
+        place = lax.broadcasted_iota(jnp.int32, (16, channels), 0)
+        first = reached.astype(bf16).astype(f32)
+        second = (reached - first).astype(bf16).astype(f32)
+        third = reached - first - second
+        parts = jnp.where(place == 0, first, jnp.where(place == 1, second, third))
+        final_ref[width_state:, here] = parts.astype(bf16)
+
+
+def scan(z, tokens, edge, slots, middle, found, taps, skip, earlier, first_head, head, experts, depth, width, length):
     maps_all, cols, rows = found
     count, channels = tokens.shape[0], taps.shape[1]
     width_state = maps_all.shape[1] // 2
     flat = list(slots) + [part for pair in middle for part in pair]
     block = lambda *shape: pl.BlockSpec(shape, lambda b, _: (b, 0))
+    final_shape = (width_state + 16, first_head * head + channels)
     return pl.pallas_call(
         functools.partial(
             scan_kernel, first_head, head, experts, depth, width, len(slots), len(middle)
@@ -219,11 +242,12 @@
                 pl.BlockSpec((rows.shape[0], length), lambda b, _: (0, b)),
                 vmem(*taps.shape),
                 vmem(*skip.shape),
-            ],
+            ]
+            + [vmem(*part.shape) for part in earlier],
             out_specs=[
                 block(length, channels),
                 block(length, channels),
-                pl.BlockSpec((width_state + 8, channels), lambda b, _: (0, 0)),
+                pl.BlockSpec(final_shape, lambda b, _: (0, 0)),
             ],
             scratch_shapes=[
                 pltpu.VMEM((experts, width, 2 * channels), bf16),
@@ -234,31 +258,29 @@
         out_shape=[
             jax.ShapeDtypeStruct((count, channels), f32),
             jax.ShapeDtypeStruct((count, channels), bf16),
-            jax.ShapeDtypeStruct((width_state + 8, channels), f32),
+            jax.ShapeDtypeStruct(final_shape, bf16),
         ],
         compiler_params=params(48),
         name="scan",
-    )(z, tokens, edge, *flat, maps_all, cols, rows, taps, skip)
+    )(z, tokens, edge, *flat, maps_all, cols, rows, taps, skip, *earlier)
 
 
 def norm_kernel(chunks, before, head, heads, pos_ref, maps_ref, cols_ref, gain_ref, *refs):
-    ys, gates = refs[:chunks], refs[chunks : 2 * chunks]
-    finals = refs[2 * chunks : 2 * chunks + chunks * before]
-    out_ref, entering = refs[2 * chunks + chunks * before :]
+    ys, gates, finals = refs[:chunks], refs[chunks : 2 * chunks], refs[2 * chunks : 2 * chunks + before]
+    theirs_ref, mine_ref, entering = refs[2 * chunks + before :]
     width_state = maps_ref.shape[1] // 2
-    channels = out_ref.shape[1]
-    each = channels // chunks
-
-    @pl.when(pl.program_id(0) == 0)
+    channels = mine_ref.shape[1]
+    step, steps = pl.program_id(0), pl.num_programs(0)
+
+    @pl.when(step == 0)
     def _():
-        for q in range(chunks):
-            total = jnp.zeros((width_state, each), f32)
-            logs = jnp.zeros((1, each), f32)
-            for s in range(before):
-                ref = finals[q * before + s]
-                total = total + jnp.exp(logs) * ref[:width_state, :]
-                logs = logs + ref[width_state : width_state + 1, :]
-            entering[:, q * each : (q + 1) * each] = total.astype(bf16)
+        total = jnp.zeros((width_state, channels), f32)
+        logs = jnp.zeros((1, channels), f32)
+        for ref in finals:
+            total = total + jnp.exp(logs) * ref[:width_state, :].astype(f32)
+            parts = ref[width_state:, :].astype(f32)
+            logs = logs + (parts[0:1] + parts[1:2] + parts[2:3])
+        entering[...] = total.astype(bf16)
 
     lane = lax.broadcasted_iota(jnp.int32, (1, channels), 1)
     growth = 0.0
@@ -274,104 +296,175 @@
     col = lax.broadcasted_iota(jnp.int32, (channels, channels), 1) // head
     same = (row == col).astype(f32)
     square = jnp.dot(gated * gated, same, precision=highest, preferred_element_type=f32) * (1.0 / head)
-    out_ref[...] = (gated * lax.rsqrt(square + 1e-05) * gain_ref[...]).astype(bf16)
-
-
-def norm(part, found, gain, ys, gates, finals, head, length):
+    normed = (gated * lax.rsqrt(square + 1e-05) * gain_ref[...]).astype(bf16)
+
+    @pl.when(step < steps // 2)
+    def _():
+        theirs_ref[...] = normed
+
+    @pl.when(step >= steps // 2)
+    def _():
+        mine_ref[...] = normed
+
+
+def norm(core, found, gain, ys, gates, finals, head, length):
     maps_all, cols, _ = found
     count, channels = maps_all.shape[0] // 2, gain.shape[1]
-    chunks, before = len(ys), len(finals[0])
+    chunks, before = len(ys), len(finals)
     steps = count // length
-    block = lambda *shape: pl.BlockSpec(shape, lambda b, at: (at[0] * steps + b, 0))
-    flat = [array for group in finals for array in group]
+    at = lambda b, core: (jnp.where(b < steps, 1 - core[0], core[0]) * steps + lax.rem(b, steps), 0)
+    block = lambda *shape: pl.BlockSpec(shape, at)
     return pl.pallas_call(
         functools.partial(norm_kernel, chunks, before, head, channels // head),
         grid_spec=pltpu.PrefetchScalarGridSpec(
             num_scalar_prefetch=1,
-            grid=(steps,),
+            grid=(2 * steps,),
             in_specs=[block(length, maps_all.shape[1]), block(length, 128), vmem(*gain.shape)]
             + [block(length, channels // chunks)] * (2 * chunks)
-            + [vmem(*array.shape) for array in flat],
-            out_specs=pl.BlockSpec((length, channels), lambda b, _: (b, 0)),
+            + [vmem(*array.shape) for array in finals],
+            out_specs=[
+                pl.BlockSpec((length, channels), lambda b, _: (jnp.minimum(b, steps - 1), 0)),
+                pl.BlockSpec((length, channels), lambda b, _: (jnp.maximum(b - steps, 0), 0)),
+            ],
             scratch_shapes=[pltpu.VMEM((maps_all.shape[1] // 2, channels), bf16)],
         ),
-        out_shape=jax.ShapeDtypeStruct((count, channels), bf16),
+        out_shape=[jax.ShapeDtypeStruct((count, channels), bf16)] * 2,
         compiler_params=params(32),
         name="norm",
-    )(part, maps_all, cols, gain, *ys, *gates, *flat)
-
-
-def out_kernel(experts, groups, pos_ref, ids_ref, mine_ref, other_ref, w_mine_ref, w_other_ref, *outs):
+    )(core, maps_all, cols, gain, *ys, *gates, *finals)
+
+
+def out_kernel(experts, groups, planes, depth, pos_ref, ids_ref, mine_ref, other_ref, *refs):
+    weights, outs = refs[:-groups], refs[-groups:]
     group, width = pos_ref[0], mine_ref.shape[0] // groups
-    chunk = w_mine_ref.shape[2]
+    chunk = weights[0].shape[-1]
+    pairs = []
+    for s in planes:
+        if s == 0 and len(weights) > 1:
+            pairs.append([weights[0][...], weights[1][...]])
+            continue
+        z = lax.rem(pos_ref[2] - s + depth, depth)
+        pairs.append([weights[0][2 * z + pos_ref[1]], weights[0][2 * z + 1 - pos_ref[1]]])
     for s in range(groups):
         rows = pl.ds(pl.multiple_of(jnp.bitwise_xor(group, s) * width, 64), width)
         chosen = ids_ref[rows, :].astype(f32)[:, 0:1]
         mine, other = mine_ref[rows, :], other_ref[rows, :]
-        zero = jnp.zeros_like(mine)
-        for k in range(2):
-            total = jnp.zeros((width, chunk), f32)
-            for e in range(experts):
-                total += jnp.dot(jnp.where(chosen == e, mine, zero), w_mine_ref[2 * e + k], preferred_element_type=f32)
-                total += jnp.dot(jnp.where(chosen == e, other, zero), w_other_ref[2 * e + k], preferred_element_type=f32)
-            outs[s][:, k * chunk : (k + 1) * chunk] = total.astype(bf16)
-
-
-def project_out(group, ids, mine, other, w_mine, w_other, groups):
-    experts, chunk = w_mine.shape[0] // 2, w_mine.shape[2]
+        second = pos_ref[1] == 1
+        both_halves = jnp.concatenate([jnp.where(second, other, mine), jnp.where(second, mine, other)], axis=1)
+        zero = jnp.zeros_like(both_halves)
+        masked = jnp.concatenate([jnp.where(chosen == e, both_halves, zero) for e in range(experts)], axis=1)
+        for at, weight in enumerate(weight for pair in pairs for weight in pair):
+            total = jnp.dot(masked, weight, preferred_element_type=f32)
+            outs[s][:, at * chunk : (at + 1) * chunk] = total.astype(bf16)
+
+
+def project_out(position, ids, mine, other, weights, planes, depth, groups):
     rows = mine.shape[0] // groups
     whole = pl.BlockSpec(memory_space=pltpu.VMEM)
-    return pl.pallas_call(
-        functools.partial(out_kernel, experts, groups),
-        in_specs=[pl.BlockSpec(memory_space=pltpu.SMEM)] + [whole] * 5,
+    shape = jax.ShapeDtypeStruct((rows, 2 * len(planes) * weights[0].shape[-1]), bf16)
+    return pl.pallas_call(
+        functools.partial(out_kernel, groups // 2, groups, planes, depth),
+        in_specs=[pl.BlockSpec(memory_space=pltpu.SMEM)] + [whole] * (3 + len(weights)),
         out_specs=[whole] * groups,
-        out_shape=[jax.ShapeDtypeStruct((rows, 2 * chunk), bf16)] * groups,
+        out_shape=[shape] * groups,
         compiler_params=params(48),
         name="project_out",
-    )(group, ids, mine, other, w_mine, w_other)
-
-
-def sum_kernel(depth, groups, pos_ref, *refs):
+    )(position, ids, mine, other, *weights)
+
+
+def sum_kernel(depth, groups, planes, pos_ref, *refs):
     out_ref = refs[-1]
-    for s in range(depth):
-        parts = refs[s * groups : (s + 1) * groups]
-        total = parts[0][...].astype(f32)
-        for part in parts[1:]:
-            total = total + part[...].astype(f32)
-        wide = total.shape[1]
-        at = pl.multiple_of(lax.rem(pos_ref[0] - s + depth, depth) * wide, 128)
-        out_ref[:, pl.ds(at, wide)] = total.astype(bf16)
-
-
-def add_up(z, parts, depth, groups):
-    rows, wide = parts[0].shape
+    chunk = out_ref.shape[1] // (2 * depth)
+    for at, several in enumerate(planes):
+        blocks = refs[at * groups : (at + 1) * groups]
+        total = blocks[0][...].astype(f32)
+        for block in blocks[1:]:
+            total = total + block[...].astype(f32)
+        total = total.astype(bf16)
+        for place, s in enumerate(several):
+            z = lax.rem(pos_ref[2] - s + depth, depth)
+            for j in range(2):
+                core = pos_ref[1] if j == 0 else 1 - pos_ref[1]
+                to = pl.multiple_of((2 * z + core) * chunk, 128)
+                span = slice((2 * place + j) * chunk, (2 * place + j + 1) * chunk)
+                out_ref[:, pl.ds(to, chunk)] = total[:, span]
+
+
+def add_up(position, blocks, planes, depth, width):
+    groups, rows = len(blocks[0]), blocks[0][0].shape[0]
+    flat = [block for several in blocks for block in several]
     whole = pl.BlockSpec(memory_space=pltpu.VMEM)
     return pl.pallas_call(
-        functools.partial(sum_kernel, depth, groups),
-        in_specs=[pl.BlockSpec(memory_space=pltpu.SMEM)] + [whole] * len(parts),
+        functools.partial(sum_kernel, depth, groups, planes),
+        in_specs=[pl.BlockSpec(memory_space=pltpu.SMEM)] + [whole] * len(flat),
         out_specs=whole,
-        out_shape=jax.ShapeDtypeStruct((rows, depth * wide), bf16),
+        out_shape=jax.ShapeDtypeStruct((rows, width), bf16),
         compiler_params=params(48),
         name="add_up",
-    )(z, *parts)
-
-
-def spread_pieces(piece_of, groups):
-    index = 2 * (lax.axis_index("exp") // 2) + lax.axis_index("ctx") % 2
+    )(position, *flat)
+
+
+def spread_pieces(sent):
     return [
-        shift(
-            piece_of(jnp.bitwise_xor(index, r)),
-            lambda z, k, e: (z, e % 2, (2 * (e // 2) + k) ^ r),
-        )
-        for r in range(groups)
+        shift(block, lambda z, k, e: (z, e % 2, (2 * (e // 2) + k) ^ r)) for r, block in enumerate(sent)
     ]
 
 
-def arrange(blocks, group):
-    stacked = jnp.zeros((len(blocks),) + blocks[0].shape, blocks[0].dtype)
-    for r, block in enumerate(blocks):
-        stacked = lax.dynamic_update_index_in_dim(stacked, block, jnp.bitwise_xor(group, r), 0)
-    return stacked
+def arrange_kernel(blocks, by_rows, pos_ref, *refs):
+    outs = refs[blocks:]
+    for r, ref in enumerate(refs[:blocks]):
+        to = jnp.bitwise_xor(pos_ref[0], r)
+        for at, out in enumerate(outs):
+            if by_rows:
+                out[to] = ref[at * out.shape[1] : (at + 1) * out.shape[1], :]
+                continue
+            channels = out.shape[2] // 2
+            for j in range(2):
+                first = (j * len(outs) + at) * channels
+                out[to, :, j * channels : (j + 1) * channels] = ref[:, first : first + channels]
+
+
+def arrange(blocks, group, parts, by_rows):
+    whole = pl.BlockSpec(memory_space=pltpu.VMEM)
+    rows, width = blocks[0].shape
+    shape = (len(blocks), rows // parts, width) if by_rows else (len(blocks), rows, width // parts)
+    return pl.pallas_call(
+        functools.partial(arrange_kernel, len(blocks), by_rows),
+        in_specs=[pl.BlockSpec(memory_space=pltpu.SMEM)] + [whole] * len(blocks),
+        out_specs=[whole] * parts,
+        out_shape=[jax.ShapeDtypeStruct(shape, blocks[0].dtype)] * parts,
+        compiler_params=params(32),
+        name="arrange",
+    )(group, *blocks)
+
+
+def cut_kernel(pos_ref, flat_ref, *outs):
+    piece = outs[0].shape[1] // 2
+    half = flat_ref.shape[1] // 2
+    for r, out in enumerate(outs):
+        for j in range(2):
+            at = pl.multiple_of(j * half + jnp.bitwise_xor(pos_ref[0], r) * piece, 128)
+            out[:, j * piece : (j + 1) * piece] = flat_ref[:, pl.ds(at, piece)]
+
+
+def cut(index, flat, groups):
+    rows, half = flat.shape[0], flat.shape[1] // 2
+    piece = half // groups
+    if piece % 128:
+        at = lambda j, r: j * half + jnp.bitwise_xor(index[0], r) * piece
+        return [
+            jnp.concatenate([lax.dynamic_slice(flat, (0, at(j, r)), (rows, piece)) for j in range(2)], axis=1)
+            for r in range(groups)
+        ]
+    whole = pl.BlockSpec(memory_space=pltpu.VMEM)
+    return pl.pallas_call(
+        cut_kernel,
+        in_specs=[pl.BlockSpec(memory_space=pltpu.SMEM), whole],
+        out_specs=[whole] * groups,
+        out_shape=[jax.ShapeDtypeStruct((rows, 2 * piece), flat.dtype)] * groups,
+        compiler_params=params(32),
+        name="cut",
+    )(index, flat)
 
 
 def on_device(
@@ -385,42 +478,34 @@
     piece = half // groups
     heads = rate.shape[0] // 2
     head = piece // heads
-    chunks = 2 if piece % 256 == 0 else 1
-    channels = piece // chunks
     count = 2 * groups * rows
     length = 256 if count % 512 == 0 else 128
     scalar = lambda v: jnp.reshape(v, (1,)).astype(jnp.int32)
-    z_at, group_at = scalar(z), scalar(group)
+    z_at, group_at, core_at = scalar(z), scalar(group), scalar(core)
     depth_weight = in_weight.shape[1]
-
-    flat = in_weight[0].reshape(depth_weight, 2 * half)
-    in_slots = []
-    for q in range(chunks):
-
-        def piece_of(p):
-            at = p * piece + q * channels
-            return jnp.concatenate(
-                [lax.dynamic_slice(flat, (0, j * half + at), (depth_weight, channels)) for j in range(2)],
-                axis=1,
-            )
-
-        shard = arrange(spread_pieces(piece_of, groups), group)
-        shard = shard.reshape(groups * depth_weight, 2 * channels)
-        in_slots.append(line_gather(shard, depth))
+    swap = lambda array: shift(array, lambda z, k, e: (z, 1 - k, e))
+    phase = lax.optimization_barrier
 
     added = jnp.concatenate(
         [expert_ids.astype(bf16), damping[:, None], jnp.zeros((rows, extra - 2), bf16)], axis=1
     )
     wide = jnp.concatenate([tokens, added], axis=1)
-    own = [wide] + [shift(wide, lambda z, k, e: (z, k, e ^ s)) for s in range(1, groups)]
-    swapped = [shift(block, lambda z, k, e: (z, 1 - k, e)) for block in own]
-    plane = jnp.zeros((count, width + extra), bf16)
-    for where, blocks in ((core, own), (1 - core, swapped)):
-        for s, block in enumerate(blocks):
-            at = (where * groups + jnp.bitwise_xor(group, s)) * rows
-            plane = lax.dynamic_update_slice(plane, block, (at, 0))
-    edge = shift(plane[count - halo :], lambda z, k, e: (z + 1, k, e) if z + 1 < depth else None)
-
+    planes = [[2 * i * groups + j for j in range(2 * groups)] for i in range(depth)]
+    flat = in_weight[0].reshape(depth_weight, 2 * half)
+    index = scalar(2 * (group // 2) + core)
+    got = spread_pieces(cut(index, flat, groups))
+    got, wide, out_weight, w_bc, w_dt, rate, dt_bias, d_skip, gain, conv_weight = phase(
+        (got, wide, out_weight, w_bc, w_dt, rate, dt_bias, d_skip, gain, conv_weight)
+    )
+
+    plane = lax.all_gather(wide, both, axis=0, tiled=True, axis_index_groups=planes)
+    (shard,) = arrange(got, group_at, 1, False)
+    shard = shard.reshape(groups * depth_weight, 2 * piece)
+    near = line_near(shard, depth)
+    columns = out_weight.shape[2]
+    out_shard = lax.all_to_all(
+        out_weight[0].reshape(groups, piece, columns), "exp", 0, 0, tiled=True
+    ).reshape(half, columns)
     local = lambda vector: lax.dynamic_slice_in_dim(vector, core * heads, heads, 0)
     lanes = lambda vector: jnp.concatenate(
         [jnp.pad(local(vector), (0, dt_lane - heads))] * (128 // dt_lane)
@@ -428,49 +513,49 @@
     picked = lax.dynamic_slice_in_dim(w_dt, (2 * group + core) * heads, heads, 0)
     picked = jnp.concatenate([jnp.pad(picked, ((0, dt_lane - heads), (0, 0)))] * (128 // dt_lane), axis=0)
     w_maps = jnp.concatenate([w_bc, picked.T], axis=1)
-    found = maps(plane, w_maps, lanes(dt_bias), lanes(rate), heads, w_bc.shape[1], length)
-
+    bias_lanes, rate_lanes = lanes(dt_bias), lanes(rate)
     half_taps = lax.dynamic_slice_in_dim(conv_weight, core * piece, piece, 1)
     half_gain = lax.dynamic_slice_in_dim(gain, core * piece, piece, 0)[None, :]
     half_skip = jnp.repeat(local(d_skip), head)[None, :]
-    ys, gates, finals = [], [], []
-    for q in range(chunks):
-        span = slice(q * channels, (q + 1) * channels)
-        y, gate, final = scan(
-            z_at, plane, edge, *in_slots[q], found, half_taps[:, span], half_skip[:, span],
-            q * channels // head, head, experts, depth, width, length,
-        )
-        ys.append(y)
-        gates.append(gate)
-        finals.append(
-            [
-                shift(final, lambda z, k, e: (z + s, k, e) if z + s < depth else None)
-                for s in range(1, depth)
-            ]
-        )
-
-    out_flat = out_weight[0]
-    out_blocks = spread_pieces(
-        lambda p: lax.dynamic_slice_in_dim(out_flat, p * piece, piece, 0), groups
-    )
-    near, middle = line_gather(arrange(out_blocks, group), depth)
-    ordered = near[:2] + [
-        jnp.where(z >= s + 2, up, down) for s, (up, down) in enumerate(middle)
-    ] + near[2:]
-    other_half = [shift(array, lambda z, k, e: (z, 1 - k, e)) for array in ordered]
-
-    theirs = norm(scalar(1 - core), found, half_gain, ys, gates, finals, head, length)
-    other = shift(theirs, lambda z, k, e: (z, 1 - k, e))
-    mine = norm(scalar(core), found, half_gain, ys, gates, finals, head, length)
-
+    shard, near, out_shard, w_maps, bias_lanes, rate_lanes, half_taps, half_gain, half_skip = phase(
+        (shard, near, out_shard, w_maps, bias_lanes, rate_lanes, half_taps, half_gain, half_skip)
+    )
+
+    far = line_far(near, depth)
+    edge = shift(plane[count - halo :], lambda z, k, e: (z + 1, k, e) if z + 1 < depth else None)
+    found = maps(plane, w_maps, bias_lanes, rate_lanes, heads, w_bc.shape[1], length)
     ids = lax.dynamic_slice(plane, (core * groups * rows, width), (groups * rows, extra))
-    blocks = []
-    for s in range(depth):
-        results = project_out(group_at, ids, mine, other, ordered[s], other_half[s], groups)
-        blocks += [results[0]] + [
+    far, plane, edge, found, out_shard, ids = phase((far, plane, edge, found, out_shard, ids))
+
+    whole_out = lax.all_gather(out_shard, "ctx", axis=0)
+    y, gate, final = scan(
+        z_at, plane, edge, [shard, *near], far, found, half_taps, half_skip,
+        [], 0, head, experts, depth, width, length,
+    )
+    y, gate, final, out_shard = phase((y, gate, final, out_shard))
+
+    finals = [
+        shift(final, lambda z, k, e: (z + s, k, e) if z + s < depth else None) for s in range(1, depth)
+    ]
+    theirs, mine = norm(core_at, found, half_gain, [y], [gate], finals, head, length)
+    out_other = swap(out_shard)
+    theirs, out_other = phase((theirs, out_other))
+    other = swap(theirs)
+    other, mine = phase((other, mine))
+
+    position = jnp.concatenate([group_at, core_at, z_at])
+
+    def send(weights, planes):
+        results = project_out(position, ids, mine, other, weights, planes, depth, groups)
+        return [results[0]] + [
             shift(results[r], lambda z, k, e: (z, k, e ^ r)) for r in range(1, groups)
         ]
-    return add_up(z_at, blocks, depth, groups)
+
+    order = [(0,), tuple(range(1, depth))]
+    blocks = [send([out_shard, out_other], order[0])]
+    whole_out, blocks = phase((whole_out, blocks))
+    blocks.append(send([whole_out], order[1]))
+    return add_up(position, blocks, order, depth, width)
 
 
 def solution(mesh):

time: 278 us -> 206 us (0.74); the launches traced: 274 us -> 206 us
  starting transfers between devices: 81.1 us -> 36.2 us
  local copies, waits for them, and re-layouts: 40.7 us -> 19 us
  between operations: 0.85 us -> 13.7 us
  Pallas kernels: 44.7 us -> 36.6 us
  other arithmetic: 5.48 us -> 1.63 us
    ppermute x55 -> x20, starting transfers between devices: 81.1 us -> 32.6 us  [shift(): return lax.ppermute(array, both, pairs)]
    dynamic_update_slice x20 -> x0, local copies, waits for them, and re-layouts: 16.9 us -> none  [the longest x8 12.4 us: on_device(): plane = lax.dynamic_update_slice(plane, block, (at, 0))]
    ppermute x55 -> x20, waiting for transfers between devices: 101 us -> 95.7 us  [shift(): return lax.ppermute(array, both, pairs)]
    all_to_all x0 -> x1, starting transfers between devices: none -> 3.47 us  [on_device(): lax.all_to_all(out_weight[0].reshape(groups, piece, columns), 'exp', 0, 0...]
    broadcast_in_dim x1 -> x0, local copies, waits for them, and re-layouts: 3.16 us -> none  [on_device(): plane = jnp.zeros((count, width + extra), bf16)]
    all_to_all x0 -> x1, waiting for transfers between devices: none -> 2.84 us  [on_device(): lax.all_to_all(out_weight[0].reshape(groups, piece, columns), 'exp', 0, 0...]
    pallas_call x2 -> x1, Pallas kernels: 18.2 us -> 15.6 us  [scan(): pl.pallas_call(functools.partial(scan_kernel, first_head, head, experts,...]
    pallas_call x2 -> x1, Pallas kernels: 6.49 us -> 3.96 us  [norm(): pl.pallas_call(functools.partial(norm_kernel, chunks, before, head, chann...]
  transfers between devices with their start and end apart: 55 -> 23, of which waited for: 20 -> 15; matrix products, arithmetic and copies ran while one was open for 13% -> 5% of each run, Pallas kernels for 16% -> 14%
where the time goes in v1:
time: 206 us
  waiting for transfers between devices  98.6 us (48%)
  Pallas kernels  36.6 us (18%)
  starting transfers between devices  36.2 us (18%)
  local copies, waits for them, and re-layouts  19 us (9%)
  between operations  13.7 us (7%)
    ppermute x20, waiting for transfers between devices, shift(): return lax.ppermute(array, both, pairs)  95.7 us
    ppermute x20, starting transfers between devices, shift(): return lax.ppermute(array, both, pairs)  32.6 us
    pallas_call x1, Pallas kernels, scan(): pl.pallas_call(functools.partial(scan_kernel, first_head, head, experts,...  15.6 us
    unnamed x35, local copies, waits for them, and re-layouts  9.99 us
    pallas_call x1, Pallas kernels, maps(): pl.pallas_call(functools.partial(maps_kernel, heads, width), grid=(count...  8.59 us
    pallas_call x2, Pallas kernels, project_out(): pl.pallas_call(functools.partial(out_kernel, groups // 2, groups, planes,...  6.52 us
    concatenate x1, local copies, waits for them, and re-layouts, on_device(): jnp.concatenate([jnp.pad(picked, ((0, dt_lane - heads), (0, 0)))] * (128...  5.57 us
  transfers between devices with their start and end apart: 23, of which 15 were waited for; matrix products, arithmetic and copies ran while one was open for 5% of the time, Pallas kernels for 14%

profile of v1, /device:TPU:16, one launch (start us, length us, event | category | flops | bytes accessed | tf_op | source)
XLA Modules:
  0.0 205.8 jit_solution(4262731402785093977)
XLA Ops:
  6.6 1.6 copy.18
  8.2 0.1 cut.1
  8.3 0.8 collective-permute-start
  9.2 2.7 %collective-permute-start.1 = (bf16[256,512]{1,0:T(8,128)(2,1)S(1)}, bf16[256,512]{1,0:T(8,128)(2,1)S(1)}, u32[]{:S(2)}, u32[]{:S(2)}) collective-permute-start(bf16[256,512]{1,0:T(8,128)(2,1)S(1)} %get-tuple-element.71), channel_id=1, source_target_pairs={{0,1},{1,5},{2,3},{3,7},{4,0},{5,4},{6,2},{7,6},{8,9},{9,13},{10,1... | collective-permute-start | bytes 786440 | tf_op jit(solution)/shard_map/ppermute | solution.py:34
  11.9 1.5 collective-permute-start.2
  13.4 1.2 collective-permute-start.3
  14.6 0.1 copy.15
  14.8 0.1 broadcast_in_dim.24
  14.9 1.1 concatenate.19
  16.0 2.5 %collective-permute-done.1.refs_1_ = bf16[256,512]{1,0:T(8,128)(2,1)S(1)} collective-permute-done((bf16[256,512]{1,0:T(8,128)(2,1)S(1)}, bf16[256,512]{1,0:T(8,128)(2,1)S(1)}, u32[]{:S(2)}, u32[]{:S(2)}) %collective-permute-start.1) | collective-permute-done | bytes 262176 | tf_op jit(solution)/shard_map/ppermute | solution.py:34
  18.6 7.2 %collective-permute-done.2.refs_2_ = bf16[256,512]{1,0:T(8,128)(2,1)S(1)} collective-permute-done((bf16[256,512]{1,0:T(8,128)(2,1)S(1)}, bf16[256,512]{1,0:T(8,128)(2,1)S(1)}, u32[]{:S(2)}, u32[]{:S(2)}) %collective-permute-start.2) | collective-permute-done | bytes 262176 | tf_op jit(solution)/shard_map/ppermute | solution.py:34
  25.8 0.9 collective-permute-done.3.refs_3_
  26.8 0.5 collective-permute-start.5
  27.3 1.6 collective-permute-start.4
  28.9 3.5 %all-to-all-start = ((bf16[4,256,256]{2,1,0:T(8,128)(2,1)}), bf16[4,256,256]{2,1,0:T(8,128)(2,1)S(1)}, u32[]{:S(2)}, u32[]{:S(2)}) async-start(bf16[4,256,256]{2,1,0:T(8,128)(2,1)} %bitcast.28), calls=%async_computation | async-start | bytes 1048576 | tf_op jit(solution)/shard_map/all_to_all | solution.py:506
  32.4 0.3 copy.17
  32.7 0.2 constant_dynamic-slice_fusion.2
  33.0 0.1 dynamic_slice.22
  33.0 0.1 concatenate.22
  33.1 0.1 dynamic_slice.23
  33.2 0.1 dynamic_slice.26
  33.3 0.1 concatenate.23
  33.4 0.1 broadcast_in_dim_reshape.3.refs_9_
  33.5 0.1 pad.11
  33.6 5.6 %concatenate.20 = bf16[128,2048]{0,1:T(8,128)(2,1)} concatenate(bf16[16,2048]{0,1:T(8,128)(2,1)S(1)} %pad.11, bf16[16,2048]{0,1:T(8,128)(2,1)S(1)} %pad.11, bf16[16,2048]{0,1:T(8,128)(2,1)S(1)} %pad.11, bf16[16,2048]{0,1:T(8,128)(2,1)S(1)} %pad.11, bf16[16,2048]{0,1:T(8,128)(2,1)S(1)} %pad.11, bf16[16,2048]{0,1:T(8,128)(2,1)S(1)} %pad.11, bf16[16,2048]{0,1:T(8,128)(2,1)S(1)} %pad.11, ...), dimensions={0} | concatenate | bytes 1048576 | tf_op jit(solution)/shard_map/concatenate | solution.py:514
  39.3 1.5 pad_maximum_fusion.w_ref
  40.8 2.8 %all-to-all-done = bf16[4,256,256]{2,1,0:T(8,128)(2,1)S(1)} async-done(((bf16[4,256,256]{2,1,0:T(8,128)(2,1)}), bf16[4,256,256]{2,1,0:T(8,128)(2,1)S(1)}, u32[]{:S(2)}, u32[]{:S(2)}) %all-to-all-start) | async-done | bytes 524320 | tf_op jit(solution)/shard_map/all_to_all | solution.py:506
  43.7 9.4 %collective-permute-done.5.refs_2_ = bf16[1024,512]{1,0:T(8,128)(2,1)} collective-permute-done((bf16[1024,512]{1,0:T(8,128)(2,1)S(1)}, bf16[1024,512]{1,0:T(8,128)(2,1)}, u32[]{:S(2)}, u32[]{:S(2)}) %collective-permute-start.5) | collective-permute-done | bytes 1048608 | tf_op jit(solution)/shard_map/ppermute | solution.py:34
  53.1 20.6 %collective-permute-done.4.refs_1_ = bf16[1024,512]{1,0:T(8,128)(2,1)} collective-permute-done((bf16[1024,512]{1,0:T(8,128)(2,1)S(1)}, bf16[1024,512]{1,0:T(8,128)(2,1)}, u32[]{:S(2)}, u32[]{:S(2)}) %collective-permute-start.4) | collective-permute-done | bytes 1048608 | tf_op jit(solution)/shard_map/ppermute | solution.py:34
  73.7 3.5 %collective-permute-start.6 = (bf16[1024,512]{1,0:T(8,128)(2,1)}, bf16[1024,512]{1,0:T(8,128)(2,1)}, u32[]{:S(2)}, u32[]{:S(2)}) collective-permute-start(bf16[1024,512]{1,0:T(8,128)(2,1)} %collective-permute-done.4.refs_1_), channel_id=1, source_target_pairs={{8,16},{9,17},{10,18},{11,19},{12,20},{13,21},{14,22},{15,23},{16,... | collective-permute-start | bytes 3145736 | tf_op jit(solution)/shard_map/ppermute | solution.py:34
  77.2 4.3 %collective-permute-start.7 = (bf16[1024,512]{1,0:T(8,128)(2,1)}, bf16[1024,512]{1,0:T(8,128)(2,1)}, u32[]{:S(2)}, u32[]{:S(2)}) collective-permute-start(bf16[1024,512]{1,0:T(8,128)(2,1)} %collective-permute-done.5.refs_2_), channel_id=1, source_target_pairs={{8,0},{9,1},{10,2},{11,3},{12,4},{13,5},{14,6},{15,7},{16,8},{17,9... | collective-permute-start | bytes 3145736 | tf_op jit(solution)/shard_map/ppermute | solution.py:34
  81.5 0.9 slice.4
  82.4 1.9 collective-permute-start.8
  84.3 2.9 %copy-done.1 = bf16[1536,2176]{1,0:T(8,128)(2,1)S(1)} copy-done((bf16[1536,2176]{1,0:T(8,128)(2,1)S(1)}, bf16[1536,2176]{1,0:T(8,128)(2,1)}, u32[]{:S(2)}) %copy-start.1) | copy-done | bytes 6684696
  87.2 8.6 %maps.1 = (bf16[1536,256]{1,0:T(8,128)(2,1)S(1)}, f32[1536,128]{1,0:T(8,128)S(1)}, f32[32,1536]{1,0:T(8,128)S(1)}) custom-call(bf16[1536,2176]{1,0:T(8,128)(2,1)S(1)} %copy-done.1, bf16[2048,384]{1,0:T(8,128)(2,1)S(1)} %pad_maximum_fusion.w_ref, f32[1,128]{1,0:T(1,128)S(1)} %bitcast.23, f32[1,128]{1,0:T(1,128)S(1)} %bitcast.24), custom_call_target="tpu_custom_call" | custom-call | tf_op jit(solution)/shard_map/maps/pallas_call | solution.py:94
  95.8 0.9 copy-done.4
  96.7 0.9 copy-done.6
  97.6 2.3 %collective-permute-done.6.refs_3_ = bf16[1024,512]{1,0:T(8,128)(2,1)} collective-permute-done((bf16[1024,512]{1,0:T(8,128)(2,1)}, bf16[1024,512]{1,0:T(8,128)(2,1)}, u32[]{:S(2)}, u32[]{:S(2)}) %collective-permute-start.6) | collective-permute-done | bytes 1048608 | tf_op jit(solution)/shard_map/ppermute | solution.py:34
  99.9 1.4 collective-permute-done.7.refs_4_
  101.4 1.1 copy-done.5
  102.5 1.1 copy-done.7
  103.6 15.6 %scan.1 = (f32[1536,256]{1,0:T(8,128)}, bf16[1536,256]{1,0:T(8,128)(2,1)S(1)}, bf16[144,256]{1,0:T(8,128)(2,1)S(1)}) custom-call(s32[1]{0:T(128)} %bitcast.2.pos_ref, bf16[1536,2176]{1,0:T(8,128)(2,1)} %all-gather.4.cloned.1.call-done.x_ref, bf16[16,2176]{1,0:T(8,128)(2,1)S(1)} %collective-permute-done.8.edge_ref, bf16[1024,512]{1,0:T(8,128)(2,1)S(1)} %bitcast.20, ...), custom_call_target="tpu_custom_call" | custom-call | tf_op jit(solution)/shard_map/scan/pallas_call | solution.py:230
  119.2 0.7 collective-permute-start.11
  119.9 1.3 collective-permute-start.10
  121.2 3.4 %collective-permute-start.9 = (bf16[144,256]{1,0:T(8,128)(2,1)S(1)}, bf16[144,256]{1,0:T(8,128)(2,1)S(1)}, u32[]{:S(2)}, u32[]{:S(2)}) collective-permute-start(bf16[144,256]{1,0:T(8,128)(2,1)S(1)} %get-tuple-element.114), channel_id=1, source_target_pairs={{0,8},{1,9},{2,10},{3,11},{4,12},{5,13},{6,14},{7,15},{8,16},{9,17... | collective-permute-start | bytes 221192 | tf_op jit(solution)/shard_map/ppermute | solution.py:34
  124.6 7.6 %collective-permute-done.10.refs_3_ = bf16[144,256]{1,0:T(8,128)(2,1)S(1)} collective-permute-done((bf16[144,256]{1,0:T(8,128)(2,1)S(1)}, bf16[144,256]{1,0:T(8,128)(2,1)S(1)}, u32[]{:S(2)}, u32[]{:S(2)}) %collective-permute-start.10) | collective-permute-done | bytes 73760 | tf_op jit(solution)/shard_map/ppermute | solution.py:34
  132.2 8.2 %collective-permute-done.9.refs_2_ = bf16[144,256]{1,0:T(8,128)(2,1)S(1)} collective-permute-done((bf16[144,256]{1,0:T(8,128)(2,1)S(1)}, bf16[144,256]{1,0:T(8,128)(2,1)S(1)}, u32[]{:S(2)}, u32[]{:S(2)}) %collective-permute-start.9) | collective-permute-done | bytes 73760 | tf_op jit(solution)/shard_map/ppermute | solution.py:34
  140.4 1.5 copy-done.8
  141.9 4.0 %norm.1 = (bf16[768,256]{1,0:T(8,128)(2,1)S(1)}, bf16[768,256]{1,0:T(8,128)(2,1)S(1)}) custom-call(s32[1]{0:T(128)} %bitcast.1.pos_ref, bf16[1536,256]{1,0:T(8,128)(2,1)S(1)} %copy-done.5, f32[1536,128]{1,0:T(8,128)S(1)} %copy-done.7, f32[1,256]{1,0:T(1,128)S(1)} %bitcast.22, f32[1536,256]{1,0:T(8,128)S(1)} %copy-done.8, ...), custom_call_target="tpu_custom_call" | custom-call | tf_op jit(solution)/shard_map/norm/pallas_call | solution.py:317
  145.9 0.2 collective-permute-start.13
  146.1 0.1 pad_add_fusion.pos_ref
  146.2 1.5 collective-permute-done.13.other_ref
  147.6 1.6 project_out.2
  149.3 1.7 collective-permute-start.14
  151.0 3.7 %collective-permute-start.15 = (bf16[192,512]{1,0:T(8,128)(2,1)S(1)}, bf16[192,512]{1,0:T(8,128)(2,1)S(1)}, u32[]{:S(2)}, u32[]{:S(2)}) collective-permute-start(bf16[192,512]{1,0:T(8,128)(2,1)S(1)} %get-tuple-element.124), channel_id=1, source_target_pairs={{0,2},{1,3},{2,0},{3,1},{4,6},{5,7},{6,4},{7,5},{8,10},{9,11},{10,... | collective-permute-start | bytes 589832 | tf_op jit(solution)/shard_map/ppermute | solution.py:34
  154.7 1.6 collective-permute-done.14.refs_1_
  156.3 7.5 %collective-permute-done.15.refs_2_ = bf16[192,512]{1,0:T(8,128)(2,1)S(1)} collective-permute-done((bf16[192,512]{1,0:T(8,128)(2,1)S(1)}, bf16[192,512]{1,0:T(8,128)(2,1)S(1)}, u32[]{:S(2)}, u32[]{:S(2)}) %collective-permute-start.15) | collective-permute-done | bytes 196640 | tf_op jit(solution)/shard_map/ppermute | solution.py:34
  163.8 4.9 %project_out.3 = (bf16[192,1536]{1,0:T(8,128)(2,1)S(1)}, bf16[192,1536]{1,0:T(8,128)(2,1)S(1)}, bf16[192,1536]{1,0:T(8,128)(2,1)S(1)}, bf16[192,1536]{1,0:T(8,128)(2,1)S(1)}) custom-call(s32[3]{0:T(128)S(1)} %pad_add_fusion.pos_ref, bf16[768,128]{1,0:T(8,128)(2,1)S(1)} %constant_dynamic-slice_fusion.ids_ref, ...), custom_call_target="tpu_custom_call" | custom-call | tf_op jit(solution)/shard_map/project_out/pallas_call | solution.py:365
  168.8 1.5 collective-permute-start.17
  170.3 0.6 collective-permute-start.18
  170.9 1.4 collective-permute-start.19
  172.3 12.8 %collective-permute-done.17.refs_5_ = bf16[192,1536]{1,0:T(8,128)(2,1)S(1)} collective-permute-done((bf16[192,1536]{1,0:T(8,128)(2,1)S(1)}, bf16[192,1536]{1,0:T(8,128)(2,1)S(1)}, u32[]{:S(2)}, u32[]{:S(2)}) %collective-permute-start.17) | collective-permute-done | bytes 589856 | tf_op jit(solution)/shard_map/ppermute | solution.py:34
  185.1 12.1 %collective-permute-done.18.refs_6_ = bf16[192,1536]{1,0:T(8,128)(2,1)S(1)} collective-permute-done((bf16[192,1536]{1,0:T(8,128)(2,1)S(1)}, bf16[192,1536]{1,0:T(8,128)(2,1)S(1)}, u32[]{:S(2)}, u32[]{:S(2)}) %collective-permute-start.18) | collective-permute-done | bytes 589856 | tf_op jit(solution)/shard_map/ppermute | solution.py:34
  197.2 1.8 add_up.1
  (51 shorter events, 0.4 us)
Async XLA Ops:
  6.5 32.7 %copy-start = (f32[4,512]{1,0:T(4,128)S(1)}, f32[4,512]{1,0:T(4,128)}, u32[]{:S(2)}) copy-start(f32[4,512]{1,0:T(4,128)} %param.23) | copy-start | bytes 24580
  6.5 8.1 %copy-start.11 = (s32[192,1]{0,1:T(1,128)S(1)}, s32[192,1]{0,1:T(1,128)}, u32[]{:S(2)}) copy-start(s32[192,1]{0,1:T(1,128)} %param.13) | copy-start | bytes 2308
  6.5 8.2 %copy-start.12 = (bf16[192]{0:T(256)(128)(2,1)S(1)}, bf16[192]{0:T(256)(128)(2,1)}, u32[]{:S(2)}) copy-start(bf16[192]{0:T(256)(128)(2,1)} %param.14) | copy-start | bytes 1156
  6.5 8.4 %copy-start.9 = (bf16[192,2048]{1,0:T(8,128)(2,1)S(1)}, bf16[192,2048]{1,0:T(8,128)(2,1)}, u32[]{:S(2)}) copy-start(bf16[192,2048]{1,0:T(8,128)(2,1)} %param.12) | copy-start | bytes 2359300
  6.5 75.0 %all-gather.4.cloned.1.call-start = ((), (), s32[]{:S(2)}) async-start(), calls=%async_computation.1 | async-start | bytes 7520256 | tf_op jit(solution)/shard_map/all_gather | solution.py:501
  8.3 24.1 %copy-start.10 = (bf16[32,2048]{1,0:T(8,128)(2,1)S(1)}, bf16[32,2048]{1,0:T(8,128)(2,1)}, u32[]{:S(2)}) copy-start(bf16[32,2048]{1,0:T(8,128)(2,1)} %param.18) | copy-start | bytes 393220
  8.3 7.7 %collective-permute-start = (bf16[256,512]{1,0:T(8,128)(2,1)S(1)}, bf16[256,512]{1,0:T(8,128)(2,1)S(1)}, u32[]{:S(2)}, u32[]{:S(2)}) collective-permute-start(bf16[256,512]{1,0:T(8,128)(2,1)S(1)} %get-tuple-element.70), channel_id=1, source_target_pairs={{0,0},{1,4},{2,2},{3,6},{4,1},{5,5},{6,3},{7,7},{8,8},{9,12},{10,1... | collective-permute-start | bytes 786440 | tf_op jit(solution)/shard_map/ppermute | solution.py:34
  9.2 9.4 %collective-permute-start.1 = (bf16[256,512]{1,0:T(8,128)(2,1)S(1)}, bf16[256,512]{1,0:T(8,128)(2,1)S(1)}, u32[]{:S(2)}, u32[]{:S(2)}) collective-permute-start(bf16[256,512]{1,0:T(8,128)(2,1)S(1)} %get-tuple-element.71), channel_id=1, source_target_pairs={{0,1},{1,5},{2,3},{3,7},{4,0},{5,4},{6,2},{7,6},{8,9},{9,13},{10,1... | collective-permute-start | bytes 786440 | tf_op jit(solution)/shard_map/ppermute | solution.py:34
  11.9 13.9 %collective-permute-start.2 = (bf16[256,512]{1,0:T(8,128)(2,1)S(1)}, bf16[256,512]{1,0:T(8,128)(2,1)S(1)}, u32[]{:S(2)}, u32[]{:S(2)}) collective-permute-start(bf16[256,512]{1,0:T(8,128)(2,1)S(1)} %get-tuple-element.72), channel_id=1, source_target_pairs={{0,2},{1,6},{2,0},{3,4},{4,3},{5,7},{6,1},{7,5},{8,10},{9,14},{10,... | collective-permute-start | bytes 786440 | tf_op jit(solution)/shard_map/ppermute | solution.py:34
  13.4 13.3 %collective-permute-start.3 = (bf16[256,512]{1,0:T(8,128)(2,1)S(1)}, bf16[256,512]{1,0:T(8,128)(2,1)S(1)}, u32[]{:S(2)}, u32[]{:S(2)}) collective-permute-start(bf16[256,512]{1,0:T(8,128)(2,1)S(1)} %get-tuple-element.73), channel_id=1, source_target_pairs={{0,3},{1,7},{2,1},{3,5},{4,2},{5,6},{6,0},{7,4},{8,11},{9,15},{10,... | collective-permute-start | bytes 786440 | tf_op jit(solution)/shard_map/ppermute | solution.py:34
  16.0 16.9 %copy-start.14 = (f32[8]{0:T(128)S(1)}, f32[8]{0:T(128)}, u32[]{:S(2)}) copy-start(f32[8]{0:T(128)} %param.20) | copy-start | bytes 100
  16.0 17.1 %copy-start.15 = (f32[8]{0:T(128)S(1)}, f32[8]{0:T(128)}, u32[]{:S(2)}) copy-start(f32[8]{0:T(128)} %param.19) | copy-start | bytes 100
  16.0 17.2 %copy-start.16 = (f32[8]{0:T(128)S(1)}, f32[8]{0:T(128)}, u32[]{:S(2)}) copy-start(f32[8]{0:T(128)} %param.21) | copy-start | bytes 100
  26.8 26.3 %collective-permute-start.5 = (bf16[1024,512]{1,0:T(8,128)(2,1)S(1)}, bf16[1024,512]{1,0:T(8,128)(2,1)}, u32[]{:S(2)}, u32[]{:S(2)}) collective-permute-start(bf16[1024,512]{1,0:T(8,128)(2,1)S(1)} %bitcast.18), channel_id=1, source_target_pairs={{0,24},{1,25},{2,26},{3,27},{4,28},{5,29},{6,30},{7,31},{8,0},{9,1... | collective-permute-start | bytes 3145736 | tf_op jit(solution)/shard_map/ppermute | solution.py:34
  27.3 46.4 %collective-permute-start.4 = (bf16[1024,512]{1,0:T(8,128)(2,1)S(1)}, bf16[1024,512]{1,0:T(8,128)(2,1)}, u32[]{:S(2)}, u32[]{:S(2)}) collective-permute-start(bf16[1024,512]{1,0:T(8,128)(2,1)S(1)} %bitcast.19), channel_id=1, source_target_pairs={{0,8},{1,9},{2,10},{3,11},{4,12},{5,13},{6,14},{7,15},{8,16},{9,17... | collective-permute-start | bytes 3145736 | tf_op jit(solution)/shard_map/ppermute | solution.py:34
  28.9 14.8 %all-to-all-start = ((bf16[4,256,256]{2,1,0:T(8,128)(2,1)}), bf16[4,256,256]{2,1,0:T(8,128)(2,1)S(1)}, u32[]{:S(2)}, u32[]{:S(2)}) async-start(bf16[4,256,256]{2,1,0:T(8,128)(2,1)} %bitcast.28), calls=%async_computation | async-start | bytes 1048576 | tf_op jit(solution)/shard_map/all_to_all | solution.py:506
  32.4 131.5 %all-gather.6.cloned.1.call-start = ((), (), s32[]{:S(2)}) async-start(), calls=%async_computation.2 | async-start | bytes 4718592 | tf_op jit(solution)/shard_map/all_gather | solution.py:530
  32.9 6.3 %copy-start.13 = (f32[512]{0:T(512)S(1)}, f32[512]{0:T(512)}, u32[]{:S(2)}) copy-start(f32[512]{0:T(512)} %param.22) | copy-start | bytes 6148
  43.7 52.1 %copy-start.2 = (bf16[4,256,256]{2,1,0:T(8,128)(2,1)}, bf16[4,256,256]{2,1,0:T(8,128)(2,1)S(1)}, u32[]{:S(2)}) copy-start(bf16[4,256,256]{2,1,0:T(8,128)(2,1)S(1)} %all-to-all-done) | copy-start | bytes 1572868
  73.7 26.2 %collective-permute-start.6 = (bf16[1024,512]{1,0:T(8,128)(2,1)}, bf16[1024,512]{1,0:T(8,128)(2,1)}, u32[]{:S(2)}, u32[]{:S(2)}) collective-permute-start(bf16[1024,512]{1,0:T(8,128)(2,1)} %collective-permute-done.4.refs_1_), channel_id=1, source_target_pairs={{8,16},{9,17},{10,18},{11,19},{12,20},{13,21},{14,22},{15,23},{16,... | collective-permute-start | bytes 3145736 | tf_op jit(solution)/shard_map/ppermute | solution.py:34
  77.2 24.1 %collective-permute-start.7 = (bf16[1024,512]{1,0:T(8,128)(2,1)}, bf16[1024,512]{1,0:T(8,128)(2,1)}, u32[]{:S(2)}, u32[]{:S(2)}) collective-permute-start(bf16[1024,512]{1,0:T(8,128)(2,1)} %collective-permute-done.5.refs_2_), channel_id=1, source_target_pairs={{8,0},{9,1},{10,2},{11,3},{12,4},{13,5},{14,6},{15,7},{16,8},{17,9... | collective-permute-start | bytes 3145736 | tf_op jit(solution)/shard_map/ppermute | solution.py:34
  82.4 18.9 %collective-permute-start.8 = (bf16[16,2176]{1,0:T(8,128)(2,1)S(1)}, bf16[16,2176]{1,0:T(8,128)(2,1)S(1)}, u32[]{:S(2)}, u32[]{:S(2)}) collective-permute-start(bf16[16,2176]{1,0:T(8,128)(2,1)S(1)} %slice.4), channel_id=1, source_target_pairs={{0,8},{1,9},{2,10},{3,11},{4,12},{5,13},{6,14},{7,15},{8,16},{9,17... | collective-permute-start | bytes 208904 | tf_op jit(solution)/shard_map/ppermute | solution.py:34
  84.3 2.9 %copy-start.1 = (bf16[1536,2176]{1,0:T(8,128)(2,1)S(1)}, bf16[1536,2176]{1,0:T(8,128)(2,1)}, u32[]{:S(2)}) copy-start(bf16[1536,2176]{1,0:T(8,128)(2,1)} %all-gather.4.cloned.1.call-done.x_ref) | copy-start | bytes 20054020
  95.8 0.9 copy-start.4
  96.7 0.9 copy-start.6
  101.4 1.1 copy-start.5
  102.5 1.1 copy-start.7
  103.6 15.6 %copy-start.3 = (bf16[4,256,256]{2,1,0:T(8,128)(2,1)S(1)}, bf16[4,256,256]{2,1,0:T(8,128)(2,1)}, u32[]{:S(2)}) copy-start(bf16[4,256,256]{2,1,0:T(8,128)(2,1)} %copy-done.2) | copy-start | bytes 1572868
  119.2 26.6 %collective-permute-start.12 = (bf16[1024,256]{1,0:T(8,128)(2,1)S(1)}, bf16[1024,256]{1,0:T(8,128)(2,1)S(1)}, u32[]{:S(2)}, u32[]{:S(2)}) collective-permute-start(bf16[1024,256]{1,0:T(8,128)(2,1)S(1)} %bitcast.16), channel_id=1, source_target_pairs={{0,4},{1,5},{2,6},{3,7},{4,0},{5,1},{6,2},{7,3},{8,12},{9,13},{10,... | collective-permute-start | bytes 1572872 | tf_op jit(solution)/shard_map/ppermute | solution.py:34
  119.2 5.4 %collective-permute-start.11 = (bf16[144,256]{1,0:T(8,128)(2,1)S(1)}, bf16[144,256]{1,0:T(8,128)(2,1)S(1)}, u32[]{:S(2)}, u32[]{:S(2)}) collective-permute-start(bf16[144,256]{1,0:T(8,128)(2,1)S(1)} %get-tuple-element.114), channel_id=1, source_target_pairs={{0,24},{1,25},{2,26},{3,27},{4,28},{5,29},{6,30},{7,31}} | collective-permute-start | bytes 221192 | tf_op jit(solution)/shard_map/ppermute | solution.py:34
  119.9 12.3 %collective-permute-start.10 = (bf16[144,256]{1,0:T(8,128)(2,1)S(1)}, bf16[144,256]{1,0:T(8,128)(2,1)S(1)}, u32[]{:S(2)}, u32[]{:S(2)}) collective-permute-start(bf16[144,256]{1,0:T(8,128)(2,1)S(1)} %get-tuple-element.114), channel_id=1, source_target_pairs={{0,16},{1,17},{2,18},{3,19},{4,20},{5,21},{6,22},{7,23},{8,24},{9,... | collective-permute-start | bytes 221192 | tf_op jit(solution)/shard_map/ppermute | solution.py:34
  121.2 19.2 %collective-permute-start.9 = (bf16[144,256]{1,0:T(8,128)(2,1)S(1)}, bf16[144,256]{1,0:T(8,128)(2,1)S(1)}, u32[]{:S(2)}, u32[]{:S(2)}) collective-permute-start(bf16[144,256]{1,0:T(8,128)(2,1)S(1)} %get-tuple-element.114), channel_id=1, source_target_pairs={{0,8},{1,9},{2,10},{3,11},{4,12},{5,13},{6,14},{7,15},{8,16},{9,17... | collective-permute-start | bytes 221192 | tf_op jit(solution)/shard_map/ppermute | solution.py:34
  140.4 1.5 copy-start.8
  145.9 1.8 collective-permute-start.13
  149.3 7.0 %collective-permute-start.14 = (bf16[192,512]{1,0:T(8,128)(2,1)S(1)}, bf16[192,512]{1,0:T(8,128)(2,1)S(1)}, u32[]{:S(2)}, u32[]{:S(2)}) collective-permute-start(bf16[192,512]{1,0:T(8,128)(2,1)S(1)} %get-tuple-element.123), channel_id=1, source_target_pairs={{0,1},{1,0},{2,3},{3,2},{4,5},{5,4},{6,7},{7,6},{8,9},{9,8},{10,11... | collective-permute-start | bytes 589832 | tf_op jit(solution)/shard_map/ppermute | solution.py:34
  151.0 12.9 %collective-permute-start.15 = (bf16[192,512]{1,0:T(8,128)(2,1)S(1)}, bf16[192,512]{1,0:T(8,128)(2,1)S(1)}, u32[]{:S(2)}, u32[]{:S(2)}) collective-permute-start(bf16[192,512]{1,0:T(8,128)(2,1)S(1)} %get-tuple-element.124), channel_id=1, source_target_pairs={{0,2},{1,3},{2,0},{3,1},{4,6},{5,7},{6,4},{7,5},{8,10},{9,11},{10,... | collective-permute-start | bytes 589832 | tf_op jit(solution)/shard_map/ppermute | solution.py:34
  154.7 9.1 %collective-permute-start.16 = (bf16[192,512]{1,0:T(8,128)(2,1)S(1)}, bf16[192,512]{1,0:T(8,128)(2,1)S(1)}, u32[]{:S(2)}, u32[]{:S(2)}) collective-permute-start(bf16[192,512]{1,0:T(8,128)(2,1)S(1)} %get-tuple-element.125), channel_id=1, source_target_pairs={{0,3},{1,2},{2,1},{3,0},{4,7},{5,6},{6,5},{7,4},{8,11},{9,10},{10,... | collective-permute-start | bytes 589832 | tf_op jit(solution)/shard_map/ppermute | solution.py:34
  168.8 16.3 %collective-permute-start.17 = (bf16[192,1536]{1,0:T(8,128)(2,1)S(1)}, bf16[192,1536]{1,0:T(8,128)(2,1)S(1)}, u32[]{:S(2)}, u32[]{:S(2)}) collective-permute-start(bf16[192,1536]{1,0:T(8,128)(2,1)S(1)} %get-tuple-element.132), channel_id=1, source_target_pairs={{0,1},{1,0},{2,3},{3,2},{4,5},{5,4},{6,7},{7,6},{8,9},{9,8},{10,11... | collective-permute-start | bytes 1769480 | tf_op jit(solution)/shard_map/ppermute | solution.py:34
  170.3 26.9 %collective-permute-start.18 = (bf16[192,1536]{1,0:T(8,128)(2,1)S(1)}, bf16[192,1536]{1,0:T(8,128)(2,1)S(1)}, u32[]{:S(2)}, u32[]{:S(2)}) collective-permute-start(bf16[192,1536]{1,0:T(8,128)(2,1)S(1)} %get-tuple-element.133), channel_id=1, source_target_pairs={{0,2},{1,3},{2,0},{3,1},{4,6},{5,7},{6,4},{7,5},{8,10},{9,11},{10,... | collective-permute-start | bytes 1769480 | tf_op jit(solution)/shard_map/ppermute | solution.py:34
  170.9 26.3 %collective-permute-start.19 = (bf16[192,1536]{1,0:T(8,128)(2,1)S(1)}, bf16[192,1536]{1,0:T(8,128)(2,1)S(1)}, u32[]{:S(2)}, u32[]{:S(2)}) collective-permute-start(bf16[192,1536]{1,0:T(8,128)(2,1)S(1)} %get-tuple-element.134), channel_id=1, source_target_pairs={{0,3},{1,2},{2,1},{3,0},{4,7},{5,6},{6,5},{7,4},{8,11},{9,10},{10,... | collective-permute-start | bytes 1769480 | tf_op jit(solution)/shard_map/ppermute | solution.py:34
Sparse Core Ops, SparseCore 0:
  26.9 51.0 all-gather.3
  101.5 51.5 all-gather.5

commit v2 on v1

--- a/solution.py
+++ b/solution.py
@@ -334,17 +334,10 @@
     )(core, maps_all, cols, gain, *ys, *gates, *finals)
 
 
-def out_kernel(experts, groups, planes, depth, pos_ref, ids_ref, mine_ref, other_ref, *refs):
+def out_kernel(experts, groups, pos_ref, ids_ref, mine_ref, other_ref, *refs):
     weights, outs = refs[:-groups], refs[-groups:]
     group, width = pos_ref[0], mine_ref.shape[0] // groups
-    chunk = weights[0].shape[-1]
-    pairs = []
-    for s in planes:
-        if s == 0 and len(weights) > 1:
-            pairs.append([weights[0][...], weights[1][...]])
-            continue
-        z = lax.rem(pos_ref[2] - s + depth, depth)
-        pairs.append([weights[0][2 * z + pos_ref[1]], weights[0][2 * z + 1 - pos_ref[1]]])
+    chunk = weights[0].shape[1]
     for s in range(groups):
         rows = pl.ds(pl.multiple_of(jnp.bitwise_xor(group, s) * width, 64), width)
         chosen = ids_ref[rows, :].astype(f32)[:, 0:1]
@@ -353,17 +346,17 @@
         both_halves = jnp.concatenate([jnp.where(second, other, mine), jnp.where(second, mine, other)], axis=1)
         zero = jnp.zeros_like(both_halves)
         masked = jnp.concatenate([jnp.where(chosen == e, both_halves, zero) for e in range(experts)], axis=1)
-        for at, weight in enumerate(weight for pair in pairs for weight in pair):
-            total = jnp.dot(masked, weight, preferred_element_type=f32)
+        for at, weight in enumerate(weights):
+            total = jnp.dot(masked, weight[...], preferred_element_type=f32)
             outs[s][:, at * chunk : (at + 1) * chunk] = total.astype(bf16)
 
 
-def project_out(position, ids, mine, other, weights, planes, depth, groups):
+def project_out(position, ids, mine, other, weights, groups):
     rows = mine.shape[0] // groups
     whole = pl.BlockSpec(memory_space=pltpu.VMEM)
-    shape = jax.ShapeDtypeStruct((rows, 2 * len(planes) * weights[0].shape[-1]), bf16)
-    return pl.pallas_call(
-        functools.partial(out_kernel, groups // 2, groups, planes, depth),
+    shape = jax.ShapeDtypeStruct((rows, len(weights) * weights[0].shape[1]), bf16)
+    return pl.pallas_call(
+        functools.partial(out_kernel, groups // 2, groups),
         in_specs=[pl.BlockSpec(memory_space=pltpu.SMEM)] + [whole] * (3 + len(weights)),
         out_specs=[whole] * groups,
         out_shape=[shape] * groups,
@@ -372,17 +365,17 @@
     )(position, ids, mine, other, *weights)
 
 
-def sum_kernel(depth, groups, planes, pos_ref, *refs):
+def sum_kernel(depth, groups, distances, pos_ref, *refs):
     out_ref = refs[-1]
     chunk = out_ref.shape[1] // (2 * depth)
-    for at, several in enumerate(planes):
+    for at, several in enumerate(distances):
         blocks = refs[at * groups : (at + 1) * groups]
         total = blocks[0][...].astype(f32)
         for block in blocks[1:]:
             total = total + block[...].astype(f32)
         total = total.astype(bf16)
-        for place, s in enumerate(several):
-            z = lax.rem(pos_ref[2] - s + depth, depth)
+        for place, distance in enumerate(several):
+            z = lax.rem(pos_ref[0] - distance + depth, depth)
             for j in range(2):
                 core = pos_ref[1] if j == 0 else 1 - pos_ref[1]
                 to = pl.multiple_of((2 * z + core) * chunk, 128)
@@ -390,12 +383,12 @@
                 out_ref[:, pl.ds(to, chunk)] = total[:, span]
 
 
-def add_up(position, blocks, planes, depth, width):
+def add_up(position, blocks, distances, depth, width):
     groups, rows = len(blocks[0]), blocks[0][0].shape[0]
     flat = [block for several in blocks for block in several]
     whole = pl.BlockSpec(memory_space=pltpu.VMEM)
     return pl.pallas_call(
-        functools.partial(sum_kernel, depth, groups, planes),
+        functools.partial(sum_kernel, depth, groups, distances),
         in_specs=[pl.BlockSpec(memory_space=pltpu.SMEM)] + [whole] * len(flat),
         out_specs=whole,
         out_shape=jax.ShapeDtypeStruct((rows, width), bf16),
@@ -438,6 +431,28 @@
     )(group, *blocks)
 
 
+def cut_rows_kernel(sources, pos_ref, *refs):
+    for r, out in enumerate(refs[sources:]):
+        piece = out.shape[0] // sources
+        rows = pl.ds(pl.multiple_of(jnp.bitwise_xor(pos_ref[0], r) * piece, 64), piece)
+        for at, ref in enumerate(refs[:sources]):
+            out[at * piece : (at + 1) * piece, :] = ref[rows, :]
+
+
+def cut_rows(group, arrays, groups):
+    whole = pl.BlockSpec(memory_space=pltpu.VMEM)
+    rows, width = arrays[0].shape
+    shape = (len(arrays) * rows // groups, width)
+    return pl.pallas_call(
+        functools.partial(cut_rows_kernel, len(arrays)),
+        in_specs=[pl.BlockSpec(memory_space=pltpu.SMEM)] + [whole] * len(arrays),
+        out_specs=[whole] * groups,
+        out_shape=[jax.ShapeDtypeStruct(shape, arrays[0].dtype)] * groups,
+        compiler_params=params(32),
+        name="cut_rows",
+    )(group, *arrays)
+
+
 def cut_kernel(pos_ref, flat_ref, *outs):
     piece = outs[0].shape[1] // 2
     half = flat_ref.shape[1] // 2
@@ -465,6 +480,33 @@
         compiler_params=params(32),
         name="cut",
     )(index, flat)
+
+
+def lay_kernel(pos_ref, *refs):
+    blocks, whole, sems = refs[:-2], refs[-2], refs[-1]
+    rows = blocks[0].shape[0]
+    copies = []
+    for at, block in enumerate(blocks):
+        row = pl.multiple_of(jnp.bitwise_xor(pos_ref[0], at) * rows, 64)
+        copies.append(pltpu.make_async_copy(block, whole.at[pl.ds(row, rows), :], sems.at[at]))
+    for copy in copies:
+        copy.start()
+    for copy in copies:
+        copy.wait()
+
+
+def lay(position, blocks):
+    rows, width = blocks[0].shape
+    place = pl.BlockSpec(memory_space=pl.ANY)
+    return pl.pallas_call(
+        lay_kernel,
+        in_specs=[pl.BlockSpec(memory_space=pltpu.SMEM)] + [place] * len(blocks),
+        out_specs=place,
+        out_shape=jax.ShapeDtypeStruct((len(blocks) * rows, width), blocks[0].dtype),
+        scratch_shapes=[pltpu.SemaphoreType.DMA((len(blocks),))],
+        compiler_params=params(16),
+        name="lay",
+    )(position, *blocks)
 
 
 def on_device(
@@ -486,26 +528,24 @@
     swap = lambda array: shift(array, lambda z, k, e: (z, 1 - k, e))
     phase = lax.optimization_barrier
 
-    added = jnp.concatenate(
-        [expert_ids.astype(bf16), damping[:, None], jnp.zeros((rows, extra - 2), bf16)], axis=1
-    )
-    wide = jnp.concatenate([tokens, added], axis=1)
-    planes = [[2 * i * groups + j for j in range(2 * groups)] for i in range(depth)]
     flat = in_weight[0].reshape(depth_weight, 2 * half)
     index = scalar(2 * (group // 2) + core)
     got = spread_pieces(cut(index, flat, groups))
-    got, wide, out_weight, w_bc, w_dt, rate, dt_bias, d_skip, gain, conv_weight = phase(
-        (got, wide, out_weight, w_bc, w_dt, rate, dt_bias, d_skip, gain, conv_weight)
-    )
-
-    plane = lax.all_gather(wide, both, axis=0, tiled=True, axis_index_groups=planes)
+    out_raw = [out_weight[0], shift(out_weight[0], lambda z, k, e: ((z - 1) % depth, k, e))]
+    added = jnp.concatenate(
+        [expert_ids.astype(bf16), damping[:, None], jnp.zeros((rows, extra - 2), bf16)], axis=1
+    )
+    wide = jnp.concatenate([tokens, added], axis=1)
+    got, wide, out_raw, w_bc, w_dt, rate, dt_bias, d_skip, gain, conv_weight = phase(
+        (got, wide, out_raw, w_bc, w_dt, rate, dt_bias, d_skip, gain, conv_weight)
+    )
+
     (shard,) = arrange(got, group_at, 1, False)
     shard = shard.reshape(groups * depth_weight, 2 * piece)
     near = line_near(shard, depth)
-    columns = out_weight.shape[2]
-    out_shard = lax.all_to_all(
-        out_weight[0].reshape(groups, piece, columns), "exp", 0, 0, tiled=True
-    ).reshape(half, columns)
+    wide, out_raw = phase((wide, out_raw, shard))[:2]
+    exchange = lambda array, r: shift(array, lambda z, k, e: (z, k, e ^ r))
+    own = [wide] + [exchange(wide, r) for r in range(1, groups)]
     local = lambda vector: lax.dynamic_slice_in_dim(vector, core * heads, heads, 0)
     lanes = lambda vector: jnp.concatenate(
         [jnp.pad(local(vector), (0, dt_lane - heads))] * (128 // dt_lane)
@@ -517,45 +557,62 @@
     half_taps = lax.dynamic_slice_in_dim(conv_weight, core * piece, piece, 1)
     half_gain = lax.dynamic_slice_in_dim(gain, core * piece, piece, 0)[None, :]
     half_skip = jnp.repeat(local(d_skip), head)[None, :]
-    shard, near, out_shard, w_maps, bias_lanes, rate_lanes, half_taps, half_gain, half_skip = phase(
-        (shard, near, out_shard, w_maps, bias_lanes, rate_lanes, half_taps, half_gain, half_skip)
+    out_sent = cut_rows(group_at, out_raw, groups)
+    out_got = [out_sent[0]]
+    for r in range(1, groups):
+        own[r], block = phase((own[r], out_sent[r]))
+        out_got.append(exchange(block, r))
+    columns = out_weight.shape[2]
+    part = lay(group_at, own)
+    out_shard, above = [array.reshape(half, columns) for array in arrange(out_got, group_at, 2, True)]
+    shard, near, part, out_shard, above, w_maps, bias_lanes, rate_lanes, half_taps, half_gain, half_skip = phase(
+        (shard, near, part, out_shard, above, w_maps, bias_lanes, rate_lanes, half_taps, half_gain, half_skip)
     )
 
     far = line_far(near, depth)
+    other_part = swap(part)
+    plane = lay(core_at, [part, other_part])
     edge = shift(plane[count - halo :], lambda z, k, e: (z + 1, k, e) if z + 1 < depth else None)
     found = maps(plane, w_maps, bias_lanes, rate_lanes, heads, w_bc.shape[1], length)
     ids = lax.dynamic_slice(plane, (core * groups * rows, width), (groups * rows, extra))
-    far, plane, edge, found, out_shard, ids = phase((far, plane, edge, found, out_shard, ids))
-
-    whole_out = lax.all_gather(out_shard, "ctx", axis=0)
+    out_shard, above, _ = phase((out_shard, above, other_part))
+    out_shard_other, above_other = swap(out_shard), swap(above)
+    far, plane, edge, found, ids, out_shard, above, out_shard_other, above_other = phase(
+        (far, plane, edge, found, ids, out_shard, above, out_shard_other, above_other)
+    )
+
     y, gate, final = scan(
         z_at, plane, edge, [shard, *near], far, found, half_taps, half_skip,
         [], 0, head, experts, depth, width, length,
     )
-    y, gate, final, out_shard = phase((y, gate, final, out_shard))
+    below = shift(out_shard, lambda z, k, e: ((z + 1) % depth, k, e))
+    y, gate, final, below = phase((y, gate, final, below))
 
     finals = [
         shift(final, lambda z, k, e: (z + s, k, e) if z + s < depth else None) for s in range(1, depth)
     ]
+    ups, downs = [below], [above]
+    for s in range(2, depth - 1):
+        ups.append(step_up(ups[-1], s, depth))
+        downs.append(step_down(downs[-1], s, depth))
     theirs, mine = norm(core_at, found, half_gain, [y], [gate], finals, head, length)
-    out_other = swap(out_shard)
-    theirs, out_other = phase((theirs, out_other))
+    theirs, mine, below = phase((theirs, mine, below))
     other = swap(theirs)
+    below_other = swap(below)
     other, mine = phase((other, mine))
 
-    position = jnp.concatenate([group_at, core_at, z_at])
-
-    def send(weights, planes):
-        results = project_out(position, ids, mine, other, weights, planes, depth, groups)
-        return [results[0]] + [
-            shift(results[r], lambda z, k, e: (z, k, e ^ r)) for r in range(1, groups)
-        ]
-
-    order = [(0,), tuple(range(1, depth))]
-    blocks = [send([out_shard, out_other], order[0])]
-    whole_out, blocks = phase((whole_out, blocks))
-    blocks.append(send([whole_out], order[1]))
-    return add_up(position, blocks, order, depth, width)
+    position = jnp.concatenate([group_at, core_at])
+
+    def send(*weights):
+        results = project_out(position, ids, mine, other, weights, groups)
+        return [results[0]] + [exchange(results[r], r) for r in range(1, groups)]
+
+    blocks = [send(out_shard, out_shard_other, above, above_other)]
+    ups, downs, below_other, blocks[0][0] = phase((ups, downs, below_other, blocks[0][0]))
+    late = [jnp.where(z >= s + 2, up, down) for s, (up, down) in enumerate(paired(ups[1:], downs[1:]))]
+    blocks.append(send(below, below_other, *[array for part in late for array in (part, swap(part))]))
+    distances = [(0, depth - 1), (1, *range(2, depth - 1))]
+    return add_up(jnp.concatenate([z_at, core_at]), blocks, distances, depth, width)
 
 
 def solution(mesh):

time: 206 us -> 190 us (0.922)
  waiting for transfers between devices: 98.6 us -> 72.2 us
  between operations: 13.7 us -> 0.39 us
  starting transfers between devices: 36.2 us -> 47.4 us
  local copies, waits for them, and re-layouts: 19 us -> 23.6 us
  Pallas kernels: 36.6 us -> 40.6 us
  other arithmetic: 1.63 us -> 4.08 us
    ppermute x20 -> x34, waiting for transfers between devices: 95.7 us -> 72.2 us  [shift(): return lax.ppermute(array, both, pairs)]
    ppermute x20 -> x34, starting transfers between devices: 32.6 us -> 47.4 us  [shift(): return lax.ppermute(array, both, pairs)]
    all_to_all x1 -> x0, starting transfers between devices: 3.47 us -> none  [on_device(): lax.all_to_all(out_weight[0].reshape(groups, piece, columns), 'exp', 0, 0...]
    all_to_all x1 -> x0, waiting for transfers between devices: 2.84 us -> none  [on_device(): lax.all_to_all(out_weight[0].reshape(groups, piece, columns), 'exp', 0, 0...]
    pallas_call x1 -> x2, Pallas kernels: 0.07 us -> 2.15 us  [arrange(): pl.pallas_call(functools.partial(arrange_kernel, len(blocks), by_rows), i...]
    unnamed x35 -> x49, local copies, waits for them, and re-layouts: 9.99 us -> 11.5 us
    pallas_call x3 -> x6, Pallas kernels: 8.32 us -> 9.21 us  [the longest x2 5.85 us: project_out(): pl.pallas_call(functools.partial(out_kernel, groups // 2, groups), in_spe...]
  transfers between devices with their start and end apart: 23 -> 34, of which waited for: 15 -> 15; matrix products, arithmetic and copies ran while one was open for 5% -> 9% of each run, Pallas kernels for 14% -> 20%
where the time goes in v2:
time: 190 us; the launch traced here: 188 us
  waiting for transfers between devices  72.2 us (38%)
  starting transfers between devices  47.4 us (25%)
  Pallas kernels  40.6 us (21%)
  local copies, waits for them, and re-layouts  23.6 us (12%)
  other arithmetic  4.08 us (2%)
    ppermute x34, waiting for transfers between devices, shift(): return lax.ppermute(array, both, pairs)  72.2 us
    ppermute x34, starting transfers between devices, shift(): return lax.ppermute(array, both, pairs)  47.4 us
    pallas_call x1, Pallas kernels, scan(): pl.pallas_call(functools.partial(scan_kernel, first_head, head, experts,...  15.8 us
    unnamed x49, local copies, waits for them, and re-layouts  11.5 us
    pallas_call x1, Pallas kernels, maps(): pl.pallas_call(functools.partial(maps_kernel, heads, width), grid=(count...  8.67 us
    concatenate x1, local copies, waits for them, and re-layouts, on_device(): jnp.concatenate([jnp.pad(picked, ((0, dt_lane - heads), (0, 0)))] * (128...  6.78 us
    pallas_call x2, Pallas kernels, project_out(): pl.pallas_call(functools.partial(out_kernel, groups // 2, groups), in_spe...  5.85 us
    pallas_call x1, Pallas kernels, norm(): pl.pallas_call(functools.partial(norm_kernel, chunks, before, head, chann...  3.94 us
  transfers between devices with their start and end apart: 34, of which 15 were waited for; matrix products, arithmetic and copies ran while one was open for 9% of the time, Pallas kernels for 20%

profile of v2, /device:TPU:16, one launch (start us, length us, event | category | flops | bytes accessed | tf_op | source)
XLA Modules:
  0.0 188.3 jit_solution(15409883138482493930)
XLA Ops:
  0.5 1.5 copy.18
  2.1 0.9 cut.1
  2.9 1.6 collective-permute-start
  4.5 1.8 collective-permute-start.1
  6.3 1.5 collective-permute-start.2
  7.9 1.2 collective-permute-start.3
  9.3 1.2 concatenate.22.refs_0_
  10.6 2.3 %collective-permute-done.1.refs_1_ = bf16[256,512]{1,0:T(8,128)(2,1)S(1)} collective-permute-done((bf16[256,512]{1,0:T(8,128)(2,1)S(1)}, bf16[256,512]{1,0:T(8,128)(2,1)S(1)}, u32[]{:S(2)}, u32[]{:S(2)}) %collective-permute-start.1) | collective-permute-done | bytes 262176 | tf_op jit(solution)/shard_map/ppermute | solution.py:34
  12.9 7.2 %collective-permute-done.2.refs_2_ = bf16[256,512]{1,0:T(8,128)(2,1)S(1)} collective-permute-done((bf16[256,512]{1,0:T(8,128)(2,1)S(1)}, bf16[256,512]{1,0:T(8,128)(2,1)S(1)}, u32[]{:S(2)}, u32[]{:S(2)}) %collective-permute-start.2) | collective-permute-done | bytes 262176 | tf_op jit(solution)/shard_map/ppermute | solution.py:34
  20.1 1.0 collective-permute-done.3.refs_3_
  21.1 1.1 arrange.2
  22.9 1.5 collective-permute-start.8
  24.4 1.4 collective-permute-start.7
  25.8 1.6 collective-permute-start.5
  27.8 1.0 copy.17
  28.8 1.2 constant_dynamic-slice_fusion.2
  30.1 0.9 pad.11
  31.0 6.8 %concatenate.23 = bf16[128,2048]{0,1:T(8,128)(2,1)} concatenate(bf16[16,2048]{0,1:T(8,128)(2,1)} %pad.11, bf16[16,2048]{0,1:T(8,128)(2,1)} %pad.11, bf16[16,2048]{0,1:T(8,128)(2,1)} %pad.11, bf16[16,2048]{0,1:T(8,128)(2,1)} %pad.11, bf16[16,2048]{0,1:T(8,128)(2,1)} %pad.11, bf16[16,2048]{0,1:T(8,128)(2,1)} %pad.11, bf16[16,2048]{0,1:T(8,128)(2,1)} %pad.11, bf16[16,2048]{0,1:T(8,128)(2,1)} %pad.11), dimensions={0} | concatenate | bytes 1048576 | tf_op jit(solution)/shard_map/concatenate | solution.py:554
  38.4 1.0 copy-done.14
  39.4 1.0 copy-done.16
  40.6 4.1 %collective-permute-done.9.refs_3_ = bf16[192,2176]{1,0:T(8,128)(2,1)S(1)} collective-permute-done((bf16[192,2176]{1,0:T(8,128)(2,1)S(1)}, bf16[192,2176]{1,0:T(8,128)(2,1)S(1)}, u32[]{:S(2)}, u32[]{:S(2)}) %collective-permute-start.9) | collective-permute-done | bytes 835616 | tf_op jit(solution)/shard_map/ppermute | solution.py:34
  44.8 0.9 copy-done.8
  46.2 16.4 %collective-permute-done.8.refs_2_ = bf16[192,2176]{1,0:T(8,128)(2,1)S(1)} collective-permute-done((bf16[192,2176]{1,0:T(8,128)(2,1)S(1)}, bf16[192,2176]{1,0:T(8,128)(2,1)S(1)}, u32[]{:S(2)}, u32[]{:S(2)}) %collective-permute-start.8) | collective-permute-done | bytes 835616 | tf_op jit(solution)/shard_map/ppermute | solution.py:34
  62.6 0.9 copy-done.10
  63.5 1.5 collective-permute-start.11
  65.0 0.9 copy-done.12
  65.9 2.8 %pad_maximum_fusion.w_ref = bf16[2048,384]{1,0:T(8,128)(2,1)} fusion(bf16[2048,128]{1,0:T(8,128)(2,1)} %bitcast.21, bf16[2048,256]{1,0:T(8,128)(2,1)} %param.17), kind=kLoop, calls=%fused_computation | loop fusion | flops 3145728 | bytes 3145728 | tf_op jit(solution)/shard_map/concatenate | solution.py:555
  69.2 2.7 %collective-permute-done.11.refs_2_ = bf16[512,256]{1,0:T(8,128)(2,1)S(1)} collective-permute-done((bf16[512,256]{1,0:T(8,128)(2,1)S(1)}, bf16[512,256]{1,0:T(8,128)(2,1)S(1)}, u32[]{:S(2)}, u32[]{:S(2)}) %collective-permute-start.11) | collective-permute-done | bytes 262176 | tf_op jit(solution)/shard_map/ppermute | solution.py:34
  71.9 1.9 %collective-permute-done.10.refs_1_ = bf16[512,256]{1,0:T(8,128)(2,1)S(1)} collective-permute-done((bf16[512,256]{1,0:T(8,128)(2,1)S(1)}, bf16[512,256]{1,0:T(8,128)(2,1)S(1)}, u32[]{:S(2)}, u32[]{:S(2)}) %collective-permute-start.10) | collective-permute-done | bytes 262176 | tf_op jit(solution)/shard_map/ppermute | solution.py:34
  73.8 1.1 arrange.3
  74.9 3.5 %collective-permute-start.13 = (bf16[1024,512]{1,0:T(8,128)(2,1)}, bf16[1024,512]{1,0:T(8,128)(2,1)}, u32[]{:S(2)}, u32[]{:S(2)}) collective-permute-start(bf16[1024,512]{1,0:T(8,128)(2,1)} %collective-permute-done.5.refs_1_), channel_id=1, source_target_pairs={{8,16},{9,17},{10,18},{11,19},{12,20},{13,21},{14,22},{15,23},{16,... | collective-permute-start | bytes 3145736 | tf_op jit(solution)/shard_map/ppermute | solution.py:34
  78.4 4.4 %collective-permute-start.14 = (bf16[1024,512]{1,0:T(8,128)(2,1)}, bf16[1024,512]{1,0:T(8,128)(2,1)}, u32[]{:S(2)}, u32[]{:S(2)}) collective-permute-start(bf16[1024,512]{1,0:T(8,128)(2,1)} %collective-permute-done.6.refs_2_), channel_id=1, source_target_pairs={{8,0},{9,1},{10,2},{11,3},{12,4},{13,5},{14,6},{15,7},{16,8},{17,9... | collective-permute-start | bytes 3145736 | tf_op jit(solution)/shard_map/ppermute | solution.py:34
  82.7 1.7 copy-done.5
  84.9 1.9 %copy-done.6 = bf16[768,2176]{1,0:T(8,128)(2,1)S(1)} copy-done((bf16[768,2176]{1,0:T(8,128)(2,1)S(1)}, bf16[768,2176]{1,0:T(8,128)(2,1)}, u32[]{:S(2)}) %copy-start.6) | copy-done | bytes 3342360
  86.9 1.0 lay.3.x_ref
  87.9 1.9 %collective-permute-start.16 = (bf16[16,2176]{1,0:T(8,128)(2,1)S(1)}, bf16[16,2176]{1,0:T(8,128)(2,1)S(1)}, u32[]{:S(2)}, u32[]{:S(2)}) collective-permute-start(bf16[16,2176]{1,0:T(8,128)(2,1)S(1)} %slice.4), channel_id=1, source_target_pairs={{0,8},{1,9},{2,10},{3,11},{4,12},{5,13},{6,14},{7,15},{8,16},{9,17... | collective-permute-start | bytes 208904 | tf_op jit(solution)/shard_map/ppermute | solution.py:34
  89.8 8.7 %maps.1 = (bf16[1536,256]{1,0:T(8,128)(2,1)S(1)}, f32[1536,128]{1,0:T(8,128)S(1)}, f32[32,1536]{1,0:T(8,128)S(1)}) custom-call(bf16[1536,2176]{1,0:T(8,128)(2,1)S(1)} %lay.3.x_ref, bf16[2048,384]{1,0:T(8,128)(2,1)S(1)} %copy-done.2, f32[1,128]{1,0:T(1,128)S(1)} %bitcast.20, f32[1,128]{1,0:T(1,128)S(1)} %bitcast.19), custom_call_target="tpu_custom_call" | custom-call | tf_op jit(solution)/shard_map/maps/pallas_call | solution.py:94
  98.5 4.5 %collective-permute-done.13.refs_3_ = bf16[1024,512]{1,0:T(8,128)(2,1)} collective-permute-done((bf16[1024,512]{1,0:T(8,128)(2,1)}, bf16[1024,512]{1,0:T(8,128)(2,1)}, u32[]{:S(2)}, u32[]{:S(2)}) %collective-permute-start.13) | collective-permute-done | bytes 1048608 | tf_op jit(solution)/shard_map/ppermute | solution.py:34
  103.0 1.8 collective-permute-done.14.refs_4_
  104.9 0.7 collective-permute-start.19
  105.6 15.8 %scan.1 = (f32[1536,256]{1,0:T(8,128)}, bf16[1536,256]{1,0:T(8,128)(2,1)S(1)}, bf16[144,256]{1,0:T(8,128)(2,1)S(1)}) custom-call(s32[1]{0:T(128)} %bitcast.pos_ref, bf16[1536,2176]{1,0:T(8,128)(2,1)} %copy-done.1, bf16[16,2176]{1,0:T(8,128)(2,1)S(1)} %collective-permute-done.16.edge_ref, bf16[1024,512]{1,0:T(8,128)(2,1)} %bitcast.5.refs_0_, ...), custom_call_target="tpu_custom_call" | custom-call | tf_op jit(solution)/shard_map/scan/pallas_call | solution.py:230
  121.4 5.6 %collective-permute-start.22 = (bf16[144,256]{1,0:T(8,128)(2,1)S(1)}, bf16[144,256]{1,0:T(8,128)(2,1)S(1)}, u32[]{:S(2)}, u32[]{:S(2)}) collective-permute-start(bf16[144,256]{1,0:T(8,128)(2,1)S(1)} %get-tuple-element.158), channel_id=1, source_target_pairs={{0,8},{1,9},{2,10},{3,11},{4,12},{5,13},{6,14},{7,15},{8,16},{9,17... | collective-permute-start | bytes 221192 | tf_op jit(solution)/shard_map/ppermute | solution.py:34
  127.1 1.3 collective-permute-start.23
  128.4 0.7 collective-permute-start.24
  129.1 4.2 %collective-permute-start.21 = (bf16[1024,256]{1,0:T(8,128)(2,1)}, bf16[1024,256]{1,0:T(8,128)(2,1)}, u32[]{:S(2)}, u32[]{:S(2)}) collective-permute-start(bf16[1024,256]{1,0:T(8,128)(2,1)} %bitcast.7.refs_2_), channel_id=1, source_target_pairs={{8,0},{9,1},{10,2},{11,3},{12,4},{13,5},{14,6},{15,7},{16,8},{17,9... | collective-permute-start | bytes 1572872 | tf_op jit(solution)/shard_map/ppermute | solution.py:34
  133.2 2.1 %collective-permute-start.20 = (bf16[1024,256]{1,0:T(8,128)(2,1)S(1)}, bf16[1024,256]{1,0:T(8,128)(2,1)}, u32[]{:S(2)}, u32[]{:S(2)}) collective-permute-start(bf16[1024,256]{1,0:T(8,128)(2,1)S(1)} %collective-permute-done.19.refs_0_), channel_id=1, source_target_pairs={{8,16},{9,17},{10,18},{11,19},{12,20},{13,21},{14,22},{15,23},{16,... | collective-permute-start | bytes 1572872 | tf_op jit(solution)/shard_map/ppermute | solution.py:34
  135.4 1.4 copy-done.7
  136.8 3.9 %norm.1 = (bf16[768,256]{1,0:T(8,128)(2,1)S(1)}, bf16[768,256]{1,0:T(8,128)(2,1)S(1)}) custom-call(s32[1]{0:T(128)} %bitcast.1.pos_ref, bf16[1536,256]{1,0:T(8,128)(2,1)S(1)} %get-tuple-element.144.refs_5_.maps_ref, f32[1536,128]{1,0:T(8,128)S(1)} %get-tuple-element.145.refs_6_.cols_ref, f32[1,256]{1,0:T(1,128)S(1)} %bitcast.18, f32[1536,256]{1,0:T(8,128)S(1)} %copy-done.7, ...), custom_call_target="tpu_custom_call" | custom-call | tf_op jit(solution)/shard_map/norm/pallas_call | solution.py:317
  141.4 1.9 %collective-permute-done.26.other_ref = bf16[768,256]{1,0:T(8,128)(2,1)S(1)} collective-permute-done((bf16[768,256]{1,0:T(8,128)(2,1)S(1)}, bf16[768,256]{1,0:T(8,128)(2,1)S(1)}, u32[]{:S(2)}, u32[]{:S(2)}) %collective-permute-start.26) | collective-permute-done | bytes 393248 | tf_op jit(solution)/shard_map/ppermute | solution.py:34
  143.3 3.4 %project_out.2 = (bf16[192,1024]{1,0:T(8,128)(2,1)S(1)}, bf16[192,1024]{1,0:T(8,128)(2,1)S(1)}, bf16[192,1024]{1,0:T(8,128)(2,1)S(1)}, bf16[192,1024]{1,0:T(8,128)(2,1)S(1)}) custom-call(s32[2]{0:T(128)S(1)} %pad_add_fusion.1.pos_ref, bf16[768,128]{1,0:T(8,128)(2,1)S(1)} %constant_dynamic-slice_fusion.ids_ref, ...), custom_call_target="tpu_custom_call" | custom-call | tf_op jit(solution)/shard_map/project_out/pallas_call | solution.py:358
  146.7 1.2 collective-permute-done.20
  147.9 1.1 broadcast_select_fusion.refs_2_
  149.1 0.9 collective-permute-start.27
  150.0 1.5 collective-permute-start.28
  151.5 1.1 collective-permute-start.29
  152.7 2.5 %project_out.3 = (bf16[192,1024]{1,0:T(8,128)(2,1)S(1)}, bf16[192,1024]{1,0:T(8,128)(2,1)S(1)}, bf16[192,1024]{1,0:T(8,128)(2,1)S(1)}, bf16[192,1024]{1,0:T(8,128)(2,1)S(1)}) custom-call(s32[2]{0:T(128)S(1)} %pad_add_fusion.1.pos_ref, bf16[768,128]{1,0:T(8,128)(2,1)S(1)} %constant_dynamic-slice_fusion.ids_ref, ...), custom_call_target="tpu_custom_call" | custom-call | tf_op jit(solution)/shard_map/project_out/pallas_call | solution.py:358
  155.1 0.9 collective-permute-start.31
  156.0 1.5 collective-permute-start.32
  157.5 3.5 %collective-permute-done.27.refs_1_ = bf16[192,1024]{1,0:T(8,128)(2,1)S(1)} collective-permute-done((bf16[192,1024]{1,0:T(8,128)(2,1)S(1)}, bf16[192,1024]{1,0:T(8,128)(2,1)S(1)}, u32[]{:S(2)}, u32[]{:S(2)}) %collective-permute-start.27) | collective-permute-done | bytes 393248 | tf_op jit(solution)/shard_map/ppermute | solution.py:34
  161.1 1.8 collective-permute-start.33
  163.0 7.4 %collective-permute-done.28.refs_2_ = bf16[192,1024]{1,0:T(8,128)(2,1)S(1)} collective-permute-done((bf16[192,1024]{1,0:T(8,128)(2,1)S(1)}, bf16[192,1024]{1,0:T(8,128)(2,1)S(1)}, u32[]{:S(2)}, u32[]{:S(2)}) %collective-permute-start.28) | collective-permute-done | bytes 393248 | tf_op jit(solution)/shard_map/ppermute | solution.py:34
  170.4 7.6 %collective-permute-done.31.refs_5_ = bf16[192,1024]{1,0:T(8,128)(2,1)S(1)} collective-permute-done((bf16[192,1024]{1,0:T(8,128)(2,1)S(1)}, bf16[192,1024]{1,0:T(8,128)(2,1)S(1)}, u32[]{:S(2)}, u32[]{:S(2)}) %collective-permute-start.31) | collective-permute-done | bytes 393248 | tf_op jit(solution)/shard_map/ppermute | solution.py:34
  178.0 8.5 %collective-permute-done.32.refs_6_ = bf16[192,1024]{1,0:T(8,128)(2,1)S(1)} collective-permute-done((bf16[192,1024]{1,0:T(8,128)(2,1)S(1)}, bf16[192,1024]{1,0:T(8,128)(2,1)S(1)}, u32[]{:S(2)}, u32[]{:S(2)}) %collective-permute-start.32) | collective-permute-done | bytes 393248 | tf_op jit(solution)/shard_map/ppermute | solution.py:34
  186.5 1.8 add_up.1
  (91 shorter events, 5.0 us)
Async XLA Ops:
  0.0 40.6 %copy-start = (f32[4,512]{1,0:T(4,128)S(1)}, f32[4,512]{1,0:T(4,128)}, u32[]{:S(2)}) copy-start(f32[4,512]{1,0:T(4,128)} %param.23) | copy-start | bytes 24580
  0.0 9.0 %copy-start.18 = (s32[192,1]{0,1:T(1,128)S(1)}, s32[192,1]{0,1:T(1,128)}, u32[]{:S(2)}) copy-start(s32[192,1]{0,1:T(1,128)} %param.13) | copy-start | bytes 2308
  0.0 9.2 %copy-start.19 = (bf16[192]{0:T(256)(128)(2,1)S(1)}, bf16[192]{0:T(256)(128)(2,1)}, u32[]{:S(2)}) copy-start(bf16[192]{0:T(256)(128)(2,1)} %param.14) | copy-start | bytes 1156
  0.0 21.1 %collective-permute-start.4 = (bf16[1024,256]{1,0:T(8,128)(2,1)}, bf16[1024,256]{1,0:T(8,128)(2,1)S(1)}, u32[]{:S(2)}, u32[]{:S(2)}) collective-permute-start(bf16[1024,256]{1,0:T(8,128)(2,1)} %bitcast.16), channel_id=1, source_target_pairs={{0,24},{1,25},{2,26},{3,27},{4,28},{5,29},{6,30},{7,31},{8,0},{9,1... | collective-permute-start | bytes 1572872 | tf_op jit(solution)/shard_map/ppermute | solution.py:34
  0.5 27.3 %copy-start.17 = (bf16[32,2048]{1,0:T(8,128)(2,1)S(1)}, bf16[32,2048]{1,0:T(8,128)(2,1)}, u32[]{:S(2)}) copy-start(bf16[32,2048]{1,0:T(8,128)(2,1)} %param.18) | copy-start | bytes 393220
  2.9 7.7 %collective-permute-start = (bf16[256,512]{1,0:T(8,128)(2,1)}, bf16[256,512]{1,0:T(8,128)(2,1)S(1)}, u32[]{:S(2)}, u32[]{:S(2)}) collective-permute-start(bf16[256,512]{1,0:T(8,128)(2,1)} %get-tuple-element.93), channel_id=1, source_target_pairs={{0,0},{1,4},{2,2},{3,6},{4,1},{5,5},{6,3},{7,7},{8,8},{9,12},{10,1... | collective-permute-start | bytes 786440 | tf_op jit(solution)/shard_map/ppermute | solution.py:34
  4.5 8.4 %collective-permute-start.1 = (bf16[256,512]{1,0:T(8,128)(2,1)S(1)}, bf16[256,512]{1,0:T(8,128)(2,1)S(1)}, u32[]{:S(2)}, u32[]{:S(2)}) collective-permute-start(bf16[256,512]{1,0:T(8,128)(2,1)S(1)} %get-tuple-element.94), channel_id=1, source_target_pairs={{0,1},{1,5},{2,3},{3,7},{4,0},{5,4},{6,2},{7,6},{8,9},{9,13},{10,1... | collective-permute-start | bytes 786440 | tf_op jit(solution)/shard_map/ppermute | solution.py:34
  6.3 13.8 %collective-permute-start.2 = (bf16[256,512]{1,0:T(8,128)(2,1)S(1)}, bf16[256,512]{1,0:T(8,128)(2,1)S(1)}, u32[]{:S(2)}, u32[]{:S(2)}) collective-permute-start(bf16[256,512]{1,0:T(8,128)(2,1)S(1)} %get-tuple-element.95), channel_id=1, source_target_pairs={{0,2},{1,6},{2,0},{3,4},{4,3},{5,7},{6,1},{7,5},{8,10},{9,14},{10,... | collective-permute-start | bytes 786440 | tf_op jit(solution)/shard_map/ppermute | solution.py:34
  7.9 13.3 %collective-permute-start.3 = (bf16[256,512]{1,0:T(8,128)(2,1)S(1)}, bf16[256,512]{1,0:T(8,128)(2,1)S(1)}, u32[]{:S(2)}, u32[]{:S(2)}) collective-permute-start(bf16[256,512]{1,0:T(8,128)(2,1)S(1)} %get-tuple-element.96), channel_id=1, source_target_pairs={{0,3},{1,7},{2,1},{3,5},{4,2},{5,6},{6,0},{7,4},{8,11},{9,15},{10,... | collective-permute-start | bytes 786440 | tf_op jit(solution)/shard_map/ppermute | solution.py:34
  10.6 27.2 %copy-start.3 = (bf16[192,2176]{1,0:T(8,128)(2,1)}, bf16[192,2176]{1,0:T(8,128)(2,1)S(1)}, u32[]{:S(2)}) copy-start(bf16[192,2176]{1,0:T(8,128)(2,1)S(1)} %concatenate.22.refs_0_) | copy-start | bytes 2506756
  21.1 1.2 copy-start.15
  22.3 22.5 %collective-permute-start.9 = (bf16[192,2176]{1,0:T(8,128)(2,1)S(1)}, bf16[192,2176]{1,0:T(8,128)(2,1)S(1)}, u32[]{:S(2)}, u32[]{:S(2)}) collective-permute-start(bf16[192,2176]{1,0:T(8,128)(2,1)S(1)} %concatenate.22.refs_0_), channel_id=1, source_target_pairs={{0,3},{1,2},{2,1},{3,0},{4,7},{5,6},{6,5},{7,4},{8,11},{9,10},{10,... | collective-permute-start | bytes 2506760 | tf_op jit(solution)/shard_map/ppermute | solution.py:34
  22.9 39.7 %collective-permute-start.8 = (bf16[192,2176]{1,0:T(8,128)(2,1)S(1)}, bf16[192,2176]{1,0:T(8,128)(2,1)S(1)}, u32[]{:S(2)}, u32[]{:S(2)}) collective-permute-start(bf16[192,2176]{1,0:T(8,128)(2,1)S(1)} %concatenate.22.refs_0_), channel_id=1, source_target_pairs={{0,2},{1,3},{2,0},{3,1},{4,6},{5,7},{6,4},{7,5},{8,10},{9,11},{10,... | collective-permute-start | bytes 2506760 | tf_op jit(solution)/shard_map/ppermute | solution.py:34
  24.4 40.6 %collective-permute-start.7 = (bf16[192,2176]{1,0:T(8,128)(2,1)S(1)}, bf16[192,2176]{1,0:T(8,128)(2,1)S(1)}, u32[]{:S(2)}, u32[]{:S(2)}) collective-permute-start(bf16[192,2176]{1,0:T(8,128)(2,1)S(1)} %concatenate.22.refs_0_), channel_id=1, source_target_pairs={{0,1},{1,0},{2,3},{3,2},{4,5},{5,4},{6,7},{7,6},{8,9},{9,8},{10,11... | collective-permute-start | bytes 2506760 | tf_op jit(solution)/shard_map/ppermute | solution.py:34
  25.8 49.1 %collective-permute-start.5 = (bf16[1024,512]{1,0:T(8,128)(2,1)}, bf16[1024,512]{1,0:T(8,128)(2,1)}, u32[]{:S(2)}, u32[]{:S(2)}) collective-permute-start(bf16[1024,512]{1,0:T(8,128)(2,1)} %bitcast.5.refs_0_), channel_id=1, source_target_pairs={{0,8},{1,9},{2,10},{3,11},{4,12},{5,13},{6,14},{7,15},{8,16},{9,17... | collective-permute-start | bytes 3145736 | tf_op jit(solution)/shard_map/ppermute | solution.py:34
  27.4 47.5 %collective-permute-start.6 = (bf16[1024,512]{1,0:T(8,128)(2,1)}, bf16[1024,512]{1,0:T(8,128)(2,1)}, u32[]{:S(2)}, u32[]{:S(2)}) collective-permute-start(bf16[1024,512]{1,0:T(8,128)(2,1)} %bitcast.5.refs_0_), channel_id=1, source_target_pairs={{0,24},{1,25},{2,26},{3,27},{4,28},{5,29},{6,30},{7,31},{8,0},{9,1... | collective-permute-start | bytes 3145736 | tf_op jit(solution)/shard_map/ppermute | solution.py:34
  30.1 7.7 %copy-start.21 = (f32[8]{0:T(128)S(1)}, f32[8]{0:T(128)}, u32[]{:S(2)}) copy-start(f32[8]{0:T(128)} %param.21) | copy-start | bytes 100
  30.1 8.0 %copy-start.22 = (f32[8]{0:T(128)S(1)}, f32[8]{0:T(128)}, u32[]{:S(2)}) copy-start(f32[8]{0:T(128)} %param.19) | copy-start | bytes 100
  30.1 8.1 %copy-start.23 = (f32[8]{0:T(128)S(1)}, f32[8]{0:T(128)}, u32[]{:S(2)}) copy-start(f32[8]{0:T(128)} %param.20) | copy-start | bytes 100
  31.0 9.5 %copy-start.20 = (f32[512]{0:T(512)S(1)}, f32[512]{0:T(512)}, u32[]{:S(2)}) copy-start(f32[512]{0:T(512)} %param.22) | copy-start | bytes 6148
  38.4 1.0 copy-start.14
  39.4 1.0 copy-start.16
  40.5 28.2 %copy-start.4 = (bf16[192,2176]{1,0:T(8,128)(2,1)S(1)}, bf16[192,2176]{1,0:T(8,128)(2,1)}, u32[]{:S(2)}) copy-start(bf16[192,2176]{1,0:T(8,128)(2,1)} %copy-done.3) | copy-start | bytes 2506756
  44.8 0.9 copy-start.8
  45.7 23.0 %copy-start.9 = (bf16[192,2176]{1,0:T(8,128)(2,1)S(1)}, bf16[192,2176]{1,0:T(8,128)(2,1)}, u32[]{:S(2)}) copy-start(bf16[192,2176]{1,0:T(8,128)(2,1)} %copy-done.8) | copy-start | bytes 2506756
  45.7 23.6 %collective-permute-start.12 = (bf16[512,256]{1,0:T(8,128)(2,1)S(1)}, bf16[512,256]{1,0:T(8,128)(2,1)S(1)}, u32[]{:S(2)}, u32[]{:S(2)}) collective-permute-start(bf16[512,256]{1,0:T(8,128)(2,1)S(1)} %get-tuple-element.116), channel_id=1, source_target_pairs={{0,3},{1,2},{2,1},{3,0},{4,7},{5,6},{6,5},{7,4},{8,11},{9,10},{10,... | collective-permute-start | bytes 786440 | tf_op jit(solution)/shard_map/ppermute | solution.py:34
  62.6 0.9 copy-start.10
  63.5 5.2 %copy-start.11 = (bf16[192,2176]{1,0:T(8,128)(2,1)S(1)}, bf16[192,2176]{1,0:T(8,128)(2,1)}, u32[]{:S(2)}) copy-start(bf16[192,2176]{1,0:T(8,128)(2,1)} %copy-done.10) | copy-start | bytes 2506756
  63.5 8.4 %collective-permute-start.11 = (bf16[512,256]{1,0:T(8,128)(2,1)S(1)}, bf16[512,256]{1,0:T(8,128)(2,1)S(1)}, u32[]{:S(2)}, u32[]{:S(2)}) collective-permute-start(bf16[512,256]{1,0:T(8,128)(2,1)S(1)} %get-tuple-element.115), channel_id=1, source_target_pairs={{0,2},{1,3},{2,0},{3,1},{4,6},{5,7},{6,4},{7,5},{8,10},{9,11},{10,... | collective-permute-start | bytes 786440 | tf_op jit(solution)/shard_map/ppermute | solution.py:34
  65.0 0.9 copy-start.12
  65.9 2.8 %copy-start.13 = (bf16[192,2176]{1,0:T(8,128)(2,1)S(1)}, bf16[192,2176]{1,0:T(8,128)(2,1)}, u32[]{:S(2)}) copy-start(bf16[192,2176]{1,0:T(8,128)(2,1)} %copy-done.12) | copy-start | bytes 2506756
  65.9 8.0 %collective-permute-start.10 = (bf16[512,256]{1,0:T(8,128)(2,1)S(1)}, bf16[512,256]{1,0:T(8,128)(2,1)S(1)}, u32[]{:S(2)}, u32[]{:S(2)}) collective-permute-start(bf16[512,256]{1,0:T(8,128)(2,1)S(1)} %get-tuple-element.114), channel_id=1, source_target_pairs={{0,1},{1,0},{2,3},{3,2},{4,5},{5,4},{6,7},{7,6},{8,9},{9,8},{10,11... | collective-permute-start | bytes 786440 | tf_op jit(solution)/shard_map/ppermute | solution.py:34
  74.9 7.9 %collective-permute-start.15 = (bf16[768,2176]{1,0:T(8,128)(2,1)S(1)}, bf16[768,2176]{1,0:T(8,128)(2,1)S(1)}, u32[]{:S(2)}, u32[]{:S(2)}) collective-permute-start(bf16[768,2176]{1,0:T(8,128)(2,1)S(1)} %lay.2.refs_0_), channel_id=1, source_target_pairs={{0,4},{1,5},{2,6},{3,7},{4,0},{5,1},{6,2},{7,3},{8,12},{9,13},{10,... | collective-permute-start | bytes 10027016 | tf_op jit(solution)/shard_map/ppermute | solution.py:34
  74.9 28.2 %collective-permute-start.13 = (bf16[1024,512]{1,0:T(8,128)(2,1)}, bf16[1024,512]{1,0:T(8,128)(2,1)}, u32[]{:S(2)}, u32[]{:S(2)}) collective-permute-start(bf16[1024,512]{1,0:T(8,128)(2,1)} %collective-permute-done.5.refs_1_), channel_id=1, source_target_pairs={{8,16},{9,17},{10,18},{11,19},{12,20},{13,21},{14,22},{15,23},{16,... | collective-permute-start | bytes 3145736 | tf_op jit(solution)/shard_map/ppermute | solution.py:34
  78.4 26.5 %collective-permute-start.14 = (bf16[1024,512]{1,0:T(8,128)(2,1)}, bf16[1024,512]{1,0:T(8,128)(2,1)}, u32[]{:S(2)}, u32[]{:S(2)}) collective-permute-start(bf16[1024,512]{1,0:T(8,128)(2,1)} %collective-permute-done.6.refs_2_), channel_id=1, source_target_pairs={{8,0},{9,1},{10,2},{11,3},{12,4},{13,5},{14,6},{15,7},{16,8},{17,9... | collective-permute-start | bytes 3145736 | tf_op jit(solution)/shard_map/ppermute | solution.py:34
  82.7 1.7 copy-start.5
  84.4 20.4 %collective-permute-start.17 = (bf16[1024,256]{1,0:T(8,128)(2,1)}, bf16[1024,256]{1,0:T(8,128)(2,1)}, u32[]{:S(2)}, u32[]{:S(2)}) collective-permute-start(bf16[1024,256]{1,0:T(8,128)(2,1)} %bitcast.6.refs_0_), channel_id=1, source_target_pairs={{0,4},{1,5},{2,6},{3,7},{4,0},{5,1},{6,2},{7,3},{8,12},{9,13},{10,... | collective-permute-start | bytes 1572872 | tf_op jit(solution)/shard_map/ppermute | solution.py:34
  84.4 20.4 %collective-permute-start.18 = (bf16[1024,256]{1,0:T(8,128)(2,1)}, bf16[1024,256]{1,0:T(8,128)(2,1)}, u32[]{:S(2)}, u32[]{:S(2)}) collective-permute-start(bf16[1024,256]{1,0:T(8,128)(2,1)} %bitcast.7.refs_2_), channel_id=1, source_target_pairs={{0,4},{1,5},{2,6},{3,7},{4,0},{5,1},{6,2},{7,3},{8,12},{9,13},{10,... | collective-permute-start | bytes 1572872 | tf_op jit(solution)/shard_map/ppermute | solution.py:34
  84.9 1.9 %copy-start.6 = (bf16[768,2176]{1,0:T(8,128)(2,1)S(1)}, bf16[768,2176]{1,0:T(8,128)(2,1)}, u32[]{:S(2)}) copy-start(bf16[768,2176]{1,0:T(8,128)(2,1)} %copy-done.5) | copy-start | bytes 10027012
  86.9 2.9 %copy-start.2 = (bf16[2048,384]{1,0:T(8,128)(2,1)S(1)}, bf16[2048,384]{1,0:T(8,128)(2,1)}, u32[]{:S(2)}) copy-start(bf16[2048,384]{1,0:T(8,128)(2,1)} %pad_maximum_fusion.w_ref) | copy-start | bytes 4718596
  87.9 10.6 %copy-start.1 = (bf16[1536,2176]{1,0:T(8,128)(2,1)}, bf16[1536,2176]{1,0:T(8,128)(2,1)S(1)}, u32[]{:S(2)}) copy-start(bf16[1536,2176]{1,0:T(8,128)(2,1)S(1)} %lay.3.x_ref) | copy-start | bytes 20054020
  87.9 17.0 %collective-permute-start.16 = (bf16[16,2176]{1,0:T(8,128)(2,1)S(1)}, bf16[16,2176]{1,0:T(8,128)(2,1)S(1)}, u32[]{:S(2)}, u32[]{:S(2)}) collective-permute-start(bf16[16,2176]{1,0:T(8,128)(2,1)S(1)} %slice.4), channel_id=1, source_target_pairs={{0,8},{1,9},{2,10},{3,11},{4,12},{5,13},{6,14},{7,15},{8,16},{9,17... | collective-permute-start | bytes 208904 | tf_op jit(solution)/shard_map/ppermute | solution.py:34
  104.9 16.6 %collective-permute-start.19 = (bf16[1024,256]{1,0:T(8,128)(2,1)}, bf16[1024,256]{1,0:T(8,128)(2,1)S(1)}, u32[]{:S(2)}, u32[]{:S(2)}) collective-permute-start(bf16[1024,256]{1,0:T(8,128)(2,1)} %bitcast.6.refs_0_), channel_id=1, source_target_pairs={{0,8},{1,9},{2,10},{3,11},{4,12},{5,13},{6,14},{7,15},{8,16},{9,17... | collective-permute-start | bytes 1572872 | tf_op jit(solution)/shard_map/ppermute | solution.py:34
  121.4 13.9 %collective-permute-start.22 = (bf16[144,256]{1,0:T(8,128)(2,1)S(1)}, bf16[144,256]{1,0:T(8,128)(2,1)S(1)}, u32[]{:S(2)}, u32[]{:S(2)}) collective-permute-start(bf16[144,256]{1,0:T(8,128)(2,1)S(1)} %get-tuple-element.158), channel_id=1, source_target_pairs={{0,8},{1,9},{2,10},{3,11},{4,12},{5,13},{6,14},{7,15},{8,16},{9,17... | collective-permute-start | bytes 221192 | tf_op jit(solution)/shard_map/ppermute | solution.py:34
  127.1 8.3 %collective-permute-start.23 = (bf16[144,256]{1,0:T(8,128)(2,1)S(1)}, bf16[144,256]{1,0:T(8,128)(2,1)S(1)}, u32[]{:S(2)}, u32[]{:S(2)}) collective-permute-start(bf16[144,256]{1,0:T(8,128)(2,1)S(1)} %get-tuple-element.158), channel_id=1, source_target_pairs={{0,16},{1,17},{2,18},{3,19},{4,20},{5,21},{6,22},{7,23},{8,24},{9,... | collective-permute-start | bytes 221192 | tf_op jit(solution)/shard_map/ppermute | solution.py:34
  128.4 7.0 %collective-permute-start.24 = (bf16[144,256]{1,0:T(8,128)(2,1)S(1)}, bf16[144,256]{1,0:T(8,128)(2,1)S(1)}, u32[]{:S(2)}, u32[]{:S(2)}) collective-permute-start(bf16[144,256]{1,0:T(8,128)(2,1)S(1)} %get-tuple-element.158), channel_id=1, source_target_pairs={{0,24},{1,25},{2,26},{3,27},{4,28},{5,29},{6,30},{7,31}} | collective-permute-start | bytes 221192 | tf_op jit(solution)/shard_map/ppermute | solution.py:34
  129.1 17.6 %collective-permute-start.21 = (bf16[1024,256]{1,0:T(8,128)(2,1)}, bf16[1024,256]{1,0:T(8,128)(2,1)}, u32[]{:S(2)}, u32[]{:S(2)}) collective-permute-start(bf16[1024,256]{1,0:T(8,128)(2,1)} %bitcast.7.refs_2_), channel_id=1, source_target_pairs={{8,0},{9,1},{10,2},{11,3},{12,4},{13,5},{14,6},{15,7},{16,8},{17,9... | collective-permute-start | bytes 1572872 | tf_op jit(solution)/shard_map/ppermute | solution.py:34
  133.2 14.7 %collective-permute-start.20 = (bf16[1024,256]{1,0:T(8,128)(2,1)S(1)}, bf16[1024,256]{1,0:T(8,128)(2,1)}, u32[]{:S(2)}, u32[]{:S(2)}) collective-permute-start(bf16[1024,256]{1,0:T(8,128)(2,1)S(1)} %collective-permute-done.19.refs_0_), channel_id=1, source_target_pairs={{8,16},{9,17},{10,18},{11,19},{12,20},{13,21},{14,22},{15,23},{16,... | collective-permute-start | bytes 1572872 | tf_op jit(solution)/shard_map/ppermute | solution.py:34
  135.4 1.4 copy-start.7
  140.7 7.2 %collective-permute-start.25 = (bf16[1024,256]{1,0:T(8,128)(2,1)S(1)}, bf16[1024,256]{1,0:T(8,128)(2,1)S(1)}, u32[]{:S(2)}, u32[]{:S(2)}) collective-permute-start(bf16[1024,256]{1,0:T(8,128)(2,1)S(1)} %collective-permute-done.19.refs_0_), channel_id=1, source_target_pairs={{0,4},{1,5},{2,6},{3,7},{4,0},{5,1},{6,2},{7,3},{8,12},{9,13},{10,... | collective-permute-start | bytes 1572872 | tf_op jit(solution)/shard_map/ppermute | solution.py:34
  140.8 2.5 %collective-permute-start.26 = (bf16[768,256]{1,0:T(8,128)(2,1)S(1)}, bf16[768,256]{1,0:T(8,128)(2,1)S(1)}, u32[]{:S(2)}, u32[]{:S(2)}) collective-permute-start(bf16[768,256]{1,0:T(8,128)(2,1)S(1)} %get-tuple-element.163), channel_id=1, source_target_pairs={{0,4},{1,5},{2,6},{3,7},{4,0},{5,1},{6,2},{7,3},{8,12},{9,13},{10,... | collective-permute-start | bytes 1179656 | tf_op jit(solution)/shard_map/ppermute | solution.py:34
  149.0 3.6 %collective-permute-start.30 = (bf16[1024,256]{1,0:T(8,128)(2,1)S(1)}, bf16[1024,256]{1,0:T(8,128)(2,1)S(1)}, u32[]{:S(2)}, u32[]{:S(2)}) collective-permute-start(bf16[1024,256]{1,0:T(8,128)(2,1)S(1)} %broadcast_select_fusion.refs_2_), channel_id=1, source_target_pairs={{0,4},{1,5},{2,6},{3,7},{4,0},{5,1},{6,2},{7,3},{8,12},{9,13},{10,... | collective-permute-start | bytes 1572872 | tf_op jit(solution)/shard_map/ppermute | solution.py:34
  149.1 12.0 %collective-permute-start.27 = (bf16[192,1024]{1,0:T(8,128)(2,1)S(1)}, bf16[192,1024]{1,0:T(8,128)(2,1)S(1)}, u32[]{:S(2)}, u32[]{:S(2)}) collective-permute-start(bf16[192,1024]{1,0:T(8,128)(2,1)S(1)} %get-tuple-element.171), channel_id=1, source_target_pairs={{0,1},{1,0},{2,3},{3,2},{4,5},{5,4},{6,7},{7,6},{8,9},{9,8},{10,11... | collective-permute-start | bytes 1179656 | tf_op jit(solution)/shard_map/ppermute | solution.py:34
  150.0 20.4 %collective-permute-start.28 = (bf16[192,1024]{1,0:T(8,128)(2,1)S(1)}, bf16[192,1024]{1,0:T(8,128)(2,1)S(1)}, u32[]{:S(2)}, u32[]{:S(2)}) collective-permute-start(bf16[192,1024]{1,0:T(8,128)(2,1)S(1)} %get-tuple-element.172), channel_id=1, source_target_pairs={{0,2},{1,3},{2,0},{3,1},{4,6},{5,7},{6,4},{7,5},{8,10},{9,11},{10,... | collective-permute-start | bytes 1179656 | tf_op jit(solution)/shard_map/ppermute | solution.py:34
  151.5 18.9 %collective-permute-start.29 = (bf16[192,1024]{1,0:T(8,128)(2,1)S(1)}, bf16[192,1024]{1,0:T(8,128)(2,1)S(1)}, u32[]{:S(2)}, u32[]{:S(2)}) collective-permute-start(bf16[192,1024]{1,0:T(8,128)(2,1)S(1)} %get-tuple-element.173), channel_id=1, source_target_pairs={{0,3},{1,2},{2,1},{3,0},{4,7},{5,6},{6,5},{7,4},{8,11},{9,10},{10,... | collective-permute-start | bytes 1179656 | tf_op jit(solution)/shard_map/ppermute | solution.py:34
  155.1 22.9 %collective-permute-start.31 = (bf16[192,1024]{1,0:T(8,128)(2,1)S(1)}, bf16[192,1024]{1,0:T(8,128)(2,1)S(1)}, u32[]{:S(2)}, u32[]{:S(2)}) collective-permute-start(bf16[192,1024]{1,0:T(8,128)(2,1)S(1)} %get-tuple-element.178), channel_id=1, source_target_pairs={{0,1},{1,0},{2,3},{3,2},{4,5},{5,4},{6,7},{7,6},{8,9},{9,8},{10,11... | collective-permute-start | bytes 1179656 | tf_op jit(solution)/shard_map/ppermute | solution.py:34
  156.0 30.5 %collective-permute-start.32 = (bf16[192,1024]{1,0:T(8,128)(2,1)S(1)}, bf16[192,1024]{1,0:T(8,128)(2,1)S(1)}, u32[]{:S(2)}, u32[]{:S(2)}) collective-permute-start(bf16[192,1024]{1,0:T(8,128)(2,1)S(1)} %get-tuple-element.179), channel_id=1, source_target_pairs={{0,2},{1,3},{2,0},{3,1},{4,6},{5,7},{6,4},{7,5},{8,10},{9,11},{10,... | collective-permute-start | bytes 1179656 | tf_op jit(solution)/shard_map/ppermute | solution.py:34
  161.1 25.4 %collective-permute-start.33 = (bf16[192,1024]{1,0:T(8,128)(2,1)S(1)}, bf16[192,1024]{1,0:T(8,128)(2,1)S(1)}, u32[]{:S(2)}, u32[]{:S(2)}) collective-permute-start(bf16[192,1024]{1,0:T(8,128)(2,1)S(1)} %get-tuple-element.180), channel_id=1, source_target_pairs={{0,3},{1,2},{2,1},{3,0},{4,7},{5,6},{6,5},{7,4},{8,11},{9,10},{10,... | collective-permute-start | bytes 1179656 | tf_op jit(solution)/shard_map/ppermute | solution.py:34

commit v3 on v2

--- a/solution.py
+++ b/solution.py
@@ -63,24 +63,41 @@
     return list(zip(ups, downs[::-1]))
 
 
-def maps_kernel(heads, width, x_ref, w_ref, bias_ref, rate_ref, maps_ref, cols_ref, rows_ref, total):
+def slice_of(z, distance, depth, rows):
+    return pl.multiple_of(lax.rem(z - distance + depth, depth) * rows, 128)
+
+
+def choose(extra_lanes, parts):
+    chosen = extra_lanes.astype(f32)[:, 0:1]
+    total = parts[0]
+    for e in range(1, len(parts)):
+        total = jnp.where(chosen == e, parts[e], total)
+    return total
+
+
+def ahead_kernel(experts, depth, width, distances, pos_ref, x_ref, w_ref, bias_ref, rate_ref, *refs):
+    slots, (part_ref, maps_ref, cols_ref, rows_ref, total) = refs[: len(distances)], refs[len(distances) :]
     length = x_ref.shape[0]
 
     @pl.when(pl.program_id(0) == 0)
     def _():
         total[...] = jnp.zeros_like(total)
 
+    added = x_ref[:, width:]
     found = jnp.dot(x_ref[:, :width], w_ref[...], preferred_element_type=f32).astype(bf16)
     state2 = maps_ref.shape[1]
     maps_ref[...] = found[:, :state2]
     raw = found[:, state2:].astype(f32) + bias_ref[...]
     steps = jnp.maximum(raw, 0.0) + jnp.log1p(jnp.exp(-jnp.abs(raw)))
-    damping = x_ref[:, width : width + extra].astype(f32)[:, 1:2]
-    logs = -(rate_ref[...] * steps + damping)
+    logs = -(rate_ref[...] * steps + added.astype(f32)[:, 1:2])
+    first = logs.astype(bf16)
+    second = (logs - first.astype(f32)).astype(bf16)
+    third = (logs - first.astype(f32) - second.astype(f32)).astype(bf16)
     row = lax.broadcasted_iota(jnp.int32, (length, length), 0)
     col = lax.broadcasted_iota(jnp.int32, (length, length), 1)
-    lower = (row >= col).astype(f32)
-    climb = jnp.dot(lower, logs, precision=highest, preferred_element_type=f32)
+    lower = (row >= col).astype(bf16)
+    sums = jnp.dot(lower, jnp.concatenate([first, second, third], axis=1), preferred_element_type=f32)
+    climb = sums[:, :128] + (sums[:, 128:256] + sums[:, 256:])
     lane = lax.broadcasted_iota(jnp.int32, climb.shape, 1)
     reach = climb + total[...]
     packed = jnp.where(lane < dt_lane, climb, jnp.where(lane < reach_lane, steps, reach))
@@ -88,83 +105,108 @@
     rows_ref[...] = jnp.transpose(packed)[: rows_ref.shape[0]]
     total[...] = reach[length - 1 : length]
 
-
-def maps(tokens, w_maps, bias, rate, heads, state2, length):
-    count, width = tokens.shape[0], w_maps.shape[0]
-    return pl.pallas_call(
-        functools.partial(maps_kernel, heads, width),
-        grid=(count // length,),
-        in_specs=[
-            pl.BlockSpec((length, tokens.shape[1]), lambda b: (b, 0)),
-            vmem(*w_maps.shape),
-            vmem(1, 128),
-            vmem(1, 128),
-        ],
-        out_specs=[
-            pl.BlockSpec((length, state2), lambda b: (b, 0)),
-            pl.BlockSpec((length, 128), lambda b: (b, 0)),
-            pl.BlockSpec((reach_lane, length), lambda b: (0, b)),
-        ],
+    depth_rows = width // depth
+    parts = []
+    for e in range(experts):
+        part = 0.0
+        for distance, slot in zip(distances, slots):
+            x = x_ref[:, pl.ds(slice_of(pos_ref[0], distance, depth, depth_rows), depth_rows)]
+            part += jnp.dot(x, slot[e * depth_rows : (e + 1) * depth_rows, :], preferred_element_type=f32)
+        parts.append(part)
+    part_ref[...] = choose(added, parts)
+
+
+def ahead(position, tokens, w_maps, bias, rate, slots, distances, experts, depth, state2, length):
+    count, width, columns = tokens.shape[0], w_maps.shape[0], slots[0].shape[1]
+    block = lambda *shape: pl.BlockSpec(shape, lambda b, _: (b, 0))
+    return pl.pallas_call(
+        functools.partial(ahead_kernel, experts, depth, width, distances),
+        grid_spec=pltpu.PrefetchScalarGridSpec(
+            num_scalar_prefetch=1,
+            grid=(count // length,),
+            in_specs=[block(length, tokens.shape[1])]
+            + [vmem(*w_maps.shape), vmem(1, 128), vmem(1, 128)]
+            + [vmem(*slot.shape) for slot in slots],
+            out_specs=[
+                block(length, columns),
+                block(length, state2),
+                block(length, 128),
+                pl.BlockSpec((reach_lane, length), lambda b, _: (0, b)),
+            ],
+            scratch_shapes=[pltpu.VMEM((1, 128), f32)],
+        ),
         out_shape=[
+            jax.ShapeDtypeStruct((count, columns), f32),
             jax.ShapeDtypeStruct((count, state2), bf16),
             jax.ShapeDtypeStruct((count, 128), f32),
             jax.ShapeDtypeStruct((reach_lane, count), f32),
         ],
-        scratch_shapes=[pltpu.VMEM((1, 128), f32)],
-        compiler_params=params(32),
-        name="maps",
-    )(tokens, w_maps, bias, rate)
-
-
-def scan_kernel(
-    first_head, head, experts, depth, width, near, middle, pos_ref, x_ref, edge_ref, *refs
-):
-    slots = refs[: near + 2 * middle]
-    maps_ref, cols_ref, rows_ref, taps_ref, skip_ref = refs[near + 2 * middle :][:5]
-    earlier = refs[near + 2 * middle + 5 : -6]
-    y_ref, gate_ref, final_ref, whole, seen, state = refs[-6:]
+        compiler_params=params(40),
+        name="ahead",
+    )(position, tokens, w_maps, bias, rate, *slots)
+
+
+def scan_kernel(head, experts, depth, width, distances, middle, pos_ref, *refs):
+    near, count = len(distances), len(middle)
+    slots, pairs = refs[:near], refs[near : near + 2 * count]
+    xs, refs = refs[near + 2 * count : near + 3 * count], refs[near + 3 * count :]
+    extra_ref, edge_ref, part_ref, maps_ref, cols_ref, rows_ref, taps_ref, skip_ref = refs[:8]
+    y_ref, gate_ref, final_ref, nears, fars, seen, state, sems = refs[8:]
     length, channels = y_ref.shape
     taps = taps_ref.shape[0]
     width_state = maps_ref.shape[1] // 2
     step, z = pl.program_id(0), pos_ref[0]
     depth_rows = width // depth
-
-    def place(ref, distance):
-        rows = pl.ds(pl.multiple_of(lax.rem(z - distance + depth, depth) * depth_rows, 128), depth_rows)
-        for e in range(experts):
-            whole[e, rows, :] = ref[e * depth_rows : (e + 1) * depth_rows, :]
-
-    def project(tokens):
-        chosen = tokens[:, width : width + extra].astype(f32)[:, 0:1]
-        total = jnp.dot(tokens[:, :width], whole[0], preferred_element_type=f32)
-        for e in range(1, experts):
-            other = jnp.dot(tokens[:, :width], whole[e], preferred_element_type=f32)
-            total = jnp.where(chosen == e, other, total)
-        total = total.astype(bf16)
-        return total[:, :channels], total[:, channels:]
+    near_copies = [pltpu.make_async_copy(slots[i], nears.at[i], sems.at[i]) for i in range(near)]
+
+    def far(m, action):
+        up, down = (
+            pltpu.make_async_copy(pairs[2 * m + i], fars.at[m], sems.at[near + m]) for i in range(2)
+        )
+
+        @pl.when(z >= middle[m])
+        def _():
+            action(up)
+
+        @pl.when(z < middle[m])
+        def _():
+            action(down)
+
+    def expert(ref, e):
+        return ref[e * depth_rows : (e + 1) * depth_rows, :]
 
     @pl.when(step == 0)
     def _():
-        for at, distance in zip(range(near), (0, 1, depth - 1)):
-            place(slots[at], distance)
-        for at in range(middle):
-            distance = at + 2
-
-            @pl.when(z >= distance)
-            def _():
-                place(slots[near + 2 * at], distance)
-
-            @pl.when(z < distance)
-            def _():
-                place(slots[near + 2 * at + 1], distance)
-
-        before, _ = project(edge_ref[...])
-        seen[0:8, :] = before[halo - 8 :].astype(f32)
+        for m in range(count):
+            far(m, lambda copy: copy.start())
+        for copy in near_copies:
+            copy.start()
         state[...] = jnp.zeros_like(state)
-
-    inner, gate = project(x_ref[...])
-    gate_ref[...] = gate
-    seen[8:, :] = inner.astype(f32)
+        for m in range(count):
+            far(m, lambda copy: copy.wait())
+        for copy in near_copies:
+            copy.wait()
+        parts = []
+        for e in range(experts):
+            total = 0.0
+            for distance, ref in [(d, nears.at[i]) for i, d in enumerate(distances)] + [
+                (d, fars.at[i]) for i, d in enumerate(middle)
+            ]:
+                x = edge_ref[:, pl.ds(slice_of(z, distance, depth, depth_rows), depth_rows)]
+                total += jnp.dot(x, expert(ref, e), preferred_element_type=f32)
+            parts.append(total)
+        before = choose(edge_ref[:, width:], parts).astype(bf16)
+        seen[0:8, :] = before[halo - 8 :, :channels].astype(f32)
+
+    parts = []
+    for e in range(experts):
+        total = 0.0
+        for m in range(count):
+            total += jnp.dot(xs[m][...], expert(fars.at[m], e), preferred_element_type=f32)
+        parts.append(total)
+    whole = (part_ref[...] + choose(extra_ref[...], parts)).astype(bf16)
+    gate_ref[...] = whole[:, channels:]
+    seen[8:, :] = whole[:, :channels].astype(f32)
     mixed = jnp.zeros((length, channels), f32)
     for tap in range(taps):
         mixed = mixed + taps_ref[tap : tap + 1, :] * seen[pl.ds(8 - (taps - 1) + tap, length), :]
@@ -179,13 +221,11 @@
     gram = jnp.where(lower, gram, 0.0)
     lane = lax.broadcasted_iota(jnp.int32, (1, channels), 1)
     rounded = values.astype(bf16)
-    inside, growth, ends, decay = [], 0.0, 0.0, 0.0
-    reached = 0.0
+    inside, growth, ends, decay, reached = [], 0.0, 0.0, 0.0, 0.0
     for j in range(channels // head):
-        at = first_head + j
         mine = lane // head == j
-        climb, size = cols_ref[:, at : at + 1], cols_ref[:, dt_lane + at : dt_lane + at + 1]
-        climb_row, size_row = rows_ref[at : at + 1, :], rows_ref[dt_lane + at : dt_lane + at + 1, :]
+        climb, size = cols_ref[:, j : j + 1], cols_ref[:, dt_lane + j : dt_lane + j + 1]
+        climb_row, size_row = rows_ref[j : j + 1, :], rows_ref[dt_lane + j : dt_lane + j + 1, :]
         spread = jnp.exp(jnp.where(lower, climb - climb_row, 0.0)) * gram * size_row
         inside.append(
             jnp.dot(
@@ -196,7 +236,7 @@
         growth = jnp.where(mine, jnp.exp(climb), growth)
         ends = jnp.where(mine, jnp.exp(last - climb) * size, ends)
         decay = jnp.where(mine, jnp.exp(last), decay)
-        reach = cols_ref[length - 1 : length, reach_lane + at : reach_lane + at + 1]
+        reach = cols_ref[length - 1 : length, reach_lane + j : reach_lane + j + 1]
         reached = jnp.where(mine, reach, reached)
     inside = inside[0] if len(inside) == 1 else jnp.concatenate(inside, axis=1)
     carried = jnp.dot(queries, state[...].astype(bf16), preferred_element_type=f32)
@@ -208,51 +248,58 @@
 
     @pl.when(step == pl.num_programs(0) - 1)
     def _():
-        here = slice(first_head * head, first_head * head + channels)
-        for ref in earlier:
-            final_ref[:, : first_head * head] = ref[...]
-        final_ref[:width_state, here] = state[...].astype(bf16)
+        final_ref[:width_state, :] = state[...].astype(bf16)
         place = lax.broadcasted_iota(jnp.int32, (16, channels), 0)
         first = reached.astype(bf16).astype(f32)
         second = (reached - first).astype(bf16).astype(f32)
         third = reached - first - second
         parts = jnp.where(place == 0, first, jnp.where(place == 1, second, third))
-        final_ref[width_state:, here] = parts.astype(bf16)
-
-
-def scan(z, tokens, edge, slots, middle, found, taps, skip, earlier, first_head, head, experts, depth, width, length):
+        final_ref[width_state:, :] = parts.astype(bf16)
+
+
+def scan(z, tokens, edge, slots, distances, middle, part, found, taps, skip, head, experts, depth, width, length):
     maps_all, cols, rows = found
     count, channels = tokens.shape[0], taps.shape[1]
     width_state = maps_all.shape[1] // 2
-    flat = list(slots) + [part for pair in middle for part in pair]
+    far_distances = tuple(range(2, 2 + len(middle)))
+    flat = [array for pair in middle for array in pair]
     block = lambda *shape: pl.BlockSpec(shape, lambda b, _: (b, 0))
-    final_shape = (width_state + 16, first_head * head + channels)
-    return pl.pallas_call(
-        functools.partial(
-            scan_kernel, first_head, head, experts, depth, width, len(slots), len(middle)
-        ),
+    depth_rows = width // depth
+
+    def columns_of(distance):
+        return pl.BlockSpec(
+            (length, depth_rows), lambda b, at: (b, lax.rem(at[0] - distance + depth, depth))
+        )
+
+    final_shape = (width_state + 16, channels)
+    return pl.pallas_call(
+        functools.partial(scan_kernel, head, experts, depth, width, distances, far_distances),
         grid_spec=pltpu.PrefetchScalarGridSpec(
             num_scalar_prefetch=1,
             grid=(count // length,),
-            in_specs=[block(length, tokens.shape[1]), vmem(*edge.shape)]
-            + [vmem(*part.shape) for part in flat]
+            in_specs=[pl.BlockSpec(memory_space=pl.ANY)] * (len(slots) + len(flat))
+            + [columns_of(distance) for distance in far_distances]
             + [
+                pl.BlockSpec((length, extra), lambda b, _: (b, width // extra)),
+                vmem(*edge.shape),
+                block(length, part.shape[1]),
                 block(length, maps_all.shape[1]),
                 block(length, 128),
                 pl.BlockSpec((rows.shape[0], length), lambda b, _: (0, b)),
                 vmem(*taps.shape),
                 vmem(*skip.shape),
-            ]
-            + [vmem(*part.shape) for part in earlier],
+            ],
             out_specs=[
                 block(length, channels),
                 block(length, channels),
                 pl.BlockSpec(final_shape, lambda b, _: (0, 0)),
             ],
             scratch_shapes=[
-                pltpu.VMEM((experts, width, 2 * channels), bf16),
+                pltpu.VMEM((len(slots),) + slots[0].shape, bf16),
+                pltpu.VMEM((len(middle),) + slots[0].shape, bf16),
                 pltpu.VMEM((8 + length, channels), f32),
                 pltpu.VMEM((width_state, channels), f32),
+                pltpu.SemaphoreType.DMA((len(slots) + len(middle),)),
             ],
         ),
         out_shape=[
@@ -260,9 +307,9 @@
             jax.ShapeDtypeStruct((count, channels), bf16),
             jax.ShapeDtypeStruct(final_shape, bf16),
         ],
-        compiler_params=params(48),
+        compiler_params=params(40),
         name="scan",
-    )(z, tokens, edge, *flat, maps_all, cols, rows, taps, skip, *earlier)
+    )(z, *slots, *flat, *[tokens] * len(far_distances), tokens, edge, part, maps_all, cols, rows, taps, skip)
 
 
 def norm_kernel(chunks, before, head, heads, pos_ref, maps_ref, cols_ref, gain_ref, *refs):
@@ -294,8 +341,12 @@
     gated = (join(ys) + carried) * (gate / (1.0 + jnp.exp(-gate)))
     row = lax.broadcasted_iota(jnp.int32, (channels, channels), 0) // head
     col = lax.broadcasted_iota(jnp.int32, (channels, channels), 1) // head
-    same = (row == col).astype(f32)
-    square = jnp.dot(gated * gated, same, precision=highest, preferred_element_type=f32) * (1.0 / head)
+    same = (row == col).astype(bf16)
+    squares = gated * gated
+    first = squares.astype(bf16)
+    second = (squares - first.astype(f32)).astype(bf16)
+    square = jnp.dot(first, same, preferred_element_type=f32) + jnp.dot(second, same, preferred_element_type=f32)
+    square = square * (1.0 / head)
     normed = (gated * lax.rsqrt(square + 1e-05) * gain_ref[...]).astype(bf16)
 
     @pl.when(step < steps // 2)
@@ -573,17 +624,20 @@
     other_part = swap(part)
     plane = lay(core_at, [part, other_part])
     edge = shift(plane[count - halo :], lambda z, k, e: (z + 1, k, e) if z + 1 < depth else None)
-    found = maps(plane, w_maps, bias_lanes, rate_lanes, heads, w_bc.shape[1], length)
     ids = lax.dynamic_slice(plane, (core * groups * rows, width), (groups * rows, extra))
+    slots, distances = [shard, *near], (0, 1, depth - 1)
+    part, *found = ahead(
+        z_at, plane, w_maps, bias_lanes, rate_lanes, slots, distances, experts, depth, w_bc.shape[1], length
+    )
     out_shard, above, _ = phase((out_shard, above, other_part))
     out_shard_other, above_other = swap(out_shard), swap(above)
-    far, plane, edge, found, ids, out_shard, above, out_shard_other, above_other = phase(
-        (far, plane, edge, found, ids, out_shard, above, out_shard_other, above_other)
+    far, plane, edge, found, part, ids, out_shard, above, out_shard_other, above_other = phase(
+        (far, plane, edge, found, part, ids, out_shard, above, out_shard_other, above_other)
     )
 
     y, gate, final = scan(
-        z_at, plane, edge, [shard, *near], far, found, half_taps, half_skip,
-        [], 0, head, experts, depth, width, length,
+        z_at, plane, edge, slots, distances, far, part, found, half_taps, half_skip,
+        head, experts, depth, width, length,
     )
     below = shift(out_shard, lambda z, k, e: ((z + 1) % depth, k, e))
     y, gate, final, below = phase((y, gate, final, below))
@@ -611,8 +665,8 @@
     ups, downs, below_other, blocks[0][0] = phase((ups, downs, below_other, blocks[0][0]))
     late = [jnp.where(z >= s + 2, up, down) for s, (up, down) in enumerate(paired(ups[1:], downs[1:]))]
     blocks.append(send(below, below_other, *[array for part in late for array in (part, swap(part))]))
-    distances = [(0, depth - 1), (1, *range(2, depth - 1))]
-    return add_up(jnp.concatenate([z_at, core_at]), blocks, distances, depth, width)
+    order = [(0, depth - 1), (1, *range(2, depth - 1))]
+    return add_up(jnp.concatenate([z_at, core_at]), blocks, order, depth, width)
 
 
 def solution(mesh):

time: 190 us -> 184 us (0.968)
  starting transfers between devices: 47.4 us -> 44.5 us
    ppermute x34, starting transfers between devices: 47.4 us -> 44.5 us  [shift(): return lax.ppermute(array, both, pairs)]
    unnamed x49 -> x47, local copies, waits for them, and re-layouts: 11.5 us -> 10.9 us
  transfers between devices with their start and end apart: 34 -> 34, of which waited for: 15 -> 15; matrix products, arithmetic and copies ran while one was open for 9% -> 10% of each run, Pallas kernels for 20% -> 20%
where the time goes in v3:
time: 184 us; the launch traced here: 183 us
  waiting for transfers between devices  71.1 us (39%)
  starting transfers between devices  44.5 us (24%)
  Pallas kernels  39.3 us (21%)
  local copies, waits for them, and re-layouts  23.8 us (13%)
  other arithmetic  4.12 us (2%)
    ppermute x34, waiting for transfers between devices, shift(): return lax.ppermute(array, both, pairs)  71.1 us
    ppermute x34, starting transfers between devices, shift(): return lax.ppermute(array, both, pairs)  44.5 us
    pallas_call x1, Pallas kernels, ahead(): pl.pallas_call(functools.partial(ahead_kernel, experts, depth, width, dis...  13.2 us
    unnamed x47, local copies, waits for them, and re-layouts  10.9 us
    pallas_call x1, Pallas kernels, scan(): pl.pallas_call(functools.partial(scan_kernel, head, experts, depth, width...  10.8 us
    concatenate x1, local copies, waits for them, and re-layouts, on_device(): jnp.concatenate([jnp.pad(picked, ((0, dt_lane - heads), (0, 0)))] * (128...  6.7 us
    pallas_call x2, Pallas kernels, project_out(): pl.pallas_call(functools.partial(out_kernel, groups // 2, groups), in_spe...  5.87 us
  transfers between devices with their start and end apart: 34, of which 15 were waited for; matrix products, arithmetic and copies ran while one was open for 10% of the time, Pallas kernels for 20%

profile of v3, /device:TPU:16, one launch (start us, length us, event | category | flops | bytes accessed | tf_op | source)
XLA Modules:
  0.0 183.2 jit_solution(464329962805427432)
XLA Ops:
  0.5 1.5 copy.18
  2.1 0.9 cut.1
  2.9 1.6 collective-permute-start
  4.5 1.8 collective-permute-start.1
  6.3 1.5 collective-permute-start.2
  7.8 1.2 collective-permute-start.3
  9.3 1.2 concatenate.22.refs_0_
  10.6 2.3 %collective-permute-done.1.refs_1_ = bf16[256,512]{1,0:T(8,128)(2,1)S(1)} collective-permute-done((bf16[256,512]{1,0:T(8,128)(2,1)S(1)}, bf16[256,512]{1,0:T(8,128)(2,1)S(1)}, u32[]{:S(2)}, u32[]{:S(2)}) %collective-permute-start.1) | collective-permute-done | bytes 262176 | tf_op jit(solution)/shard_map/ppermute | solution.py:34
  12.9 7.2 %collective-permute-done.2.refs_2_ = bf16[256,512]{1,0:T(8,128)(2,1)S(1)} collective-permute-done((bf16[256,512]{1,0:T(8,128)(2,1)S(1)}, bf16[256,512]{1,0:T(8,128)(2,1)S(1)}, u32[]{:S(2)}, u32[]{:S(2)}) %collective-permute-start.2) | collective-permute-done | bytes 262176 | tf_op jit(solution)/shard_map/ppermute | solution.py:34
  20.1 1.0 collective-permute-done.3.refs_3_
  21.1 1.1 arrange.2
  22.9 1.5 collective-permute-start.8
  24.4 1.4 collective-permute-start.7
  25.8 1.6 collective-permute-start.5
  27.8 1.0 copy.17
  28.8 1.2 constant_dynamic-slice_fusion.2
  30.1 0.9 pad.11
  31.0 6.7 %concatenate.23 = bf16[128,2048]{0,1:T(8,128)(2,1)} concatenate(bf16[16,2048]{0,1:T(8,128)(2,1)} %pad.11, bf16[16,2048]{0,1:T(8,128)(2,1)} %pad.11, bf16[16,2048]{0,1:T(8,128)(2,1)} %pad.11, bf16[16,2048]{0,1:T(8,128)(2,1)} %pad.11, bf16[16,2048]{0,1:T(8,128)(2,1)} %pad.11, bf16[16,2048]{0,1:T(8,128)(2,1)} %pad.11, bf16[16,2048]{0,1:T(8,128)(2,1)} %pad.11, bf16[16,2048]{0,1:T(8,128)(2,1)} %pad.11), dimensions={0} | concatenate | bytes 1048576 | tf_op jit(solution)/shard_map/concatenate | solution.py:605
  38.3 1.0 copy-done.13
  39.3 1.0 copy-done.15
  40.5 4.2 %collective-permute-done.9.refs_3_ = bf16[192,2176]{1,0:T(8,128)(2,1)S(1)} collective-permute-done((bf16[192,2176]{1,0:T(8,128)(2,1)S(1)}, bf16[192,2176]{1,0:T(8,128)(2,1)S(1)}, u32[]{:S(2)}, u32[]{:S(2)}) %collective-permute-start.9) | collective-permute-done | bytes 835616 | tf_op jit(solution)/shard_map/ppermute | solution.py:34
  44.8 0.9 copy-done.7
  46.2 16.4 %collective-permute-done.8.refs_2_ = bf16[192,2176]{1,0:T(8,128)(2,1)S(1)} collective-permute-done((bf16[192,2176]{1,0:T(8,128)(2,1)S(1)}, bf16[192,2176]{1,0:T(8,128)(2,1)S(1)}, u32[]{:S(2)}, u32[]{:S(2)}) %collective-permute-start.8) | collective-permute-done | bytes 835616 | tf_op jit(solution)/shard_map/ppermute | solution.py:34
  62.6 0.9 copy-done.9
  63.5 1.5 collective-permute-start.11
  65.0 0.9 copy-done.11
  65.9 2.8 %pad_maximum_fusion.w_ref = bf16[2048,384]{1,0:T(8,128)(2,1)} fusion(bf16[2048,128]{1,0:T(8,128)(2,1)} %bitcast.21, bf16[2048,256]{1,0:T(8,128)(2,1)} %param.17), kind=kLoop, calls=%fused_computation | loop fusion | flops 3145728 | bytes 3145728 | tf_op jit(solution)/shard_map/concatenate | solution.py:606
  69.3 2.6 %collective-permute-done.11.refs_2_ = bf16[512,256]{1,0:T(8,128)(2,1)S(1)} collective-permute-done((bf16[512,256]{1,0:T(8,128)(2,1)S(1)}, bf16[512,256]{1,0:T(8,128)(2,1)S(1)}, u32[]{:S(2)}, u32[]{:S(2)}) %collective-permute-start.11) | collective-permute-done | bytes 262176 | tf_op jit(solution)/shard_map/ppermute | solution.py:34
  71.9 1.9 %collective-permute-done.10.refs_1_ = bf16[512,256]{1,0:T(8,128)(2,1)S(1)} collective-permute-done((bf16[512,256]{1,0:T(8,128)(2,1)S(1)}, bf16[512,256]{1,0:T(8,128)(2,1)S(1)}, u32[]{:S(2)}, u32[]{:S(2)}) %collective-permute-start.10) | collective-permute-done | bytes 262176 | tf_op jit(solution)/shard_map/ppermute | solution.py:34
  73.8 1.1 arrange.3
  74.9 3.5 %collective-permute-start.13 = (bf16[1024,512]{1,0:T(8,128)(2,1)}, bf16[1024,512]{1,0:T(8,128)(2,1)}, u32[]{:S(2)}, u32[]{:S(2)}) collective-permute-start(bf16[1024,512]{1,0:T(8,128)(2,1)} %collective-permute-done.5.refs_1_), channel_id=1, source_target_pairs={{8,16},{9,17},{10,18},{11,19},{12,20},{13,21},{14,22},{15,23},{16,... | collective-permute-start | bytes 3145736 | tf_op jit(solution)/shard_map/ppermute | solution.py:34
  78.4 4.4 %collective-permute-start.14 = (bf16[1024,512]{1,0:T(8,128)(2,1)}, bf16[1024,512]{1,0:T(8,128)(2,1)}, u32[]{:S(2)}, u32[]{:S(2)}) collective-permute-start(bf16[1024,512]{1,0:T(8,128)(2,1)} %collective-permute-done.6.refs_2_), channel_id=1, source_target_pairs={{8,0},{9,1},{10,2},{11,3},{12,4},{13,5},{14,6},{15,7},{16,8},{17,9... | collective-permute-start | bytes 3145736 | tf_op jit(solution)/shard_map/ppermute | solution.py:34
  82.8 1.7 copy-done.5
  85.0 1.9 %copy-done.6 = bf16[768,2176]{1,0:T(8,128)(2,1)S(1)} copy-done((bf16[768,2176]{1,0:T(8,128)(2,1)S(1)}, bf16[768,2176]{1,0:T(8,128)(2,1)}, u32[]{:S(2)}) %copy-start.6) | copy-done | bytes 3342360
  86.9 1.0 lay.3.x_ref.refs_5_.refs_6_
  87.9 1.9 %collective-permute-start.16 = (bf16[16,2176]{1,0:T(8,128)(2,1)S(1)}, bf16[16,2176]{1,0:T(8,128)(2,1)S(1)}, u32[]{:S(2)}, u32[]{:S(2)}) collective-permute-start(bf16[16,2176]{1,0:T(8,128)(2,1)S(1)} %slice.4), channel_id=1, source_target_pairs={{0,8},{1,9},{2,10},{3,11},{4,12},{5,13},{6,14},{7,15},{8,16},{9,17... | collective-permute-start | bytes 208904 | tf_op jit(solution)/shard_map/ppermute | solution.py:34
  89.8 0.8 copy-done.1
  90.6 13.2 %ahead.1 = (f32[1536,512]{1,0:T(8,128)S(1)}, bf16[1536,256]{1,0:T(8,128)(2,1)S(1)}, f32[1536,128]{1,0:T(8,128)S(1)}, f32[32,1536]{1,0:T(8,128)S(1)}) custom-call(s32[1]{0:T(128)} %bitcast.pos_ref, bf16[1536,2176]{1,0:T(8,128)(2,1)} %copy-done.1, bf16[2048,384]{1,0:T(8,128)(2,1)S(1)} %copy-done.2, f32[1,128]{1,0:T(1,128)S(1)} %bitcast.20, ...), custom_call_target="tpu_custom_call" | custom-call | tf_op jit(solution)/shard_map/ahead/pallas_call | solution.py:122
  103.8 0.9 constant_dynamic-slice_fusion.ids_ref
  104.9 0.8 collective-permute-start.19
  105.6 10.8 %scan.1 = (f32[1536,256]{1,0:T(8,128)S(1)}, bf16[1536,256]{1,0:T(8,128)(2,1)S(1)}, bf16[144,256]{1,0:T(8,128)(2,1)S(1)}) custom-call(s32[1]{0:T(128)} %bitcast.pos_ref, bf16[1024,512]{1,0:T(8,128)(2,1)} %bitcast.5.refs_0_, bf16[1024,512]{1,0:T(8,128)(2,1)} %collective-permute-done.5.refs_1_, bf16[1024,512]{1,0:T(8,128)(2,1)} %collective-permute-done.6.refs_2_, ...), custom_call_target="tpu_custom_call" | custom-call | tf_op jit(solution)/shard_map/scan/pallas_call | solution.py:275
  116.5 2.6 %collective-permute-done.19.refs_0_ = bf16[1024,256]{1,0:T(8,128)(2,1)S(1)} collective-permute-done((bf16[1024,256]{1,0:T(8,128)(2,1)}, bf16[1024,256]{1,0:T(8,128)(2,1)S(1)}, u32[]{:S(2)}, u32[]{:S(2)}) %collective-permute-start.19) | collective-permute-done | bytes 524320 | tf_op jit(solution)/shard_map/ppermute | solution.py:34
  119.1 3.5 %collective-permute-start.22 = (bf16[144,256]{1,0:T(8,128)(2,1)S(1)}, bf16[144,256]{1,0:T(8,128)(2,1)S(1)}, u32[]{:S(2)}, u32[]{:S(2)}) collective-permute-start(bf16[144,256]{1,0:T(8,128)(2,1)S(1)} %get-tuple-element.162), channel_id=1, source_target_pairs={{0,8},{1,9},{2,10},{3,11},{4,12},{5,13},{6,14},{7,15},{8,16},{9,17... | collective-permute-start | bytes 221192 | tf_op jit(solution)/shard_map/ppermute | solution.py:34
  122.7 1.3 collective-permute-start.23
  124.0 0.7 collective-permute-start.24
  124.6 3.4 %collective-permute-start.21 = (bf16[1024,256]{1,0:T(8,128)(2,1)}, bf16[1024,256]{1,0:T(8,128)(2,1)S(1)}, u32[]{:S(2)}, u32[]{:S(2)}) collective-permute-start(bf16[1024,256]{1,0:T(8,128)(2,1)} %bitcast.7.refs_2_), channel_id=1, source_target_pairs={{8,0},{9,1},{10,2},{11,3},{12,4},{13,5},{14,6},{15,7},{16,8},{17,9... | collective-permute-start | bytes 1572872 | tf_op jit(solution)/shard_map/ppermute | solution.py:34
  128.0 2.1 %collective-permute-start.20 = (bf16[1024,256]{1,0:T(8,128)(2,1)S(1)}, bf16[1024,256]{1,0:T(8,128)(2,1)}, u32[]{:S(2)}, u32[]{:S(2)}) collective-permute-start(bf16[1024,256]{1,0:T(8,128)(2,1)S(1)} %collective-permute-done.19.refs_0_), channel_id=1, source_target_pairs={{8,16},{9,17},{10,18},{11,19},{12,20},{13,21},{14,22},{15,23},{16,... | collective-permute-start | bytes 1572872 | tf_op jit(solution)/shard_map/ppermute | solution.py:34
  130.2 3.1 %norm.1 = (bf16[768,256]{1,0:T(8,128)(2,1)S(1)}, bf16[768,256]{1,0:T(8,128)(2,1)S(1)}) custom-call(s32[1]{0:T(128)} %bitcast.1.pos_ref, bf16[1536,256]{1,0:T(8,128)(2,1)S(1)} %get-tuple-element.148.refs_9_.maps_ref, f32[1536,128]{1,0:T(8,128)S(1)} %get-tuple-element.149.refs_10_.cols_ref, f32[1,256]{1,0:T(1,128)S(1)} %bitcast.18, ...), custom_call_target="tpu_custom_call" | custom-call | tf_op jit(solution)/shard_map/norm/pallas_call | solution.py:368
  133.9 1.9 %collective-permute-done.26.other_ref = bf16[768,256]{1,0:T(8,128)(2,1)S(1)} collective-permute-done((bf16[768,256]{1,0:T(8,128)(2,1)S(1)}, bf16[768,256]{1,0:T(8,128)(2,1)S(1)}, u32[]{:S(2)}, u32[]{:S(2)}) %collective-permute-start.26) | collective-permute-done | bytes 393248 | tf_op jit(solution)/shard_map/ppermute | solution.py:34
  135.8 3.4 %project_out.2 = (bf16[192,1024]{1,0:T(8,128)(2,1)S(1)}, bf16[192,1024]{1,0:T(8,128)(2,1)S(1)}, bf16[192,1024]{1,0:T(8,128)(2,1)S(1)}, bf16[192,1024]{1,0:T(8,128)(2,1)S(1)}) custom-call(s32[2]{0:T(128)S(1)} %pad_add_fusion.1.pos_ref, bf16[768,128]{1,0:T(8,128)(2,1)S(1)} %constant_dynamic-slice_fusion.ids_ref, ...), custom_call_target="tpu_custom_call" | custom-call | tf_op jit(solution)/shard_map/project_out/pallas_call | solution.py:409
  139.2 3.6 %collective-permute-done.20 = bf16[1024,256]{1,0:T(8,128)(2,1)} collective-permute-done((bf16[1024,256]{1,0:T(8,128)(2,1)S(1)}, bf16[1024,256]{1,0:T(8,128)(2,1)}, u32[]{:S(2)}, u32[]{:S(2)}) %collective-permute-start.20) | collective-permute-done | bytes 524320 | tf_op jit(solution)/shard_map/ppermute | solution.py:34
  142.8 1.1 broadcast_select_fusion.refs_2_
  144.0 0.9 collective-permute-start.27
  144.9 1.5 collective-permute-start.28
  146.4 1.2 collective-permute-start.29
  147.6 2.4 %project_out.3 = (bf16[192,1024]{1,0:T(8,128)(2,1)S(1)}, bf16[192,1024]{1,0:T(8,128)(2,1)S(1)}, bf16[192,1024]{1,0:T(8,128)(2,1)S(1)}, bf16[192,1024]{1,0:T(8,128)(2,1)S(1)}) custom-call(s32[2]{0:T(128)S(1)} %pad_add_fusion.1.pos_ref, bf16[768,128]{1,0:T(8,128)(2,1)S(1)} %constant_dynamic-slice_fusion.ids_ref, ...), custom_call_target="tpu_custom_call" | custom-call | tf_op jit(solution)/shard_map/project_out/pallas_call | solution.py:409
  150.1 0.9 collective-permute-start.31
  150.9 1.5 collective-permute-start.32
  152.5 3.6 %collective-permute-done.27.refs_1_ = bf16[192,1024]{1,0:T(8,128)(2,1)S(1)} collective-permute-done((bf16[192,1024]{1,0:T(8,128)(2,1)S(1)}, bf16[192,1024]{1,0:T(8,128)(2,1)S(1)}, u32[]{:S(2)}, u32[]{:S(2)}) %collective-permute-start.27) | collective-permute-done | bytes 393248 | tf_op jit(solution)/shard_map/ppermute | solution.py:34
  156.0 1.8 collective-permute-start.33
  157.9 7.4 %collective-permute-done.28.refs_2_ = bf16[192,1024]{1,0:T(8,128)(2,1)S(1)} collective-permute-done((bf16[192,1024]{1,0:T(8,128)(2,1)S(1)}, bf16[192,1024]{1,0:T(8,128)(2,1)S(1)}, u32[]{:S(2)}, u32[]{:S(2)}) %collective-permute-start.28) | collective-permute-done | bytes 393248 | tf_op jit(solution)/shard_map/ppermute | solution.py:34
  165.3 7.6 %collective-permute-done.31.refs_5_ = bf16[192,1024]{1,0:T(8,128)(2,1)S(1)} collective-permute-done((bf16[192,1024]{1,0:T(8,128)(2,1)S(1)}, bf16[192,1024]{1,0:T(8,128)(2,1)S(1)}, u32[]{:S(2)}, u32[]{:S(2)}) %collective-permute-start.31) | collective-permute-done | bytes 393248 | tf_op jit(solution)/shard_map/ppermute | solution.py:34
  172.9 8.5 %collective-permute-done.32.refs_6_ = bf16[192,1024]{1,0:T(8,128)(2,1)S(1)} collective-permute-done((bf16[192,1024]{1,0:T(8,128)(2,1)S(1)}, bf16[192,1024]{1,0:T(8,128)(2,1)S(1)}, u32[]{:S(2)}, u32[]{:S(2)}) %collective-permute-start.32) | collective-permute-done | bytes 393248 | tf_op jit(solution)/shard_map/ppermute | solution.py:34
  181.4 1.8 add_up.1
  (89 shorter events, 5.1 us)
Async XLA Ops:
  0.0 40.5 %copy-start = (f32[4,512]{1,0:T(4,128)S(1)}, f32[4,512]{1,0:T(4,128)}, u32[]{:S(2)}) copy-start(f32[4,512]{1,0:T(4,128)} %param.23) | copy-start | bytes 24580
  0.0 9.0 %copy-start.17 = (s32[192,1]{0,1:T(1,128)S(1)}, s32[192,1]{0,1:T(1,128)}, u32[]{:S(2)}) copy-start(s32[192,1]{0,1:T(1,128)} %param.13) | copy-start | bytes 2308
  0.0 9.2 %copy-start.18 = (bf16[192]{0:T(256)(128)(2,1)S(1)}, bf16[192]{0:T(256)(128)(2,1)}, u32[]{:S(2)}) copy-start(bf16[192]{0:T(256)(128)(2,1)} %param.14) | copy-start | bytes 1156
  0.0 21.1 %collective-permute-start.4 = (bf16[1024,256]{1,0:T(8,128)(2,1)}, bf16[1024,256]{1,0:T(8,128)(2,1)S(1)}, u32[]{:S(2)}, u32[]{:S(2)}) collective-permute-start(bf16[1024,256]{1,0:T(8,128)(2,1)} %bitcast.16), channel_id=1, source_target_pairs={{0,24},{1,25},{2,26},{3,27},{4,28},{5,29},{6,30},{7,31},{8,0},{9,1... | collective-permute-start | bytes 1572872 | tf_op jit(solution)/shard_map/ppermute | solution.py:34
  0.5 27.3 %copy-start.16 = (bf16[32,2048]{1,0:T(8,128)(2,1)S(1)}, bf16[32,2048]{1,0:T(8,128)(2,1)}, u32[]{:S(2)}) copy-start(bf16[32,2048]{1,0:T(8,128)(2,1)} %param.18) | copy-start | bytes 393220
  2.9 7.7 %collective-permute-start = (bf16[256,512]{1,0:T(8,128)(2,1)}, bf16[256,512]{1,0:T(8,128)(2,1)S(1)}, u32[]{:S(2)}, u32[]{:S(2)}) collective-permute-start(bf16[256,512]{1,0:T(8,128)(2,1)} %get-tuple-element.95), channel_id=1, source_target_pairs={{0,0},{1,4},{2,2},{3,6},{4,1},{5,5},{6,3},{7,7},{8,8},{9,12},{10,1... | collective-permute-start | bytes 786440 | tf_op jit(solution)/shard_map/ppermute | solution.py:34
  4.5 8.4 %collective-permute-start.1 = (bf16[256,512]{1,0:T(8,128)(2,1)S(1)}, bf16[256,512]{1,0:T(8,128)(2,1)S(1)}, u32[]{:S(2)}, u32[]{:S(2)}) collective-permute-start(bf16[256,512]{1,0:T(8,128)(2,1)S(1)} %get-tuple-element.96), channel_id=1, source_target_pairs={{0,1},{1,5},{2,3},{3,7},{4,0},{5,4},{6,2},{7,6},{8,9},{9,13},{10,1... | collective-permute-start | bytes 786440 | tf_op jit(solution)/shard_map/ppermute | solution.py:34
  6.3 13.8 %collective-permute-start.2 = (bf16[256,512]{1,0:T(8,128)(2,1)S(1)}, bf16[256,512]{1,0:T(8,128)(2,1)S(1)}, u32[]{:S(2)}, u32[]{:S(2)}) collective-permute-start(bf16[256,512]{1,0:T(8,128)(2,1)S(1)} %get-tuple-element.97), channel_id=1, source_target_pairs={{0,2},{1,6},{2,0},{3,4},{4,3},{5,7},{6,1},{7,5},{8,10},{9,14},{10,... | collective-permute-start | bytes 786440 | tf_op jit(solution)/shard_map/ppermute | solution.py:34
  7.8 13.3 %collective-permute-start.3 = (bf16[256,512]{1,0:T(8,128)(2,1)S(1)}, bf16[256,512]{1,0:T(8,128)(2,1)S(1)}, u32[]{:S(2)}, u32[]{:S(2)}) collective-permute-start(bf16[256,512]{1,0:T(8,128)(2,1)S(1)} %get-tuple-element.98), channel_id=1, source_target_pairs={{0,3},{1,7},{2,1},{3,5},{4,2},{5,6},{6,0},{7,4},{8,11},{9,15},{10,... | collective-permute-start | bytes 786440 | tf_op jit(solution)/shard_map/ppermute | solution.py:34
  10.6 27.1 %copy-start.3 = (bf16[192,2176]{1,0:T(8,128)(2,1)}, bf16[192,2176]{1,0:T(8,128)(2,1)S(1)}, u32[]{:S(2)}) copy-start(bf16[192,2176]{1,0:T(8,128)(2,1)S(1)} %concatenate.22.refs_0_) | copy-start | bytes 2506756
  21.1 1.2 copy-start.14
  22.3 22.5 %collective-permute-start.9 = (bf16[192,2176]{1,0:T(8,128)(2,1)S(1)}, bf16[192,2176]{1,0:T(8,128)(2,1)S(1)}, u32[]{:S(2)}, u32[]{:S(2)}) collective-permute-start(bf16[192,2176]{1,0:T(8,128)(2,1)S(1)} %concatenate.22.refs_0_), channel_id=1, source_target_pairs={{0,3},{1,2},{2,1},{3,0},{4,7},{5,6},{6,5},{7,4},{8,11},{9,10},{10,... | collective-permute-start | bytes 2506760 | tf_op jit(solution)/shard_map/ppermute | solution.py:34
  22.9 39.7 %collective-permute-start.8 = (bf16[192,2176]{1,0:T(8,128)(2,1)S(1)}, bf16[192,2176]{1,0:T(8,128)(2,1)S(1)}, u32[]{:S(2)}, u32[]{:S(2)}) collective-permute-start(bf16[192,2176]{1,0:T(8,128)(2,1)S(1)} %concatenate.22.refs_0_), channel_id=1, source_target_pairs={{0,2},{1,3},{2,0},{3,1},{4,6},{5,7},{6,4},{7,5},{8,10},{9,11},{10,... | collective-permute-start | bytes 2506760 | tf_op jit(solution)/shard_map/ppermute | solution.py:34
  24.4 40.6 %collective-permute-start.7 = (bf16[192,2176]{1,0:T(8,128)(2,1)S(1)}, bf16[192,2176]{1,0:T(8,128)(2,1)S(1)}, u32[]{:S(2)}, u32[]{:S(2)}) collective-permute-start(bf16[192,2176]{1,0:T(8,128)(2,1)S(1)} %concatenate.22.refs_0_), channel_id=1, source_target_pairs={{0,1},{1,0},{2,3},{3,2},{4,5},{5,4},{6,7},{7,6},{8,9},{9,8},{10,11... | collective-permute-start | bytes 2506760 | tf_op jit(solution)/shard_map/ppermute | solution.py:34
  25.8 49.1 %collective-permute-start.5 = (bf16[1024,512]{1,0:T(8,128)(2,1)}, bf16[1024,512]{1,0:T(8,128)(2,1)}, u32[]{:S(2)}, u32[]{:S(2)}) collective-permute-start(bf16[1024,512]{1,0:T(8,128)(2,1)} %bitcast.5.refs_0_), channel_id=1, source_target_pairs={{0,8},{1,9},{2,10},{3,11},{4,12},{5,13},{6,14},{7,15},{8,16},{9,17... | collective-permute-start | bytes 3145736 | tf_op jit(solution)/shard_map/ppermute | solution.py:34
  27.4 47.5 %collective-permute-start.6 = (bf16[1024,512]{1,0:T(8,128)(2,1)}, bf16[1024,512]{1,0:T(8,128)(2,1)}, u32[]{:S(2)}, u32[]{:S(2)}) collective-permute-start(bf16[1024,512]{1,0:T(8,128)(2,1)} %bitcast.5.refs_0_), channel_id=1, source_target_pairs={{0,24},{1,25},{2,26},{3,27},{4,28},{5,29},{6,30},{7,31},{8,0},{9,1... | collective-permute-start | bytes 3145736 | tf_op jit(solution)/shard_map/ppermute | solution.py:34
  30.1 7.6 %copy-start.20 = (f32[8]{0:T(128)S(1)}, f32[8]{0:T(128)}, u32[]{:S(2)}) copy-start(f32[8]{0:T(128)} %param.21) | copy-start | bytes 100
  30.1 7.9 %copy-start.21 = (f32[8]{0:T(128)S(1)}, f32[8]{0:T(128)}, u32[]{:S(2)}) copy-start(f32[8]{0:T(128)} %param.19) | copy-start | bytes 100
  30.1 8.0 %copy-start.22 = (f32[8]{0:T(128)S(1)}, f32[8]{0:T(128)}, u32[]{:S(2)}) copy-start(f32[8]{0:T(128)} %param.20) | copy-start | bytes 100
  31.0 9.5 %copy-start.19 = (f32[512]{0:T(512)S(1)}, f32[512]{0:T(512)}, u32[]{:S(2)}) copy-start(f32[512]{0:T(512)} %param.22) | copy-start | bytes 6148
  38.3 1.0 copy-start.13
  39.3 1.0 copy-start.15
  40.4 28.3 %copy-start.4 = (bf16[192,2176]{1,0:T(8,128)(2,1)S(1)}, bf16[192,2176]{1,0:T(8,128)(2,1)}, u32[]{:S(2)}) copy-start(bf16[192,2176]{1,0:T(8,128)(2,1)} %copy-done.3) | copy-start | bytes 2506756
  44.8 0.9 copy-start.7
  45.7 23.0 %copy-start.8 = (bf16[192,2176]{1,0:T(8,128)(2,1)S(1)}, bf16[192,2176]{1,0:T(8,128)(2,1)}, u32[]{:S(2)}) copy-start(bf16[192,2176]{1,0:T(8,128)(2,1)} %copy-done.7) | copy-start | bytes 2506756
  45.7 23.6 %collective-permute-start.12 = (bf16[512,256]{1,0:T(8,128)(2,1)S(1)}, bf16[512,256]{1,0:T(8,128)(2,1)S(1)}, u32[]{:S(2)}, u32[]{:S(2)}) collective-permute-start(bf16[512,256]{1,0:T(8,128)(2,1)S(1)} %get-tuple-element.118), channel_id=1, source_target_pairs={{0,3},{1,2},{2,1},{3,0},{4,7},{5,6},{6,5},{7,4},{8,11},{9,10},{10,... | collective-permute-start | bytes 786440 | tf_op jit(solution)/shard_map/ppermute | solution.py:34
  62.6 0.9 copy-start.9
  63.5 5.2 %copy-start.10 = (bf16[192,2176]{1,0:T(8,128)(2,1)S(1)}, bf16[192,2176]{1,0:T(8,128)(2,1)}, u32[]{:S(2)}) copy-start(bf16[192,2176]{1,0:T(8,128)(2,1)} %copy-done.9) | copy-start | bytes 2506756
  63.5 8.4 %collective-permute-start.11 = (bf16[512,256]{1,0:T(8,128)(2,1)S(1)}, bf16[512,256]{1,0:T(8,128)(2,1)S(1)}, u32[]{:S(2)}, u32[]{:S(2)}) collective-permute-start(bf16[512,256]{1,0:T(8,128)(2,1)S(1)} %get-tuple-element.117), channel_id=1, source_target_pairs={{0,2},{1,3},{2,0},{3,1},{4,6},{5,7},{6,4},{7,5},{8,10},{9,11},{10,... | collective-permute-start | bytes 786440 | tf_op jit(solution)/shard_map/ppermute | solution.py:34
  65.0 0.9 copy-start.11
  65.9 2.9 %copy-start.12 = (bf16[192,2176]{1,0:T(8,128)(2,1)S(1)}, bf16[192,2176]{1,0:T(8,128)(2,1)}, u32[]{:S(2)}) copy-start(bf16[192,2176]{1,0:T(8,128)(2,1)} %copy-done.11) | copy-start | bytes 2506756
  65.9 8.0 %collective-permute-start.10 = (bf16[512,256]{1,0:T(8,128)(2,1)S(1)}, bf16[512,256]{1,0:T(8,128)(2,1)S(1)}, u32[]{:S(2)}, u32[]{:S(2)}) collective-permute-start(bf16[512,256]{1,0:T(8,128)(2,1)S(1)} %get-tuple-element.116), channel_id=1, source_target_pairs={{0,1},{1,0},{2,3},{3,2},{4,5},{5,4},{6,7},{7,6},{8,9},{9,8},{10,11... | collective-permute-start | bytes 786440 | tf_op jit(solution)/shard_map/ppermute | solution.py:34
  74.9 7.9 %collective-permute-start.15 = (bf16[768,2176]{1,0:T(8,128)(2,1)S(1)}, bf16[768,2176]{1,0:T(8,128)(2,1)S(1)}, u32[]{:S(2)}, u32[]{:S(2)}) collective-permute-start(bf16[768,2176]{1,0:T(8,128)(2,1)S(1)} %lay.2.refs_0_), channel_id=1, source_target_pairs={{0,4},{1,5},{2,6},{3,7},{4,0},{5,1},{6,2},{7,3},{8,12},{9,13},{10,... | collective-permute-start | bytes 10027016 | tf_op jit(solution)/shard_map/ppermute | solution.py:34
  74.9 29.9 %collective-permute-start.13 = (bf16[1024,512]{1,0:T(8,128)(2,1)}, bf16[1024,512]{1,0:T(8,128)(2,1)}, u32[]{:S(2)}, u32[]{:S(2)}) collective-permute-start(bf16[1024,512]{1,0:T(8,128)(2,1)} %collective-permute-done.5.refs_1_), channel_id=1, source_target_pairs={{8,16},{9,17},{10,18},{11,19},{12,20},{13,21},{14,22},{15,23},{16,... | collective-permute-start | bytes 3145736 | tf_op jit(solution)/shard_map/ppermute | solution.py:34
  78.4 26.5 %collective-permute-start.14 = (bf16[1024,512]{1,0:T(8,128)(2,1)}, bf16[1024,512]{1,0:T(8,128)(2,1)}, u32[]{:S(2)}, u32[]{:S(2)}) collective-permute-start(bf16[1024,512]{1,0:T(8,128)(2,1)} %collective-permute-done.6.refs_2_), channel_id=1, source_target_pairs={{8,0},{9,1},{10,2},{11,3},{12,4},{13,5},{14,6},{15,7},{16,8},{17,9... | collective-permute-start | bytes 3145736 | tf_op jit(solution)/shard_map/ppermute | solution.py:34
  82.8 1.7 copy-start.5
  84.5 20.4 %collective-permute-start.17 = (bf16[1024,256]{1,0:T(8,128)(2,1)}, bf16[1024,256]{1,0:T(8,128)(2,1)}, u32[]{:S(2)}, u32[]{:S(2)}) collective-permute-start(bf16[1024,256]{1,0:T(8,128)(2,1)} %bitcast.6.refs_0_), channel_id=1, source_target_pairs={{0,4},{1,5},{2,6},{3,7},{4,0},{5,1},{6,2},{7,3},{8,12},{9,13},{10,... | collective-permute-start | bytes 1572872 | tf_op jit(solution)/shard_map/ppermute | solution.py:34
  84.5 20.4 %collective-permute-start.18 = (bf16[1024,256]{1,0:T(8,128)(2,1)}, bf16[1024,256]{1,0:T(8,128)(2,1)}, u32[]{:S(2)}, u32[]{:S(2)}) collective-permute-start(bf16[1024,256]{1,0:T(8,128)(2,1)} %bitcast.7.refs_2_), channel_id=1, source_target_pairs={{0,4},{1,5},{2,6},{3,7},{4,0},{5,1},{6,2},{7,3},{8,12},{9,13},{10,... | collective-permute-start | bytes 1572872 | tf_op jit(solution)/shard_map/ppermute | solution.py:34
  85.0 1.9 %copy-start.6 = (bf16[768,2176]{1,0:T(8,128)(2,1)S(1)}, bf16[768,2176]{1,0:T(8,128)(2,1)}, u32[]{:S(2)}) copy-start(bf16[768,2176]{1,0:T(8,128)(2,1)} %copy-done.5) | copy-start | bytes 10027012
  86.9 3.7 %copy-start.2 = (bf16[2048,384]{1,0:T(8,128)(2,1)S(1)}, bf16[2048,384]{1,0:T(8,128)(2,1)}, u32[]{:S(2)}) copy-start(bf16[2048,384]{1,0:T(8,128)(2,1)} %pad_maximum_fusion.w_ref) | copy-start | bytes 4718596
  87.9 2.7 %copy-start.1 = (bf16[1536,2176]{1,0:T(8,128)(2,1)}, bf16[1536,2176]{1,0:T(8,128)(2,1)S(1)}, u32[]{:S(2)}) copy-start(bf16[1536,2176]{1,0:T(8,128)(2,1)S(1)} %lay.3.x_ref.refs_5_.refs_6_) | copy-start | bytes 20054020
  87.9 17.0 %collective-permute-start.16 = (bf16[16,2176]{1,0:T(8,128)(2,1)S(1)}, bf16[16,2176]{1,0:T(8,128)(2,1)S(1)}, u32[]{:S(2)}, u32[]{:S(2)}) collective-permute-start(bf16[16,2176]{1,0:T(8,128)(2,1)S(1)} %slice.4), channel_id=1, source_target_pairs={{0,8},{1,9},{2,10},{3,11},{4,12},{5,13},{6,14},{7,15},{8,16},{9,17... | collective-permute-start | bytes 208904 | tf_op jit(solution)/shard_map/ppermute | solution.py:34
  104.9 14.2 %collective-permute-start.19 = (bf16[1024,256]{1,0:T(8,128)(2,1)}, bf16[1024,256]{1,0:T(8,128)(2,1)S(1)}, u32[]{:S(2)}, u32[]{:S(2)}) collective-permute-start(bf16[1024,256]{1,0:T(8,128)(2,1)} %bitcast.6.refs_0_), channel_id=1, source_target_pairs={{0,8},{1,9},{2,10},{3,11},{4,12},{5,13},{6,14},{7,15},{8,16},{9,17... | collective-permute-start | bytes 1572872 | tf_op jit(solution)/shard_map/ppermute | solution.py:34
  119.1 11.0 %collective-permute-start.22 = (bf16[144,256]{1,0:T(8,128)(2,1)S(1)}, bf16[144,256]{1,0:T(8,128)(2,1)S(1)}, u32[]{:S(2)}, u32[]{:S(2)}) collective-permute-start(bf16[144,256]{1,0:T(8,128)(2,1)S(1)} %get-tuple-element.162), channel_id=1, source_target_pairs={{0,8},{1,9},{2,10},{3,11},{4,12},{5,13},{6,14},{7,15},{8,16},{9,17... | collective-permute-start | bytes 221192 | tf_op jit(solution)/shard_map/ppermute | solution.py:34
  122.7 7.5 %collective-permute-start.23 = (bf16[144,256]{1,0:T(8,128)(2,1)S(1)}, bf16[144,256]{1,0:T(8,128)(2,1)S(1)}, u32[]{:S(2)}, u32[]{:S(2)}) collective-permute-start(bf16[144,256]{1,0:T(8,128)(2,1)S(1)} %get-tuple-element.162), channel_id=1, source_target_pairs={{0,16},{1,17},{2,18},{3,19},{4,20},{5,21},{6,22},{7,23},{8,24},{9,... | collective-permute-start | bytes 221192 | tf_op jit(solution)/shard_map/ppermute | solution.py:34
  124.0 6.2 %collective-permute-start.24 = (bf16[144,256]{1,0:T(8,128)(2,1)S(1)}, bf16[144,256]{1,0:T(8,128)(2,1)S(1)}, u32[]{:S(2)}, u32[]{:S(2)}) collective-permute-start(bf16[144,256]{1,0:T(8,128)(2,1)S(1)} %get-tuple-element.162), channel_id=1, source_target_pairs={{0,24},{1,25},{2,26},{3,27},{4,28},{5,29},{6,30},{7,31}} | collective-permute-start | bytes 221192 | tf_op jit(solution)/shard_map/ppermute | solution.py:34
  124.6 14.6 %collective-permute-start.21 = (bf16[1024,256]{1,0:T(8,128)(2,1)}, bf16[1024,256]{1,0:T(8,128)(2,1)S(1)}, u32[]{:S(2)}, u32[]{:S(2)}) collective-permute-start(bf16[1024,256]{1,0:T(8,128)(2,1)} %bitcast.7.refs_2_), channel_id=1, source_target_pairs={{8,0},{9,1},{10,2},{11,3},{12,4},{13,5},{14,6},{15,7},{16,8},{17,9... | collective-permute-start | bytes 1572872 | tf_op jit(solution)/shard_map/ppermute | solution.py:34
  128.0 14.8 %collective-permute-start.20 = (bf16[1024,256]{1,0:T(8,128)(2,1)S(1)}, bf16[1024,256]{1,0:T(8,128)(2,1)}, u32[]{:S(2)}, u32[]{:S(2)}) collective-permute-start(bf16[1024,256]{1,0:T(8,128)(2,1)S(1)} %collective-permute-done.19.refs_0_), channel_id=1, source_target_pairs={{8,16},{9,17},{10,18},{11,19},{12,20},{13,21},{14,22},{15,23},{16,... | collective-permute-start | bytes 1572872 | tf_op jit(solution)/shard_map/ppermute | solution.py:34
  133.3 9.6 %collective-permute-start.25 = (bf16[1024,256]{1,0:T(8,128)(2,1)S(1)}, bf16[1024,256]{1,0:T(8,128)(2,1)S(1)}, u32[]{:S(2)}, u32[]{:S(2)}) collective-permute-start(bf16[1024,256]{1,0:T(8,128)(2,1)S(1)} %collective-permute-done.19.refs_0_), channel_id=1, source_target_pairs={{0,4},{1,5},{2,6},{3,7},{4,0},{5,1},{6,2},{7,3},{8,12},{9,13},{10,... | collective-permute-start | bytes 1572872 | tf_op jit(solution)/shard_map/ppermute | solution.py:34
  133.3 2.5 %collective-permute-start.26 = (bf16[768,256]{1,0:T(8,128)(2,1)S(1)}, bf16[768,256]{1,0:T(8,128)(2,1)S(1)}, u32[]{:S(2)}, u32[]{:S(2)}) collective-permute-start(bf16[768,256]{1,0:T(8,128)(2,1)S(1)} %get-tuple-element.167), channel_id=1, source_target_pairs={{0,4},{1,5},{2,6},{3,7},{4,0},{5,1},{6,2},{7,3},{8,12},{9,13},{10,... | collective-permute-start | bytes 1179656 | tf_op jit(solution)/shard_map/ppermute | solution.py:34
  144.0 3.6 %collective-permute-start.30 = (bf16[1024,256]{1,0:T(8,128)(2,1)S(1)}, bf16[1024,256]{1,0:T(8,128)(2,1)S(1)}, u32[]{:S(2)}, u32[]{:S(2)}) collective-permute-start(bf16[1024,256]{1,0:T(8,128)(2,1)S(1)} %broadcast_select_fusion.refs_2_), channel_id=1, source_target_pairs={{0,4},{1,5},{2,6},{3,7},{4,0},{5,1},{6,2},{7,3},{8,12},{9,13},{10,... | collective-permute-start | bytes 1572872 | tf_op jit(solution)/shard_map/ppermute | solution.py:34
  144.0 12.0 %collective-permute-start.27 = (bf16[192,1024]{1,0:T(8,128)(2,1)S(1)}, bf16[192,1024]{1,0:T(8,128)(2,1)S(1)}, u32[]{:S(2)}, u32[]{:S(2)}) collective-permute-start(bf16[192,1024]{1,0:T(8,128)(2,1)S(1)} %get-tuple-element.175), channel_id=1, source_target_pairs={{0,1},{1,0},{2,3},{3,2},{4,5},{5,4},{6,7},{7,6},{8,9},{9,8},{10,11... | collective-permute-start | bytes 1179656 | tf_op jit(solution)/shard_map/ppermute | solution.py:34
  144.9 20.4 %collective-permute-start.28 = (bf16[192,1024]{1,0:T(8,128)(2,1)S(1)}, bf16[192,1024]{1,0:T(8,128)(2,1)S(1)}, u32[]{:S(2)}, u32[]{:S(2)}) collective-permute-start(bf16[192,1024]{1,0:T(8,128)(2,1)S(1)} %get-tuple-element.176), channel_id=1, source_target_pairs={{0,2},{1,3},{2,0},{3,1},{4,6},{5,7},{6,4},{7,5},{8,10},{9,11},{10,... | collective-permute-start | bytes 1179656 | tf_op jit(solution)/shard_map/ppermute | solution.py:34
  146.4 18.9 %collective-permute-start.29 = (bf16[192,1024]{1,0:T(8,128)(2,1)S(1)}, bf16[192,1024]{1,0:T(8,128)(2,1)S(1)}, u32[]{:S(2)}, u32[]{:S(2)}) collective-permute-start(bf16[192,1024]{1,0:T(8,128)(2,1)S(1)} %get-tuple-element.177), channel_id=1, source_target_pairs={{0,3},{1,2},{2,1},{3,0},{4,7},{5,6},{6,5},{7,4},{8,11},{9,10},{10,... | collective-permute-start | bytes 1179656 | tf_op jit(solution)/shard_map/ppermute | solution.py:34
  150.1 22.9 %collective-permute-start.31 = (bf16[192,1024]{1,0:T(8,128)(2,1)S(1)}, bf16[192,1024]{1,0:T(8,128)(2,1)S(1)}, u32[]{:S(2)}, u32[]{:S(2)}) collective-permute-start(bf16[192,1024]{1,0:T(8,128)(2,1)S(1)} %get-tuple-element.182), channel_id=1, source_target_pairs={{0,1},{1,0},{2,3},{3,2},{4,5},{5,4},{6,7},{7,6},{8,9},{9,8},{10,11... | collective-permute-start | bytes 1179656 | tf_op jit(solution)/shard_map/ppermute | solution.py:34
  150.9 30.5 %collective-permute-start.32 = (bf16[192,1024]{1,0:T(8,128)(2,1)S(1)}, bf16[192,1024]{1,0:T(8,128)(2,1)S(1)}, u32[]{:S(2)}, u32[]{:S(2)}) collective-permute-start(bf16[192,1024]{1,0:T(8,128)(2,1)S(1)} %get-tuple-element.183), channel_id=1, source_target_pairs={{0,2},{1,3},{2,0},{3,1},{4,6},{5,7},{6,4},{7,5},{8,10},{9,11},{10,... | collective-permute-start | bytes 1179656 | tf_op jit(solution)/shard_map/ppermute | solution.py:34
  156.0 25.4 %collective-permute-start.33 = (bf16[192,1024]{1,0:T(8,128)(2,1)S(1)}, bf16[192,1024]{1,0:T(8,128)(2,1)S(1)}, u32[]{:S(2)}, u32[]{:S(2)}) collective-permute-start(bf16[192,1024]{1,0:T(8,128)(2,1)S(1)} %get-tuple-element.184), channel_id=1, source_target_pairs={{0,3},{1,2},{2,1},{3,0},{4,7},{5,6},{6,5},{7,4},{8,11},{9,10},{10,... | collective-permute-start | bytes 1179656 | tf_op jit(solution)/shard_map/ppermute | solution.py:34

commit v4 on v3

--- a/solution.py
+++ b/solution.py
@@ -195,8 +195,8 @@
                 x = edge_ref[:, pl.ds(slice_of(z, distance, depth, depth_rows), depth_rows)]
                 total += jnp.dot(x, expert(ref, e), preferred_element_type=f32)
             parts.append(total)
-        before = choose(edge_ref[:, width:], parts).astype(bf16)
-        seen[0:8, :] = before[halo - 8 :, :channels].astype(f32)
+        before = choose(edge_ref[:, width:], parts).astype(bf16).astype(f32)
+        seen[0:8, :] = before[halo - 8 :, :channels]
 
     parts = []
     for e in range(experts):
@@ -664,7 +664,13 @@
     blocks = [send(out_shard, out_shard_other, above, above_other)]
     ups, downs, below_other, blocks[0][0] = phase((ups, downs, below_other, blocks[0][0]))
     late = [jnp.where(z >= s + 2, up, down) for s, (up, down) in enumerate(paired(ups[1:], downs[1:]))]
-    blocks.append(send(below, below_other, *[array for part in late for array in (part, swap(part))]))
+    def swap_in_parts(array):
+        rows_each = array.shape[0] // 2
+        return jnp.concatenate(
+            [swap(array[i * rows_each : (i + 1) * rows_each]) for i in range(2)], axis=0
+        )
+
+    blocks.append(send(below, below_other, *[array for part in late for array in (part, swap_in_parts(part))]))
     order = [(0, depth - 1), (1, *range(2, depth - 1))]
     return add_up(jnp.concatenate([z_at, core_at]), blocks, order, depth, width)
 

time: 184 us -> 184 us (level)
    ppermute x34 -> x35, starting transfers between devices: 44.5 us -> 44.1 us  [shift(): return lax.ppermute(array, both, pairs)]
    ppermute x34 -> x35, waiting for transfers between devices: 71.1 us -> 70.9 us  [shift(): return lax.ppermute(array, both, pairs)]
  transfers between devices with their start and end apart: 34 -> 35, of which waited for: 15 -> 14; matrix products, arithmetic and copies ran while one was open for 10% -> 10% of each run, Pallas kernels for 20% -> 20%
where the time goes in v4:
time: 184 us; the launch traced here: 183 us
  waiting for transfers between devices  70.9 us (39%)
  starting transfers between devices  44.1 us (24%)
  Pallas kernels  39.3 us (21%)
  local copies, waits for them, and re-layouts  23.9 us (13%)
  other arithmetic  4.14 us (2%)
    ppermute x35, waiting for transfers between devices, shift(): return lax.ppermute(array, both, pairs)  70.9 us
    ppermute x35, starting transfers between devices, shift(): return lax.ppermute(array, both, pairs)  44.1 us
    pallas_call x1, Pallas kernels, ahead(): pl.pallas_call(functools.partial(ahead_kernel, experts, depth, width, dis...  13.2 us
    unnamed x47, local copies, waits for them, and re-layouts  10.9 us
    pallas_call x1, Pallas kernels, scan(): pl.pallas_call(functools.partial(scan_kernel, head, experts, depth, width...  10.8 us
    concatenate x1, local copies, waits for them, and re-layouts, on_device(): jnp.concatenate([jnp.pad(picked, ((0, dt_lane - heads), (0, 0)))] * (128...  6.78 us
    pallas_call x2, Pallas kernels, project_out(): pl.pallas_call(functools.partial(out_kernel, groups // 2, groups), in_spe...  5.86 us
  transfers between devices with their start and end apart: 35, of which 14 were waited for; matrix products, arithmetic and copies ran while one was open for 10% of the time, Pallas kernels for 20%

profile of v4, /device:TPU:16, one launch (start us, length us, event | category | flops | bytes accessed | tf_op | source)
XLA Modules:
  0.0 182.8 jit_solution(16733685470735647003)
XLA Ops:
  0.5 1.5 copy.18
  2.1 0.9 cut.1
  2.9 1.6 collective-permute-start
  4.5 1.8 collective-permute-start.1
  6.3 1.5 collective-permute-start.2
  7.8 1.2 collective-permute-start.3
  9.3 1.2 concatenate.25.refs_0_
  10.6 2.3 %collective-permute-done.1.refs_1_ = bf16[256,512]{1,0:T(8,128)(2,1)S(1)} collective-permute-done((bf16[256,512]{1,0:T(8,128)(2,1)S(1)}, bf16[256,512]{1,0:T(8,128)(2,1)S(1)}, u32[]{:S(2)}, u32[]{:S(2)}) %collective-permute-start.1) | collective-permute-done | bytes 262176 | tf_op jit(solution)/shard_map/ppermute | solution.py:34
  12.9 7.2 %collective-permute-done.2.refs_2_ = bf16[256,512]{1,0:T(8,128)(2,1)S(1)} collective-permute-done((bf16[256,512]{1,0:T(8,128)(2,1)S(1)}, bf16[256,512]{1,0:T(8,128)(2,1)S(1)}, u32[]{:S(2)}, u32[]{:S(2)}) %collective-permute-start.2) | collective-permute-done | bytes 262176 | tf_op jit(solution)/shard_map/ppermute | solution.py:34
  20.1 1.0 collective-permute-done.3.refs_3_
  21.1 1.1 arrange.2
  22.3 0.6 collective-permute-start.9
  22.9 1.5 collective-permute-start.8
  24.4 1.4 collective-permute-start.7
  25.8 1.6 collective-permute-start.5
  27.8 1.0 copy.17
  28.8 1.2 constant_dynamic-slice_fusion.2
  30.1 0.9 pad.11
  31.0 6.8 %concatenate.26 = bf16[128,2048]{0,1:T(8,128)(2,1)} concatenate(bf16[16,2048]{0,1:T(8,128)(2,1)} %pad.11, bf16[16,2048]{0,1:T(8,128)(2,1)} %pad.11, bf16[16,2048]{0,1:T(8,128)(2,1)} %pad.11, bf16[16,2048]{0,1:T(8,128)(2,1)} %pad.11, bf16[16,2048]{0,1:T(8,128)(2,1)} %pad.11, bf16[16,2048]{0,1:T(8,128)(2,1)} %pad.11, bf16[16,2048]{0,1:T(8,128)(2,1)} %pad.11, bf16[16,2048]{0,1:T(8,128)(2,1)} %pad.11), dimensions={0} | concatenate | bytes 1048576 | tf_op jit(solution)/shard_map/concatenate | solution.py:605
  38.3 1.0 copy-done.13
  39.4 1.0 copy-done.15
  40.6 4.1 %collective-permute-done.9.refs_3_ = bf16[192,2176]{1,0:T(8,128)(2,1)S(1)} collective-permute-done((bf16[192,2176]{1,0:T(8,128)(2,1)S(1)}, bf16[192,2176]{1,0:T(8,128)(2,1)S(1)}, u32[]{:S(2)}, u32[]{:S(2)}) %collective-permute-start.9) | collective-permute-done | bytes 835616 | tf_op jit(solution)/shard_map/ppermute | solution.py:34
  44.7 0.9 copy-done.7
  46.1 16.4 %collective-permute-done.8.refs_2_ = bf16[192,2176]{1,0:T(8,128)(2,1)S(1)} collective-permute-done((bf16[192,2176]{1,0:T(8,128)(2,1)S(1)}, bf16[192,2176]{1,0:T(8,128)(2,1)S(1)}, u32[]{:S(2)}, u32[]{:S(2)}) %collective-permute-start.8) | collective-permute-done | bytes 835616 | tf_op jit(solution)/shard_map/ppermute | solution.py:34
  62.6 0.9 copy-done.9
  63.5 1.5 collective-permute-start.11
  64.9 0.9 copy-done.11
  65.9 2.8 %pad_maximum_fusion.w_ref = bf16[2048,384]{1,0:T(8,128)(2,1)} fusion(bf16[2048,128]{1,0:T(8,128)(2,1)} %bitcast.21, bf16[2048,256]{1,0:T(8,128)(2,1)} %param.17), kind=kLoop, calls=%fused_computation | loop fusion | flops 3145728 | bytes 3145728 | tf_op jit(solution)/shard_map/concatenate | solution.py:606
  69.2 2.6 %collective-permute-done.11.refs_2_ = bf16[512,256]{1,0:T(8,128)(2,1)S(1)} collective-permute-done((bf16[512,256]{1,0:T(8,128)(2,1)S(1)}, bf16[512,256]{1,0:T(8,128)(2,1)S(1)}, u32[]{:S(2)}, u32[]{:S(2)}) %collective-permute-start.11) | collective-permute-done | bytes 262176 | tf_op jit(solution)/shard_map/ppermute | solution.py:34
  71.9 1.9 %collective-permute-done.10.refs_1_ = bf16[512,256]{1,0:T(8,128)(2,1)S(1)} collective-permute-done((bf16[512,256]{1,0:T(8,128)(2,1)S(1)}, bf16[512,256]{1,0:T(8,128)(2,1)S(1)}, u32[]{:S(2)}, u32[]{:S(2)}) %collective-permute-start.10) | collective-permute-done | bytes 262176 | tf_op jit(solution)/shard_map/ppermute | solution.py:34
  73.8 1.1 arrange.3
  74.9 3.5 %collective-permute-start.13 = (bf16[1024,512]{1,0:T(8,128)(2,1)}, bf16[1024,512]{1,0:T(8,128)(2,1)}, u32[]{:S(2)}, u32[]{:S(2)}) collective-permute-start(bf16[1024,512]{1,0:T(8,128)(2,1)} %collective-permute-done.5.refs_1_), channel_id=1, source_target_pairs={{8,16},{9,17},{10,18},{11,19},{12,20},{13,21},{14,22},{15,23},{16,... | collective-permute-start | bytes 3145736 | tf_op jit(solution)/shard_map/ppermute | solution.py:34
  78.4 4.4 %collective-permute-start.14 = (bf16[1024,512]{1,0:T(8,128)(2,1)}, bf16[1024,512]{1,0:T(8,128)(2,1)}, u32[]{:S(2)}, u32[]{:S(2)}) collective-permute-start(bf16[1024,512]{1,0:T(8,128)(2,1)} %collective-permute-done.6.refs_2_), channel_id=1, source_target_pairs={{8,0},{9,1},{10,2},{11,3},{12,4},{13,5},{14,6},{15,7},{16,8},{17,9... | collective-permute-start | bytes 3145736 | tf_op jit(solution)/shard_map/ppermute | solution.py:34
  82.7 1.7 copy-done.5
  84.9 1.9 %copy-done.6 = bf16[768,2176]{1,0:T(8,128)(2,1)S(1)} copy-done((bf16[768,2176]{1,0:T(8,128)(2,1)S(1)}, bf16[768,2176]{1,0:T(8,128)(2,1)}, u32[]{:S(2)}) %copy-start.6) | copy-done | bytes 3342360
  86.9 1.0 lay.3.x_ref.refs_5_.refs_6_
  87.9 1.9 %collective-permute-start.16 = (bf16[16,2176]{1,0:T(8,128)(2,1)S(1)}, bf16[16,2176]{1,0:T(8,128)(2,1)S(1)}, u32[]{:S(2)}, u32[]{:S(2)}) collective-permute-start(bf16[16,2176]{1,0:T(8,128)(2,1)S(1)} %slice.12), channel_id=1, source_target_pairs={{0,8},{1,9},{2,10},{3,11},{4,12},{5,13},{6,14},{7,15},{8,16},{9,17... | collective-permute-start | bytes 208904 | tf_op jit(solution)/shard_map/ppermute | solution.py:34
  89.8 0.8 copy-done.1
  90.6 13.2 %ahead.1 = (f32[1536,512]{1,0:T(8,128)S(1)}, bf16[1536,256]{1,0:T(8,128)(2,1)S(1)}, f32[1536,128]{1,0:T(8,128)S(1)}, f32[32,1536]{1,0:T(8,128)S(1)}) custom-call(s32[1]{0:T(128)} %bitcast.pos_ref, bf16[1536,2176]{1,0:T(8,128)(2,1)} %copy-done.1, bf16[2048,384]{1,0:T(8,128)(2,1)S(1)} %copy-done.2, f32[1,128]{1,0:T(1,128)S(1)} %bitcast.20, ...), custom_call_target="tpu_custom_call" | custom-call | tf_op jit(solution)/shard_map/ahead/pallas_call | solution.py:122
  103.8 0.9 constant_dynamic-slice_fusion.ids_ref
  104.9 0.8 collective-permute-start.19
  105.6 10.8 %scan.1 = (f32[1536,256]{1,0:T(8,128)S(1)}, bf16[1536,256]{1,0:T(8,128)(2,1)S(1)}, bf16[144,256]{1,0:T(8,128)(2,1)S(1)}) custom-call(s32[1]{0:T(128)} %bitcast.pos_ref, bf16[1024,512]{1,0:T(8,128)(2,1)} %bitcast.5.refs_0_, bf16[1024,512]{1,0:T(8,128)(2,1)} %collective-permute-done.5.refs_1_, bf16[1024,512]{1,0:T(8,128)(2,1)} %collective-permute-done.6.refs_2_, ...), custom_call_target="tpu_custom_call" | custom-call | tf_op jit(solution)/shard_map/scan/pallas_call | solution.py:275
  116.5 2.6 %collective-permute-done.19.refs_0_ = bf16[1024,256]{1,0:T(8,128)(2,1)S(1)} collective-permute-done((bf16[1024,256]{1,0:T(8,128)(2,1)}, bf16[1024,256]{1,0:T(8,128)(2,1)S(1)}, u32[]{:S(2)}, u32[]{:S(2)}) %collective-permute-start.19) | collective-permute-done | bytes 524320 | tf_op jit(solution)/shard_map/ppermute | solution.py:34
  119.1 3.5 %collective-permute-start.22 = (bf16[144,256]{1,0:T(8,128)(2,1)S(1)}, bf16[144,256]{1,0:T(8,128)(2,1)S(1)}, u32[]{:S(2)}, u32[]{:S(2)}) collective-permute-start(bf16[144,256]{1,0:T(8,128)(2,1)S(1)} %get-tuple-element.162), channel_id=1, source_target_pairs={{0,8},{1,9},{2,10},{3,11},{4,12},{5,13},{6,14},{7,15},{8,16},{9,17... | collective-permute-start | bytes 221192 | tf_op jit(solution)/shard_map/ppermute | solution.py:34
  122.6 1.3 collective-permute-start.23
  123.9 0.7 collective-permute-start.24
  124.6 3.4 %collective-permute-start.21 = (bf16[1024,256]{1,0:T(8,128)(2,1)}, bf16[1024,256]{1,0:T(8,128)(2,1)S(1)}, u32[]{:S(2)}, u32[]{:S(2)}) collective-permute-start(bf16[1024,256]{1,0:T(8,128)(2,1)} %bitcast.7.refs_2_), channel_id=1, source_target_pairs={{8,0},{9,1},{10,2},{11,3},{12,4},{13,5},{14,6},{15,7},{16,8},{17,9... | collective-permute-start | bytes 1572872 | tf_op jit(solution)/shard_map/ppermute | solution.py:34
  128.0 2.1 %collective-permute-start.20 = (bf16[1024,256]{1,0:T(8,128)(2,1)S(1)}, bf16[1024,256]{1,0:T(8,128)(2,1)}, u32[]{:S(2)}, u32[]{:S(2)}) collective-permute-start(bf16[1024,256]{1,0:T(8,128)(2,1)S(1)} %collective-permute-done.19.refs_0_), channel_id=1, source_target_pairs={{8,16},{9,17},{10,18},{11,19},{12,20},{13,21},{14,22},{15,23},{16,... | collective-permute-start | bytes 1572872 | tf_op jit(solution)/shard_map/ppermute | solution.py:34
  130.2 3.1 %norm.1 = (bf16[768,256]{1,0:T(8,128)(2,1)S(1)}, bf16[768,256]{1,0:T(8,128)(2,1)S(1)}) custom-call(s32[1]{0:T(128)} %bitcast.1.pos_ref, bf16[1536,256]{1,0:T(8,128)(2,1)S(1)} %get-tuple-element.148.refs_9_.maps_ref, f32[1536,128]{1,0:T(8,128)S(1)} %get-tuple-element.149.refs_10_.cols_ref, f32[1,256]{1,0:T(1,128)S(1)} %bitcast.18, ...), custom_call_target="tpu_custom_call" | custom-call | tf_op jit(solution)/shard_map/norm/pallas_call | solution.py:368
  133.9 1.9 %collective-permute-done.26.other_ref = bf16[768,256]{1,0:T(8,128)(2,1)S(1)} collective-permute-done((bf16[768,256]{1,0:T(8,128)(2,1)S(1)}, bf16[768,256]{1,0:T(8,128)(2,1)S(1)}, u32[]{:S(2)}, u32[]{:S(2)}) %collective-permute-start.26) | collective-permute-done | bytes 393248 | tf_op jit(solution)/shard_map/ppermute | solution.py:34
  135.8 3.4 %project_out.2 = (bf16[192,1024]{1,0:T(8,128)(2,1)S(1)}, bf16[192,1024]{1,0:T(8,128)(2,1)S(1)}, bf16[192,1024]{1,0:T(8,128)(2,1)S(1)}, bf16[192,1024]{1,0:T(8,128)(2,1)S(1)}) custom-call(s32[2]{0:T(128)S(1)} %pad_add_fusion.1.pos_ref, bf16[768,128]{1,0:T(8,128)(2,1)S(1)} %constant_dynamic-slice_fusion.ids_ref, ...), custom_call_target="tpu_custom_call" | custom-call | tf_op jit(solution)/shard_map/project_out/pallas_call | solution.py:409
  139.2 0.9 collective-permute-start.27
  140.1 2.7 %collective-permute-done.20 = bf16[1024,256]{1,0:T(8,128)(2,1)} collective-permute-done((bf16[1024,256]{1,0:T(8,128)(2,1)S(1)}, bf16[1024,256]{1,0:T(8,128)(2,1)}, u32[]{:S(2)}, u32[]{:S(2)}) %collective-permute-start.20) | collective-permute-done | bytes 524320 | tf_op jit(solution)/shard_map/ppermute | solution.py:34
  142.8 1.1 broadcast_select_fusion.refs_2_
  144.6 0.7 collective-permute-start.28
  145.3 1.5 collective-permute-start.29
  146.9 2.4 %project_out.3 = (bf16[192,1024]{1,0:T(8,128)(2,1)S(1)}, bf16[192,1024]{1,0:T(8,128)(2,1)S(1)}, bf16[192,1024]{1,0:T(8,128)(2,1)S(1)}, bf16[192,1024]{1,0:T(8,128)(2,1)S(1)}) custom-call(s32[2]{0:T(128)S(1)} %pad_add_fusion.1.pos_ref, bf16[768,128]{1,0:T(8,128)(2,1)S(1)} %constant_dynamic-slice_fusion.ids_ref, ...), custom_call_target="tpu_custom_call" | custom-call | tf_op jit(solution)/shard_map/project_out/pallas_call | solution.py:409
  149.3 1.3 collective-permute-start.32
  150.6 0.7 collective-permute-start.33
  151.4 1.6 collective-permute-start.34
  153.1 11.9 %collective-permute-done.28.refs_2_ = bf16[192,1024]{1,0:T(8,128)(2,1)S(1)} collective-permute-done((bf16[192,1024]{1,0:T(8,128)(2,1)S(1)}, bf16[192,1024]{1,0:T(8,128)(2,1)S(1)}, u32[]{:S(2)}, u32[]{:S(2)}) %collective-permute-start.28) | collective-permute-done | bytes 393248 | tf_op jit(solution)/shard_map/ppermute | solution.py:34
  165.0 3.2 %collective-permute-done.32.refs_5_ = bf16[192,1024]{1,0:T(8,128)(2,1)S(1)} collective-permute-done((bf16[192,1024]{1,0:T(8,128)(2,1)S(1)}, bf16[192,1024]{1,0:T(8,128)(2,1)S(1)}, u32[]{:S(2)}, u32[]{:S(2)}) %collective-permute-start.32) | collective-permute-done | bytes 393248 | tf_op jit(solution)/shard_map/ppermute | solution.py:34
  168.1 12.8 %collective-permute-done.33.refs_6_ = bf16[192,1024]{1,0:T(8,128)(2,1)S(1)} collective-permute-done((bf16[192,1024]{1,0:T(8,128)(2,1)S(1)}, bf16[192,1024]{1,0:T(8,128)(2,1)S(1)}, u32[]{:S(2)}, u32[]{:S(2)}) %collective-permute-start.33) | collective-permute-done | bytes 393248 | tf_op jit(solution)/shard_map/ppermute | solution.py:34
  180.9 1.8 add_up.1
  (93 shorter events, 5.1 us)
Async XLA Ops:
  0.0 40.6 %copy-start = (f32[4,512]{1,0:T(4,128)S(1)}, f32[4,512]{1,0:T(4,128)}, u32[]{:S(2)}) copy-start(f32[4,512]{1,0:T(4,128)} %param.23) | copy-start | bytes 24580
  0.0 9.0 %copy-start.17 = (s32[192,1]{0,1:T(1,128)S(1)}, s32[192,1]{0,1:T(1,128)}, u32[]{:S(2)}) copy-start(s32[192,1]{0,1:T(1,128)} %param.13) | copy-start | bytes 2308
  0.0 9.2 %copy-start.18 = (bf16[192]{0:T(256)(128)(2,1)S(1)}, bf16[192]{0:T(256)(128)(2,1)}, u32[]{:S(2)}) copy-start(bf16[192]{0:T(256)(128)(2,1)} %param.14) | copy-start | bytes 1156
  0.0 21.1 %collective-permute-start.4 = (bf16[1024,256]{1,0:T(8,128)(2,1)}, bf16[1024,256]{1,0:T(8,128)(2,1)S(1)}, u32[]{:S(2)}, u32[]{:S(2)}) collective-permute-start(bf16[1024,256]{1,0:T(8,128)(2,1)} %bitcast.16), channel_id=1, source_target_pairs={{0,24},{1,25},{2,26},{3,27},{4,28},{5,29},{6,30},{7,31},{8,0},{9,1... | collective-permute-start | bytes 1572872 | tf_op jit(solution)/shard_map/ppermute | solution.py:34
  0.5 27.3 %copy-start.16 = (bf16[32,2048]{1,0:T(8,128)(2,1)S(1)}, bf16[32,2048]{1,0:T(8,128)(2,1)}, u32[]{:S(2)}) copy-start(bf16[32,2048]{1,0:T(8,128)(2,1)} %param.18) | copy-start | bytes 393220
  2.9 7.7 %collective-permute-start = (bf16[256,512]{1,0:T(8,128)(2,1)}, bf16[256,512]{1,0:T(8,128)(2,1)S(1)}, u32[]{:S(2)}, u32[]{:S(2)}) collective-permute-start(bf16[256,512]{1,0:T(8,128)(2,1)} %get-tuple-element.95), channel_id=1, source_target_pairs={{0,0},{1,4},{2,2},{3,6},{4,1},{5,5},{6,3},{7,7},{8,8},{9,12},{10,1... | collective-permute-start | bytes 786440 | tf_op jit(solution)/shard_map/ppermute | solution.py:34
  4.5 8.4 %collective-permute-start.1 = (bf16[256,512]{1,0:T(8,128)(2,1)S(1)}, bf16[256,512]{1,0:T(8,128)(2,1)S(1)}, u32[]{:S(2)}, u32[]{:S(2)}) collective-permute-start(bf16[256,512]{1,0:T(8,128)(2,1)S(1)} %get-tuple-element.96), channel_id=1, source_target_pairs={{0,1},{1,5},{2,3},{3,7},{4,0},{5,4},{6,2},{7,6},{8,9},{9,13},{10,1... | collective-permute-start | bytes 786440 | tf_op jit(solution)/shard_map/ppermute | solution.py:34
  6.3 13.8 %collective-permute-start.2 = (bf16[256,512]{1,0:T(8,128)(2,1)S(1)}, bf16[256,512]{1,0:T(8,128)(2,1)S(1)}, u32[]{:S(2)}, u32[]{:S(2)}) collective-permute-start(bf16[256,512]{1,0:T(8,128)(2,1)S(1)} %get-tuple-element.97), channel_id=1, source_target_pairs={{0,2},{1,6},{2,0},{3,4},{4,3},{5,7},{6,1},{7,5},{8,10},{9,14},{10,... | collective-permute-start | bytes 786440 | tf_op jit(solution)/shard_map/ppermute | solution.py:34
  7.8 13.3 %collective-permute-start.3 = (bf16[256,512]{1,0:T(8,128)(2,1)S(1)}, bf16[256,512]{1,0:T(8,128)(2,1)S(1)}, u32[]{:S(2)}, u32[]{:S(2)}) collective-permute-start(bf16[256,512]{1,0:T(8,128)(2,1)S(1)} %get-tuple-element.98), channel_id=1, source_target_pairs={{0,3},{1,7},{2,1},{3,5},{4,2},{5,6},{6,0},{7,4},{8,11},{9,15},{10,... | collective-permute-start | bytes 786440 | tf_op jit(solution)/shard_map/ppermute | solution.py:34
  10.6 27.2 %copy-start.3 = (bf16[192,2176]{1,0:T(8,128)(2,1)}, bf16[192,2176]{1,0:T(8,128)(2,1)S(1)}, u32[]{:S(2)}) copy-start(bf16[192,2176]{1,0:T(8,128)(2,1)S(1)} %concatenate.25.refs_0_) | copy-start | bytes 2506756
  21.1 1.1 copy-start.14
  22.3 22.5 %collective-permute-start.9 = (bf16[192,2176]{1,0:T(8,128)(2,1)S(1)}, bf16[192,2176]{1,0:T(8,128)(2,1)S(1)}, u32[]{:S(2)}, u32[]{:S(2)}) collective-permute-start(bf16[192,2176]{1,0:T(8,128)(2,1)S(1)} %concatenate.25.refs_0_), channel_id=1, source_target_pairs={{0,3},{1,2},{2,1},{3,0},{4,7},{5,6},{6,5},{7,4},{8,11},{9,10},{10,... | collective-permute-start | bytes 2506760 | tf_op jit(solution)/shard_map/ppermute | solution.py:34
  22.9 39.7 %collective-permute-start.8 = (bf16[192,2176]{1,0:T(8,128)(2,1)S(1)}, bf16[192,2176]{1,0:T(8,128)(2,1)S(1)}, u32[]{:S(2)}, u32[]{:S(2)}) collective-permute-start(bf16[192,2176]{1,0:T(8,128)(2,1)S(1)} %concatenate.25.refs_0_), channel_id=1, source_target_pairs={{0,2},{1,3},{2,0},{3,1},{4,6},{5,7},{6,4},{7,5},{8,10},{9,11},{10,... | collective-permute-start | bytes 2506760 | tf_op jit(solution)/shard_map/ppermute | solution.py:34
  24.4 40.6 %collective-permute-start.7 = (bf16[192,2176]{1,0:T(8,128)(2,1)S(1)}, bf16[192,2176]{1,0:T(8,128)(2,1)S(1)}, u32[]{:S(2)}, u32[]{:S(2)}) collective-permute-start(bf16[192,2176]{1,0:T(8,128)(2,1)S(1)} %concatenate.25.refs_0_), channel_id=1, source_target_pairs={{0,1},{1,0},{2,3},{3,2},{4,5},{5,4},{6,7},{7,6},{8,9},{9,8},{10,11... | collective-permute-start | bytes 2506760 | tf_op jit(solution)/shard_map/ppermute | solution.py:34
  25.8 49.1 %collective-permute-start.5 = (bf16[1024,512]{1,0:T(8,128)(2,1)}, bf16[1024,512]{1,0:T(8,128)(2,1)}, u32[]{:S(2)}, u32[]{:S(2)}) collective-permute-start(bf16[1024,512]{1,0:T(8,128)(2,1)} %bitcast.5.refs_0_), channel_id=1, source_target_pairs={{0,8},{1,9},{2,10},{3,11},{4,12},{5,13},{6,14},{7,15},{8,16},{9,17... | collective-permute-start | bytes 3145736 | tf_op jit(solution)/shard_map/ppermute | solution.py:34
  27.3 47.5 %collective-permute-start.6 = (bf16[1024,512]{1,0:T(8,128)(2,1)}, bf16[1024,512]{1,0:T(8,128)(2,1)}, u32[]{:S(2)}, u32[]{:S(2)}) collective-permute-start(bf16[1024,512]{1,0:T(8,128)(2,1)} %bitcast.5.refs_0_), channel_id=1, source_target_pairs={{0,24},{1,25},{2,26},{3,27},{4,28},{5,29},{6,30},{7,31},{8,0},{9,1... | collective-permute-start | bytes 3145736 | tf_op jit(solution)/shard_map/ppermute | solution.py:34
  30.0 7.7 %copy-start.20 = (f32[8]{0:T(128)S(1)}, f32[8]{0:T(128)}, u32[]{:S(2)}) copy-start(f32[8]{0:T(128)} %param.21) | copy-start | bytes 100
  30.0 8.0 %copy-start.21 = (f32[8]{0:T(128)S(1)}, f32[8]{0:T(128)}, u32[]{:S(2)}) copy-start(f32[8]{0:T(128)} %param.19) | copy-start | bytes 100
  30.1 8.1 %copy-start.22 = (f32[8]{0:T(128)S(1)}, f32[8]{0:T(128)}, u32[]{:S(2)}) copy-start(f32[8]{0:T(128)} %param.20) | copy-start | bytes 100
  31.0 9.5 %copy-start.19 = (f32[512]{0:T(512)S(1)}, f32[512]{0:T(512)}, u32[]{:S(2)}) copy-start(f32[512]{0:T(512)} %param.22) | copy-start | bytes 6148
  38.3 1.0 copy-start.13
  39.4 1.0 copy-start.15
  40.4 28.3 %copy-start.4 = (bf16[192,2176]{1,0:T(8,128)(2,1)S(1)}, bf16[192,2176]{1,0:T(8,128)(2,1)}, u32[]{:S(2)}) copy-start(bf16[192,2176]{1,0:T(8,128)(2,1)} %copy-done.3) | copy-start | bytes 2506756
  44.7 0.9 copy-start.7
  45.6 23.0 %copy-start.8 = (bf16[192,2176]{1,0:T(8,128)(2,1)S(1)}, bf16[192,2176]{1,0:T(8,128)(2,1)}, u32[]{:S(2)}) copy-start(bf16[192,2176]{1,0:T(8,128)(2,1)} %copy-done.7) | copy-start | bytes 2506756
  45.6 23.6 %collective-permute-start.12 = (bf16[512,256]{1,0:T(8,128)(2,1)S(1)}, bf16[512,256]{1,0:T(8,128)(2,1)S(1)}, u32[]{:S(2)}, u32[]{:S(2)}) collective-permute-start(bf16[512,256]{1,0:T(8,128)(2,1)S(1)} %get-tuple-element.118), channel_id=1, source_target_pairs={{0,3},{1,2},{2,1},{3,0},{4,7},{5,6},{6,5},{7,4},{8,11},{9,10},{10,... | collective-permute-start | bytes 786440 | tf_op jit(solution)/shard_map/ppermute | solution.py:34
  62.6 0.9 copy-start.9
  63.5 5.2 %copy-start.10 = (bf16[192,2176]{1,0:T(8,128)(2,1)S(1)}, bf16[192,2176]{1,0:T(8,128)(2,1)}, u32[]{:S(2)}) copy-start(bf16[192,2176]{1,0:T(8,128)(2,1)} %copy-done.9) | copy-start | bytes 2506756
  63.5 8.4 %collective-permute-start.11 = (bf16[512,256]{1,0:T(8,128)(2,1)S(1)}, bf16[512,256]{1,0:T(8,128)(2,1)S(1)}, u32[]{:S(2)}, u32[]{:S(2)}) collective-permute-start(bf16[512,256]{1,0:T(8,128)(2,1)S(1)} %get-tuple-element.117), channel_id=1, source_target_pairs={{0,2},{1,3},{2,0},{3,1},{4,6},{5,7},{6,4},{7,5},{8,10},{9,11},{10,... | collective-permute-start | bytes 786440 | tf_op jit(solution)/shard_map/ppermute | solution.py:34
  64.9 0.9 copy-start.11
  65.8 2.8 %copy-start.12 = (bf16[192,2176]{1,0:T(8,128)(2,1)S(1)}, bf16[192,2176]{1,0:T(8,128)(2,1)}, u32[]{:S(2)}) copy-start(bf16[192,2176]{1,0:T(8,128)(2,1)} %copy-done.11) | copy-start | bytes 2506756
  65.9 8.0 %collective-permute-start.10 = (bf16[512,256]{1,0:T(8,128)(2,1)S(1)}, bf16[512,256]{1,0:T(8,128)(2,1)S(1)}, u32[]{:S(2)}, u32[]{:S(2)}) collective-permute-start(bf16[512,256]{1,0:T(8,128)(2,1)S(1)} %get-tuple-element.116), channel_id=1, source_target_pairs={{0,1},{1,0},{2,3},{3,2},{4,5},{5,4},{6,7},{7,6},{8,9},{9,8},{10,11... | collective-permute-start | bytes 786440 | tf_op jit(solution)/shard_map/ppermute | solution.py:34
  74.9 7.9 %collective-permute-start.15 = (bf16[768,2176]{1,0:T(8,128)(2,1)S(1)}, bf16[768,2176]{1,0:T(8,128)(2,1)S(1)}, u32[]{:S(2)}, u32[]{:S(2)}) collective-permute-start(bf16[768,2176]{1,0:T(8,128)(2,1)S(1)} %lay.2.refs_0_), channel_id=1, source_target_pairs={{0,4},{1,5},{2,6},{3,7},{4,0},{5,1},{6,2},{7,3},{8,12},{9,13},{10,... | collective-permute-start | bytes 10027016 | tf_op jit(solution)/shard_map/ppermute | solution.py:34
  74.9 29.9 %collective-permute-start.13 = (bf16[1024,512]{1,0:T(8,128)(2,1)}, bf16[1024,512]{1,0:T(8,128)(2,1)}, u32[]{:S(2)}, u32[]{:S(2)}) collective-permute-start(bf16[1024,512]{1,0:T(8,128)(2,1)} %collective-permute-done.5.refs_1_), channel_id=1, source_target_pairs={{8,16},{9,17},{10,18},{11,19},{12,20},{13,21},{14,22},{15,23},{16,... | collective-permute-start | bytes 3145736 | tf_op jit(solution)/shard_map/ppermute | solution.py:34
  78.4 26.5 %collective-permute-start.14 = (bf16[1024,512]{1,0:T(8,128)(2,1)}, bf16[1024,512]{1,0:T(8,128)(2,1)}, u32[]{:S(2)}, u32[]{:S(2)}) collective-permute-start(bf16[1024,512]{1,0:T(8,128)(2,1)} %collective-permute-done.6.refs_2_), channel_id=1, source_target_pairs={{8,0},{9,1},{10,2},{11,3},{12,4},{13,5},{14,6},{15,7},{16,8},{17,9... | collective-permute-start | bytes 3145736 | tf_op jit(solution)/shard_map/ppermute | solution.py:34
  82.7 1.7 copy-start.5
  84.4 20.4 %collective-permute-start.17 = (bf16[1024,256]{1,0:T(8,128)(2,1)}, bf16[1024,256]{1,0:T(8,128)(2,1)}, u32[]{:S(2)}, u32[]{:S(2)}) collective-permute-start(bf16[1024,256]{1,0:T(8,128)(2,1)} %bitcast.6.refs_0_), channel_id=1, source_target_pairs={{0,4},{1,5},{2,6},{3,7},{4,0},{5,1},{6,2},{7,3},{8,12},{9,13},{10,... | collective-permute-start | bytes 1572872 | tf_op jit(solution)/shard_map/ppermute | solution.py:34
  84.4 20.4 %collective-permute-start.18 = (bf16[1024,256]{1,0:T(8,128)(2,1)}, bf16[1024,256]{1,0:T(8,128)(2,1)}, u32[]{:S(2)}, u32[]{:S(2)}) collective-permute-start(bf16[1024,256]{1,0:T(8,128)(2,1)} %bitcast.7.refs_2_), channel_id=1, source_target_pairs={{0,4},{1,5},{2,6},{3,7},{4,0},{5,1},{6,2},{7,3},{8,12},{9,13},{10,... | collective-permute-start | bytes 1572872 | tf_op jit(solution)/shard_map/ppermute | solution.py:34
  84.9 1.9 %copy-start.6 = (bf16[768,2176]{1,0:T(8,128)(2,1)S(1)}, bf16[768,2176]{1,0:T(8,128)(2,1)}, u32[]{:S(2)}) copy-start(bf16[768,2176]{1,0:T(8,128)(2,1)} %copy-done.5) | copy-start | bytes 10027012
  86.9 3.7 %copy-start.2 = (bf16[2048,384]{1,0:T(8,128)(2,1)S(1)}, bf16[2048,384]{1,0:T(8,128)(2,1)}, u32[]{:S(2)}) copy-start(bf16[2048,384]{1,0:T(8,128)(2,1)} %pad_maximum_fusion.w_ref) | copy-start | bytes 4718596
  87.8 2.8 %copy-start.1 = (bf16[1536,2176]{1,0:T(8,128)(2,1)}, bf16[1536,2176]{1,0:T(8,128)(2,1)S(1)}, u32[]{:S(2)}) copy-start(bf16[1536,2176]{1,0:T(8,128)(2,1)S(1)} %lay.3.x_ref.refs_5_.refs_6_) | copy-start | bytes 20054020
  87.9 17.0 %collective-permute-start.16 = (bf16[16,2176]{1,0:T(8,128)(2,1)S(1)}, bf16[16,2176]{1,0:T(8,128)(2,1)S(1)}, u32[]{:S(2)}, u32[]{:S(2)}) collective-permute-start(bf16[16,2176]{1,0:T(8,128)(2,1)S(1)} %slice.12), channel_id=1, source_target_pairs={{0,8},{1,9},{2,10},{3,11},{4,12},{5,13},{6,14},{7,15},{8,16},{9,17... | collective-permute-start | bytes 208904 | tf_op jit(solution)/shard_map/ppermute | solution.py:34
  104.9 14.2 %collective-permute-start.19 = (bf16[1024,256]{1,0:T(8,128)(2,1)}, bf16[1024,256]{1,0:T(8,128)(2,1)S(1)}, u32[]{:S(2)}, u32[]{:S(2)}) collective-permute-start(bf16[1024,256]{1,0:T(8,128)(2,1)} %bitcast.6.refs_0_), channel_id=1, source_target_pairs={{0,8},{1,9},{2,10},{3,11},{4,12},{5,13},{6,14},{7,15},{8,16},{9,17... | collective-permute-start | bytes 1572872 | tf_op jit(solution)/shard_map/ppermute | solution.py:34
  119.1 11.0 %collective-permute-start.22 = (bf16[144,256]{1,0:T(8,128)(2,1)S(1)}, bf16[144,256]{1,0:T(8,128)(2,1)S(1)}, u32[]{:S(2)}, u32[]{:S(2)}) collective-permute-start(bf16[144,256]{1,0:T(8,128)(2,1)S(1)} %get-tuple-element.162), channel_id=1, source_target_pairs={{0,8},{1,9},{2,10},{3,11},{4,12},{5,13},{6,14},{7,15},{8,16},{9,17... | collective-permute-start | bytes 221192 | tf_op jit(solution)/shard_map/ppermute | solution.py:34
  122.6 7.5 %collective-permute-start.23 = (bf16[144,256]{1,0:T(8,128)(2,1)S(1)}, bf16[144,256]{1,0:T(8,128)(2,1)S(1)}, u32[]{:S(2)}, u32[]{:S(2)}) collective-permute-start(bf16[144,256]{1,0:T(8,128)(2,1)S(1)} %get-tuple-element.162), channel_id=1, source_target_pairs={{0,16},{1,17},{2,18},{3,19},{4,20},{5,21},{6,22},{7,23},{8,24},{9,... | collective-permute-start | bytes 221192 | tf_op jit(solution)/shard_map/ppermute | solution.py:34
  123.9 6.2 %collective-permute-start.24 = (bf16[144,256]{1,0:T(8,128)(2,1)S(1)}, bf16[144,256]{1,0:T(8,128)(2,1)S(1)}, u32[]{:S(2)}, u32[]{:S(2)}) collective-permute-start(bf16[144,256]{1,0:T(8,128)(2,1)S(1)} %get-tuple-element.162), channel_id=1, source_target_pairs={{0,24},{1,25},{2,26},{3,27},{4,28},{5,29},{6,30},{7,31}} | collective-permute-start | bytes 221192 | tf_op jit(solution)/shard_map/ppermute | solution.py:34
  124.6 15.5 %collective-permute-start.21 = (bf16[1024,256]{1,0:T(8,128)(2,1)}, bf16[1024,256]{1,0:T(8,128)(2,1)S(1)}, u32[]{:S(2)}, u32[]{:S(2)}) collective-permute-start(bf16[1024,256]{1,0:T(8,128)(2,1)} %bitcast.7.refs_2_), channel_id=1, source_target_pairs={{8,0},{9,1},{10,2},{11,3},{12,4},{13,5},{14,6},{15,7},{16,8},{17,9... | collective-permute-start | bytes 1572872 | tf_op jit(solution)/shard_map/ppermute | solution.py:34
  128.0 14.8 %collective-permute-start.20 = (bf16[1024,256]{1,0:T(8,128)(2,1)S(1)}, bf16[1024,256]{1,0:T(8,128)(2,1)}, u32[]{:S(2)}, u32[]{:S(2)}) collective-permute-start(bf16[1024,256]{1,0:T(8,128)(2,1)S(1)} %collective-permute-done.19.refs_0_), channel_id=1, source_target_pairs={{8,16},{9,17},{10,18},{11,19},{12,20},{13,21},{14,22},{15,23},{16,... | collective-permute-start | bytes 1572872 | tf_op jit(solution)/shard_map/ppermute | solution.py:34
  133.2 9.6 %collective-permute-start.25 = (bf16[1024,256]{1,0:T(8,128)(2,1)S(1)}, bf16[1024,256]{1,0:T(8,128)(2,1)S(1)}, u32[]{:S(2)}, u32[]{:S(2)}) collective-permute-start(bf16[1024,256]{1,0:T(8,128)(2,1)S(1)} %collective-permute-done.19.refs_0_), channel_id=1, source_target_pairs={{0,4},{1,5},{2,6},{3,7},{4,0},{5,1},{6,2},{7,3},{8,12},{9,13},{10,... | collective-permute-start | bytes 1572872 | tf_op jit(solution)/shard_map/ppermute | solution.py:34
  133.3 2.5 %collective-permute-start.26 = (bf16[768,256]{1,0:T(8,128)(2,1)S(1)}, bf16[768,256]{1,0:T(8,128)(2,1)S(1)}, u32[]{:S(2)}, u32[]{:S(2)}) collective-permute-start(bf16[768,256]{1,0:T(8,128)(2,1)S(1)} %get-tuple-element.167), channel_id=1, source_target_pairs={{0,4},{1,5},{2,6},{3,7},{4,0},{5,1},{6,2},{7,3},{8,12},{9,13},{10,... | collective-permute-start | bytes 1179656 | tf_op jit(solution)/shard_map/ppermute | solution.py:34
  139.2 12.2 %collective-permute-start.27 = (bf16[192,1024]{1,0:T(8,128)(2,1)S(1)}, bf16[192,1024]{1,0:T(8,128)(2,1)S(1)}, u32[]{:S(2)}, u32[]{:S(2)}) collective-permute-start(bf16[192,1024]{1,0:T(8,128)(2,1)S(1)} %get-tuple-element.175), channel_id=1, source_target_pairs={{0,1},{1,0},{2,3},{3,2},{4,5},{5,4},{6,7},{7,6},{8,9},{9,8},{10,11... | collective-permute-start | bytes 1179656 | tf_op jit(solution)/shard_map/ppermute | solution.py:34
  144.0 2.9 %collective-permute-start.30 = (bf16[512,256]{1,0:T(8,128)(2,1)S(1)}, bf16[512,256]{1,0:T(8,128)(2,1)S(1)}, u32[]{:S(2)}, u32[]{:S(2)}) collective-permute-start(bf16[512,256]{1,0:T(8,128)(2,1)S(1)} %get-tuple-element.185), channel_id=1, source_target_pairs={{0,4},{1,5},{2,6},{3,7},{4,0},{5,1},{6,2},{7,3},{8,12},{9,13},{10,... | collective-permute-start | bytes 786440 | tf_op jit(solution)/shard_map/ppermute | solution.py:34
  144.1 2.8 %collective-permute-start.31 = (bf16[512,256]{1,0:T(8,128)(2,1)S(1)}, bf16[512,256]{1,0:T(8,128)(2,1)S(1)}, u32[]{:S(2)}, u32[]{:S(2)}) collective-permute-start(bf16[512,256]{1,0:T(8,128)(2,1)S(1)} %get-tuple-element.186), channel_id=1, source_target_pairs={{0,4},{1,5},{2,6},{3,7},{4,0},{5,1},{6,2},{7,3},{8,12},{9,13},{10,... | collective-permute-start | bytes 786440 | tf_op jit(solution)/shard_map/ppermute | solution.py:34
  144.6 20.4 %collective-permute-start.28 = (bf16[192,1024]{1,0:T(8,128)(2,1)S(1)}, bf16[192,1024]{1,0:T(8,128)(2,1)S(1)}, u32[]{:S(2)}, u32[]{:S(2)}) collective-permute-start(bf16[192,1024]{1,0:T(8,128)(2,1)S(1)} %get-tuple-element.176), channel_id=1, source_target_pairs={{0,2},{1,3},{2,0},{3,1},{4,6},{5,7},{6,4},{7,5},{8,10},{9,11},{10,... | collective-permute-start | bytes 1179656 | tf_op jit(solution)/shard_map/ppermute | solution.py:34
  145.3 19.7 %collective-permute-start.29 = (bf16[192,1024]{1,0:T(8,128)(2,1)S(1)}, bf16[192,1024]{1,0:T(8,128)(2,1)S(1)}, u32[]{:S(2)}, u32[]{:S(2)}) collective-permute-start(bf16[192,1024]{1,0:T(8,128)(2,1)S(1)} %get-tuple-element.177), channel_id=1, source_target_pairs={{0,3},{1,2},{2,1},{3,0},{4,7},{5,6},{6,5},{7,4},{8,11},{9,10},{10,... | collective-permute-start | bytes 1179656 | tf_op jit(solution)/shard_map/ppermute | solution.py:34
  149.3 18.8 %collective-permute-start.32 = (bf16[192,1024]{1,0:T(8,128)(2,1)S(1)}, bf16[192,1024]{1,0:T(8,128)(2,1)S(1)}, u32[]{:S(2)}, u32[]{:S(2)}) collective-permute-start(bf16[192,1024]{1,0:T(8,128)(2,1)S(1)} %get-tuple-element.182), channel_id=1, source_target_pairs={{0,1},{1,0},{2,3},{3,2},{4,5},{5,4},{6,7},{7,6},{8,9},{9,8},{10,11... | collective-permute-start | bytes 1179656 | tf_op jit(solution)/shard_map/ppermute | solution.py:34
  150.6 30.3 %collective-permute-start.33 = (bf16[192,1024]{1,0:T(8,128)(2,1)S(1)}, bf16[192,1024]{1,0:T(8,128)(2,1)S(1)}, u32[]{:S(2)}, u32[]{:S(2)}) collective-permute-start(bf16[192,1024]{1,0:T(8,128)(2,1)S(1)} %get-tuple-element.183), channel_id=1, source_target_pairs={{0,2},{1,3},{2,0},{3,1},{4,6},{5,7},{6,4},{7,5},{8,10},{9,11},{10,... | collective-permute-start | bytes 1179656 | tf_op jit(solution)/shard_map/ppermute | solution.py:34
  151.4 29.6 %collective-permute-start.34 = (bf16[192,1024]{1,0:T(8,128)(2,1)S(1)}, bf16[192,1024]{1,0:T(8,128)(2,1)S(1)}, u32[]{:S(2)}, u32[]{:S(2)}) collective-permute-start(bf16[192,1024]{1,0:T(8,128)(2,1)S(1)} %get-tuple-element.184), channel_id=1, source_target_pairs={{0,3},{1,2},{2,1},{3,0},{4,7},{5,6},{6,5},{7,4},{8,11},{9,10},{10,... | collective-permute-start | bytes 1179656 | tf_op jit(solution)/shard_map/ppermute | solution.py:34

commit v5 on v4

--- a/solution.py
+++ b/solution.py
@@ -596,7 +596,7 @@
     near = line_near(shard, depth)
     wide, out_raw = phase((wide, out_raw, shard))[:2]
     exchange = lambda array, r: shift(array, lambda z, k, e: (z, k, e ^ r))
-    own = [wide] + [exchange(wide, r) for r in range(1, groups)]
+    own = [wide] + [exchange(wide, r) for r in range(groups - 1, 0, -1)][::-1]
     local = lambda vector: lax.dynamic_slice_in_dim(vector, core * heads, heads, 0)
     lanes = lambda vector: jnp.concatenate(
         [jnp.pad(local(vector), (0, dt_lane - heads))] * (128 // dt_lane)
@@ -640,15 +640,17 @@
         head, experts, depth, width, length,
     )
     below = shift(out_shard, lambda z, k, e: ((z + 1) % depth, k, e))
+    downs = [above]
+    for s in range(2, depth - 1):
+        downs.append(step_down(downs[-1], s, depth))
     y, gate, final, below = phase((y, gate, final, below))
 
     finals = [
         shift(final, lambda z, k, e: (z + s, k, e) if z + s < depth else None) for s in range(1, depth)
     ]
-    ups, downs = [below], [above]
+    ups = [below]
     for s in range(2, depth - 1):
         ups.append(step_up(ups[-1], s, depth))
-        downs.append(step_down(downs[-1], s, depth))
     theirs, mine = norm(core_at, found, half_gain, [y], [gate], finals, head, length)
     theirs, mine, below = phase((theirs, mine, below))
     other = swap(theirs)
@@ -659,7 +661,7 @@
 
     def send(*weights):
         results = project_out(position, ids, mine, other, weights, groups)
-        return [results[0]] + [exchange(results[r], r) for r in range(1, groups)]
+        return [results[0]] + [exchange(results[r], r) for r in range(groups - 1, 0, -1)][::-1]
 
     blocks = [send(out_shard, out_shard_other, above, above_other)]
     ups, downs, below_other, blocks[0][0] = phase((ups, downs, below_other, blocks[0][0]))

time: 184 us -> 184 us (level)
  no operation moved by 1% of the time
where the time goes in v5:
time: 184 us; the launch traced here: 183 us
  waiting for transfers between devices  70.9 us (39%)
  starting transfers between devices  44.1 us (24%)
  Pallas kernels  39.3 us (21%)
  local copies, waits for them, and re-layouts  23.9 us (13%)
  other arithmetic  4.14 us (2%)
    ppermute x35, waiting for transfers between devices, shift(): return lax.ppermute(array, both, pairs)  70.9 us
    ppermute x35, starting transfers between devices, shift(): return lax.ppermute(array, both, pairs)  44.1 us
    pallas_call x1, Pallas kernels, ahead(): pl.pallas_call(functools.partial(ahead_kernel, experts, depth, width, dis...  13.2 us
    unnamed x47, local copies, waits for them, and re-layouts  10.9 us
    pallas_call x1, Pallas kernels, scan(): pl.pallas_call(functools.partial(scan_kernel, head, experts, depth, width...  10.8 us
    concatenate x1, local copies, waits for them, and re-layouts, on_device(): jnp.concatenate([jnp.pad(picked, ((0, dt_lane - heads), (0, 0)))] * (128...  6.78 us
    pallas_call x2, Pallas kernels, project_out(): pl.pallas_call(functools.partial(out_kernel, groups // 2, groups), in_spe...  5.86 us
  transfers between devices with their start and end apart: 35, of which 14 were waited for; matrix products, arithmetic and copies ran while one was open for 10% of the time, Pallas kernels for 20%

profile of v5, /device:TPU:16, one launch (start us, length us, event | category | flops | bytes accessed | tf_op | source)
XLA Modules:
  0.0 182.8 jit_solution(16733685470735647003)
XLA Ops:
  0.5 1.5 copy.18
  2.1 0.9 cut.1
  2.9 1.6 collective-permute-start
  4.5 1.8 collective-permute-start.1
  6.3 1.5 collective-permute-start.2
  7.8 1.2 collective-permute-start.3
  9.3 1.2 concatenate.25.refs_0_
  10.6 2.3 %collective-permute-done.1.refs_1_ = bf16[256,512]{1,0:T(8,128)(2,1)S(1)} collective-permute-done((bf16[256,512]{1,0:T(8,128)(2,1)S(1)}, bf16[256,512]{1,0:T(8,128)(2,1)S(1)}, u32[]{:S(2)}, u32[]{:S(2)}) %collective-permute-start.1) | collective-permute-done | bytes 262176 | tf_op jit(solution)/shard_map/ppermute | solution.py:34
  12.9 7.2 %collective-permute-done.2.refs_2_ = bf16[256,512]{1,0:T(8,128)(2,1)S(1)} collective-permute-done((bf16[256,512]{1,0:T(8,128)(2,1)S(1)}, bf16[256,512]{1,0:T(8,128)(2,1)S(1)}, u32[]{:S(2)}, u32[]{:S(2)}) %collective-permute-start.2) | collective-permute-done | bytes 262176 | tf_op jit(solution)/shard_map/ppermute | solution.py:34
  20.1 1.0 collective-permute-done.3.refs_3_
  21.1 1.1 arrange.2
  22.3 0.6 collective-permute-start.9
  22.9 1.5 collective-permute-start.8
  24.4 1.4 collective-permute-start.7
  25.8 1.6 collective-permute-start.5
  27.8 1.0 copy.17
  28.8 1.2 constant_dynamic-slice_fusion.2
  30.1 0.9 pad.11
  31.0 6.8 %concatenate.26 = bf16[128,2048]{0,1:T(8,128)(2,1)} concatenate(bf16[16,2048]{0,1:T(8,128)(2,1)} %pad.11, bf16[16,2048]{0,1:T(8,128)(2,1)} %pad.11, bf16[16,2048]{0,1:T(8,128)(2,1)} %pad.11, bf16[16,2048]{0,1:T(8,128)(2,1)} %pad.11, bf16[16,2048]{0,1:T(8,128)(2,1)} %pad.11, bf16[16,2048]{0,1:T(8,128)(2,1)} %pad.11, bf16[16,2048]{0,1:T(8,128)(2,1)} %pad.11, bf16[16,2048]{0,1:T(8,128)(2,1)} %pad.11), dimensions={0} | concatenate | bytes 1048576 | tf_op jit(solution)/shard_map/concatenate | solution.py:605
  38.3 1.0 copy-done.13
  39.4 1.0 copy-done.15
  40.6 4.1 %collective-permute-done.9.refs_3_ = bf16[192,2176]{1,0:T(8,128)(2,1)S(1)} collective-permute-done((bf16[192,2176]{1,0:T(8,128)(2,1)S(1)}, bf16[192,2176]{1,0:T(8,128)(2,1)S(1)}, u32[]{:S(2)}, u32[]{:S(2)}) %collective-permute-start.9) | collective-permute-done | bytes 835616 | tf_op jit(solution)/shard_map/ppermute | solution.py:34
  44.7 0.9 copy-done.7
  46.1 16.4 %collective-permute-done.8.refs_2_ = bf16[192,2176]{1,0:T(8,128)(2,1)S(1)} collective-permute-done((bf16[192,2176]{1,0:T(8,128)(2,1)S(1)}, bf16[192,2176]{1,0:T(8,128)(2,1)S(1)}, u32[]{:S(2)}, u32[]{:S(2)}) %collective-permute-start.8) | collective-permute-done | bytes 835616 | tf_op jit(solution)/shard_map/ppermute | solution.py:34
  62.6 0.9 copy-done.9
  63.5 1.5 collective-permute-start.11
  64.9 0.9 copy-done.11
  65.9 2.8 %pad_maximum_fusion.w_ref = bf16[2048,384]{1,0:T(8,128)(2,1)} fusion(bf16[2048,128]{1,0:T(8,128)(2,1)} %bitcast.21, bf16[2048,256]{1,0:T(8,128)(2,1)} %param.17), kind=kLoop, calls=%fused_computation | loop fusion | flops 3145728 | bytes 3145728 | tf_op jit(solution)/shard_map/concatenate | solution.py:606
  69.2 2.6 %collective-permute-done.11.refs_2_ = bf16[512,256]{1,0:T(8,128)(2,1)S(1)} collective-permute-done((bf16[512,256]{1,0:T(8,128)(2,1)S(1)}, bf16[512,256]{1,0:T(8,128)(2,1)S(1)}, u32[]{:S(2)}, u32[]{:S(2)}) %collective-permute-start.11) | collective-permute-done | bytes 262176 | tf_op jit(solution)/shard_map/ppermute | solution.py:34
  71.9 1.9 %collective-permute-done.10.refs_1_ = bf16[512,256]{1,0:T(8,128)(2,1)S(1)} collective-permute-done((bf16[512,256]{1,0:T(8,128)(2,1)S(1)}, bf16[512,256]{1,0:T(8,128)(2,1)S(1)}, u32[]{:S(2)}, u32[]{:S(2)}) %collective-permute-start.10) | collective-permute-done | bytes 262176 | tf_op jit(solution)/shard_map/ppermute | solution.py:34
  73.8 1.1 arrange.3
  74.9 3.5 %collective-permute-start.13 = (bf16[1024,512]{1,0:T(8,128)(2,1)}, bf16[1024,512]{1,0:T(8,128)(2,1)}, u32[]{:S(2)}, u32[]{:S(2)}) collective-permute-start(bf16[1024,512]{1,0:T(8,128)(2,1)} %collective-permute-done.5.refs_1_), channel_id=1, source_target_pairs={{8,16},{9,17},{10,18},{11,19},{12,20},{13,21},{14,22},{15,23},{16,... | collective-permute-start | bytes 3145736 | tf_op jit(solution)/shard_map/ppermute | solution.py:34
  78.4 4.4 %collective-permute-start.14 = (bf16[1024,512]{1,0:T(8,128)(2,1)}, bf16[1024,512]{1,0:T(8,128)(2,1)}, u32[]{:S(2)}, u32[]{:S(2)}) collective-permute-start(bf16[1024,512]{1,0:T(8,128)(2,1)} %collective-permute-done.6.refs_2_), channel_id=1, source_target_pairs={{8,0},{9,1},{10,2},{11,3},{12,4},{13,5},{14,6},{15,7},{16,8},{17,9... | collective-permute-start | bytes 3145736 | tf_op jit(solution)/shard_map/ppermute | solution.py:34
  82.7 1.7 copy-done.5
  84.9 1.9 %copy-done.6 = bf16[768,2176]{1,0:T(8,128)(2,1)S(1)} copy-done((bf16[768,2176]{1,0:T(8,128)(2,1)S(1)}, bf16[768,2176]{1,0:T(8,128)(2,1)}, u32[]{:S(2)}) %copy-start.6) | copy-done | bytes 3342360
  86.9 1.0 lay.3.x_ref.refs_5_.refs_6_
  87.9 1.9 %collective-permute-start.16 = (bf16[16,2176]{1,0:T(8,128)(2,1)S(1)}, bf16[16,2176]{1,0:T(8,128)(2,1)S(1)}, u32[]{:S(2)}, u32[]{:S(2)}) collective-permute-start(bf16[16,2176]{1,0:T(8,128)(2,1)S(1)} %slice.12), channel_id=1, source_target_pairs={{0,8},{1,9},{2,10},{3,11},{4,12},{5,13},{6,14},{7,15},{8,16},{9,17... | collective-permute-start | bytes 208904 | tf_op jit(solution)/shard_map/ppermute | solution.py:34
  89.8 0.8 copy-done.1
  90.6 13.2 %ahead.1 = (f32[1536,512]{1,0:T(8,128)S(1)}, bf16[1536,256]{1,0:T(8,128)(2,1)S(1)}, f32[1536,128]{1,0:T(8,128)S(1)}, f32[32,1536]{1,0:T(8,128)S(1)}) custom-call(s32[1]{0:T(128)} %bitcast.pos_ref, bf16[1536,2176]{1,0:T(8,128)(2,1)} %copy-done.1, bf16[2048,384]{1,0:T(8,128)(2,1)S(1)} %copy-done.2, f32[1,128]{1,0:T(1,128)S(1)} %bitcast.20, ...), custom_call_target="tpu_custom_call" | custom-call | tf_op jit(solution)/shard_map/ahead/pallas_call | solution.py:122
  103.8 0.9 constant_dynamic-slice_fusion.ids_ref
  104.9 0.8 collective-permute-start.19
  105.6 10.8 %scan.1 = (f32[1536,256]{1,0:T(8,128)S(1)}, bf16[1536,256]{1,0:T(8,128)(2,1)S(1)}, bf16[144,256]{1,0:T(8,128)(2,1)S(1)}) custom-call(s32[1]{0:T(128)} %bitcast.pos_ref, bf16[1024,512]{1,0:T(8,128)(2,1)} %bitcast.5.refs_0_, bf16[1024,512]{1,0:T(8,128)(2,1)} %collective-permute-done.5.refs_1_, bf16[1024,512]{1,0:T(8,128)(2,1)} %collective-permute-done.6.refs_2_, ...), custom_call_target="tpu_custom_call" | custom-call | tf_op jit(solution)/shard_map/scan/pallas_call | solution.py:275
  116.5 2.6 %collective-permute-done.19.refs_0_ = bf16[1024,256]{1,0:T(8,128)(2,1)S(1)} collective-permute-done((bf16[1024,256]{1,0:T(8,128)(2,1)}, bf16[1024,256]{1,0:T(8,128)(2,1)S(1)}, u32[]{:S(2)}, u32[]{:S(2)}) %collective-permute-start.19) | collective-permute-done | bytes 524320 | tf_op jit(solution)/shard_map/ppermute | solution.py:34
  119.1 3.5 %collective-permute-start.22 = (bf16[144,256]{1,0:T(8,128)(2,1)S(1)}, bf16[144,256]{1,0:T(8,128)(2,1)S(1)}, u32[]{:S(2)}, u32[]{:S(2)}) collective-permute-start(bf16[144,256]{1,0:T(8,128)(2,1)S(1)} %get-tuple-element.162), channel_id=1, source_target_pairs={{0,8},{1,9},{2,10},{3,11},{4,12},{5,13},{6,14},{7,15},{8,16},{9,17... | collective-permute-start | bytes 221192 | tf_op jit(solution)/shard_map/ppermute | solution.py:34
  122.6 1.3 collective-permute-start.23
  123.9 0.7 collective-permute-start.24
  124.6 3.4 %collective-permute-start.21 = (bf16[1024,256]{1,0:T(8,128)(2,1)}, bf16[1024,256]{1,0:T(8,128)(2,1)S(1)}, u32[]{:S(2)}, u32[]{:S(2)}) collective-permute-start(bf16[1024,256]{1,0:T(8,128)(2,1)} %bitcast.7.refs_2_), channel_id=1, source_target_pairs={{8,0},{9,1},{10,2},{11,3},{12,4},{13,5},{14,6},{15,7},{16,8},{17,9... | collective-permute-start | bytes 1572872 | tf_op jit(solution)/shard_map/ppermute | solution.py:34
  128.0 2.1 %collective-permute-start.20 = (bf16[1024,256]{1,0:T(8,128)(2,1)S(1)}, bf16[1024,256]{1,0:T(8,128)(2,1)}, u32[]{:S(2)}, u32[]{:S(2)}) collective-permute-start(bf16[1024,256]{1,0:T(8,128)(2,1)S(1)} %collective-permute-done.19.refs_0_), channel_id=1, source_target_pairs={{8,16},{9,17},{10,18},{11,19},{12,20},{13,21},{14,22},{15,23},{16,... | collective-permute-start | bytes 1572872 | tf_op jit(solution)/shard_map/ppermute | solution.py:34
  130.2 3.1 %norm.1 = (bf16[768,256]{1,0:T(8,128)(2,1)S(1)}, bf16[768,256]{1,0:T(8,128)(2,1)S(1)}) custom-call(s32[1]{0:T(128)} %bitcast.1.pos_ref, bf16[1536,256]{1,0:T(8,128)(2,1)S(1)} %get-tuple-element.148.refs_9_.maps_ref, f32[1536,128]{1,0:T(8,128)S(1)} %get-tuple-element.149.refs_10_.cols_ref, f32[1,256]{1,0:T(1,128)S(1)} %bitcast.18, ...), custom_call_target="tpu_custom_call" | custom-call | tf_op jit(solution)/shard_map/norm/pallas_call | solution.py:368
  133.9 1.9 %collective-permute-done.26.other_ref = bf16[768,256]{1,0:T(8,128)(2,1)S(1)} collective-permute-done((bf16[768,256]{1,0:T(8,128)(2,1)S(1)}, bf16[768,256]{1,0:T(8,128)(2,1)S(1)}, u32[]{:S(2)}, u32[]{:S(2)}) %collective-permute-start.26) | collective-permute-done | bytes 393248 | tf_op jit(solution)/shard_map/ppermute | solution.py:34
  135.8 3.4 %project_out.2 = (bf16[192,1024]{1,0:T(8,128)(2,1)S(1)}, bf16[192,1024]{1,0:T(8,128)(2,1)S(1)}, bf16[192,1024]{1,0:T(8,128)(2,1)S(1)}, bf16[192,1024]{1,0:T(8,128)(2,1)S(1)}) custom-call(s32[2]{0:T(128)S(1)} %pad_add_fusion.1.pos_ref, bf16[768,128]{1,0:T(8,128)(2,1)S(1)} %constant_dynamic-slice_fusion.ids_ref, ...), custom_call_target="tpu_custom_call" | custom-call | tf_op jit(solution)/shard_map/project_out/pallas_call | solution.py:409
  139.2 0.9 collective-permute-start.27
  140.1 2.7 %collective-permute-done.20 = bf16[1024,256]{1,0:T(8,128)(2,1)} collective-permute-done((bf16[1024,256]{1,0:T(8,128)(2,1)S(1)}, bf16[1024,256]{1,0:T(8,128)(2,1)}, u32[]{:S(2)}, u32[]{:S(2)}) %collective-permute-start.20) | collective-permute-done | bytes 524320 | tf_op jit(solution)/shard_map/ppermute | solution.py:34
  142.8 1.1 broadcast_select_fusion.refs_2_
  144.6 0.7 collective-permute-start.28
  145.3 1.5 collective-permute-start.29
  146.9 2.4 %project_out.3 = (bf16[192,1024]{1,0:T(8,128)(2,1)S(1)}, bf16[192,1024]{1,0:T(8,128)(2,1)S(1)}, bf16[192,1024]{1,0:T(8,128)(2,1)S(1)}, bf16[192,1024]{1,0:T(8,128)(2,1)S(1)}) custom-call(s32[2]{0:T(128)S(1)} %pad_add_fusion.1.pos_ref, bf16[768,128]{1,0:T(8,128)(2,1)S(1)} %constant_dynamic-slice_fusion.ids_ref, ...), custom_call_target="tpu_custom_call" | custom-call | tf_op jit(solution)/shard_map/project_out/pallas_call | solution.py:409
  149.3 1.3 collective-permute-start.32
  150.6 0.7 collective-permute-start.33
  151.4 1.6 collective-permute-start.34
  153.1 11.9 %collective-permute-done.28.refs_2_ = bf16[192,1024]{1,0:T(8,128)(2,1)S(1)} collective-permute-done((bf16[192,1024]{1,0:T(8,128)(2,1)S(1)}, bf16[192,1024]{1,0:T(8,128)(2,1)S(1)}, u32[]{:S(2)}, u32[]{:S(2)}) %collective-permute-start.28) | collective-permute-done | bytes 393248 | tf_op jit(solution)/shard_map/ppermute | solution.py:34
  165.0 3.2 %collective-permute-done.32.refs_5_ = bf16[192,1024]{1,0:T(8,128)(2,1)S(1)} collective-permute-done((bf16[192,1024]{1,0:T(8,128)(2,1)S(1)}, bf16[192,1024]{1,0:T(8,128)(2,1)S(1)}, u32[]{:S(2)}, u32[]{:S(2)}) %collective-permute-start.32) | collective-permute-done | bytes 393248 | tf_op jit(solution)/shard_map/ppermute | solution.py:34
  168.1 12.8 %collective-permute-done.33.refs_6_ = bf16[192,1024]{1,0:T(8,128)(2,1)S(1)} collective-permute-done((bf16[192,1024]{1,0:T(8,128)(2,1)S(1)}, bf16[192,1024]{1,0:T(8,128)(2,1)S(1)}, u32[]{:S(2)}, u32[]{:S(2)}) %collective-permute-start.33) | collective-permute-done | bytes 393248 | tf_op jit(solution)/shard_map/ppermute | solution.py:34
  180.9 1.8 add_up.1
  (93 shorter events, 5.1 us)
Async XLA Ops:
  0.0 40.6 %copy-start = (f32[4,512]{1,0:T(4,128)S(1)}, f32[4,512]{1,0:T(4,128)}, u32[]{:S(2)}) copy-start(f32[4,512]{1,0:T(4,128)} %param.23) | copy-start | bytes 24580
  0.0 9.0 %copy-start.17 = (s32[192,1]{0,1:T(1,128)S(1)}, s32[192,1]{0,1:T(1,128)}, u32[]{:S(2)}) copy-start(s32[192,1]{0,1:T(1,128)} %param.13) | copy-start | bytes 2308
  0.0 9.2 %copy-start.18 = (bf16[192]{0:T(256)(128)(2,1)S(1)}, bf16[192]{0:T(256)(128)(2,1)}, u32[]{:S(2)}) copy-start(bf16[192]{0:T(256)(128)(2,1)} %param.14) | copy-start | bytes 1156
  0.0 21.1 %collective-permute-start.4 = (bf16[1024,256]{1,0:T(8,128)(2,1)}, bf16[1024,256]{1,0:T(8,128)(2,1)S(1)}, u32[]{:S(2)}, u32[]{:S(2)}) collective-permute-start(bf16[1024,256]{1,0:T(8,128)(2,1)} %bitcast.16), channel_id=1, source_target_pairs={{0,24},{1,25},{2,26},{3,27},{4,28},{5,29},{6,30},{7,31},{8,0},{9,1... | collective-permute-start | bytes 1572872 | tf_op jit(solution)/shard_map/ppermute | solution.py:34
  0.5 27.3 %copy-start.16 = (bf16[32,2048]{1,0:T(8,128)(2,1)S(1)}, bf16[32,2048]{1,0:T(8,128)(2,1)}, u32[]{:S(2)}) copy-start(bf16[32,2048]{1,0:T(8,128)(2,1)} %param.18) | copy-start | bytes 393220
  2.9 7.7 %collective-permute-start = (bf16[256,512]{1,0:T(8,128)(2,1)}, bf16[256,512]{1,0:T(8,128)(2,1)S(1)}, u32[]{:S(2)}, u32[]{:S(2)}) collective-permute-start(bf16[256,512]{1,0:T(8,128)(2,1)} %get-tuple-element.95), channel_id=1, source_target_pairs={{0,0},{1,4},{2,2},{3,6},{4,1},{5,5},{6,3},{7,7},{8,8},{9,12},{10,1... | collective-permute-start | bytes 786440 | tf_op jit(solution)/shard_map/ppermute | solution.py:34
  4.5 8.4 %collective-permute-start.1 = (bf16[256,512]{1,0:T(8,128)(2,1)S(1)}, bf16[256,512]{1,0:T(8,128)(2,1)S(1)}, u32[]{:S(2)}, u32[]{:S(2)}) collective-permute-start(bf16[256,512]{1,0:T(8,128)(2,1)S(1)} %get-tuple-element.96), channel_id=1, source_target_pairs={{0,1},{1,5},{2,3},{3,7},{4,0},{5,4},{6,2},{7,6},{8,9},{9,13},{10,1... | collective-permute-start | bytes 786440 | tf_op jit(solution)/shard_map/ppermute | solution.py:34
  6.3 13.8 %collective-permute-start.2 = (bf16[256,512]{1,0:T(8,128)(2,1)S(1)}, bf16[256,512]{1,0:T(8,128)(2,1)S(1)}, u32[]{:S(2)}, u32[]{:S(2)}) collective-permute-start(bf16[256,512]{1,0:T(8,128)(2,1)S(1)} %get-tuple-element.97), channel_id=1, source_target_pairs={{0,2},{1,6},{2,0},{3,4},{4,3},{5,7},{6,1},{7,5},{8,10},{9,14},{10,... | collective-permute-start | bytes 786440 | tf_op jit(solution)/shard_map/ppermute | solution.py:34
  7.8 13.3 %collective-permute-start.3 = (bf16[256,512]{1,0:T(8,128)(2,1)S(1)}, bf16[256,512]{1,0:T(8,128)(2,1)S(1)}, u32[]{:S(2)}, u32[]{:S(2)}) collective-permute-start(bf16[256,512]{1,0:T(8,128)(2,1)S(1)} %get-tuple-element.98), channel_id=1, source_target_pairs={{0,3},{1,7},{2,1},{3,5},{4,2},{5,6},{6,0},{7,4},{8,11},{9,15},{10,... | collective-permute-start | bytes 786440 | tf_op jit(solution)/shard_map/ppermute | solution.py:34
  10.6 27.2 %copy-start.3 = (bf16[192,2176]{1,0:T(8,128)(2,1)}, bf16[192,2176]{1,0:T(8,128)(2,1)S(1)}, u32[]{:S(2)}) copy-start(bf16[192,2176]{1,0:T(8,128)(2,1)S(1)} %concatenate.25.refs_0_) | copy-start | bytes 2506756
  21.1 1.1 copy-start.14
  22.3 22.5 %collective-permute-start.9 = (bf16[192,2176]{1,0:T(8,128)(2,1)S(1)}, bf16[192,2176]{1,0:T(8,128)(2,1)S(1)}, u32[]{:S(2)}, u32[]{:S(2)}) collective-permute-start(bf16[192,2176]{1,0:T(8,128)(2,1)S(1)} %concatenate.25.refs_0_), channel_id=1, source_target_pairs={{0,3},{1,2},{2,1},{3,0},{4,7},{5,6},{6,5},{7,4},{8,11},{9,10},{10,... | collective-permute-start | bytes 2506760 | tf_op jit(solution)/shard_map/ppermute | solution.py:34
  22.9 39.7 %collective-permute-start.8 = (bf16[192,2176]{1,0:T(8,128)(2,1)S(1)}, bf16[192,2176]{1,0:T(8,128)(2,1)S(1)}, u32[]{:S(2)}, u32[]{:S(2)}) collective-permute-start(bf16[192,2176]{1,0:T(8,128)(2,1)S(1)} %concatenate.25.refs_0_), channel_id=1, source_target_pairs={{0,2},{1,3},{2,0},{3,1},{4,6},{5,7},{6,4},{7,5},{8,10},{9,11},{10,... | collective-permute-start | bytes 2506760 | tf_op jit(solution)/shard_map/ppermute | solution.py:34
  24.4 40.6 %collective-permute-start.7 = (bf16[192,2176]{1,0:T(8,128)(2,1)S(1)}, bf16[192,2176]{1,0:T(8,128)(2,1)S(1)}, u32[]{:S(2)}, u32[]{:S(2)}) collective-permute-start(bf16[192,2176]{1,0:T(8,128)(2,1)S(1)} %concatenate.25.refs_0_), channel_id=1, source_target_pairs={{0,1},{1,0},{2,3},{3,2},{4,5},{5,4},{6,7},{7,6},{8,9},{9,8},{10,11... | collective-permute-start | bytes 2506760 | tf_op jit(solution)/shard_map/ppermute | solution.py:34
  25.8 49.1 %collective-permute-start.5 = (bf16[1024,512]{1,0:T(8,128)(2,1)}, bf16[1024,512]{1,0:T(8,128)(2,1)}, u32[]{:S(2)}, u32[]{:S(2)}) collective-permute-start(bf16[1024,512]{1,0:T(8,128)(2,1)} %bitcast.5.refs_0_), channel_id=1, source_target_pairs={{0,8},{1,9},{2,10},{3,11},{4,12},{5,13},{6,14},{7,15},{8,16},{9,17... | collective-permute-start | bytes 3145736 | tf_op jit(solution)/shard_map/ppermute | solution.py:34
  27.3 47.5 %collective-permute-start.6 = (bf16[1024,512]{1,0:T(8,128)(2,1)}, bf16[1024,512]{1,0:T(8,128)(2,1)}, u32[]{:S(2)}, u32[]{:S(2)}) collective-permute-start(bf16[1024,512]{1,0:T(8,128)(2,1)} %bitcast.5.refs_0_), channel_id=1, source_target_pairs={{0,24},{1,25},{2,26},{3,27},{4,28},{5,29},{6,30},{7,31},{8,0},{9,1... | collective-permute-start | bytes 3145736 | tf_op jit(solution)/shard_map/ppermute | solution.py:34
  30.0 7.7 %copy-start.20 = (f32[8]{0:T(128)S(1)}, f32[8]{0:T(128)}, u32[]{:S(2)}) copy-start(f32[8]{0:T(128)} %param.21) | copy-start | bytes 100
  30.0 8.0 %copy-start.21 = (f32[8]{0:T(128)S(1)}, f32[8]{0:T(128)}, u32[]{:S(2)}) copy-start(f32[8]{0:T(128)} %param.19) | copy-start | bytes 100
  30.1 8.1 %copy-start.22 = (f32[8]{0:T(128)S(1)}, f32[8]{0:T(128)}, u32[]{:S(2)}) copy-start(f32[8]{0:T(128)} %param.20) | copy-start | bytes 100
  31.0 9.5 %copy-start.19 = (f32[512]{0:T(512)S(1)}, f32[512]{0:T(512)}, u32[]{:S(2)}) copy-start(f32[512]{0:T(512)} %param.22) | copy-start | bytes 6148
  38.3 1.0 copy-start.13
  39.4 1.0 copy-start.15
  40.4 28.3 %copy-start.4 = (bf16[192,2176]{1,0:T(8,128)(2,1)S(1)}, bf16[192,2176]{1,0:T(8,128)(2,1)}, u32[]{:S(2)}) copy-start(bf16[192,2176]{1,0:T(8,128)(2,1)} %copy-done.3) | copy-start | bytes 2506756
  44.7 0.9 copy-start.7
  45.6 23.0 %copy-start.8 = (bf16[192,2176]{1,0:T(8,128)(2,1)S(1)}, bf16[192,2176]{1,0:T(8,128)(2,1)}, u32[]{:S(2)}) copy-start(bf16[192,2176]{1,0:T(8,128)(2,1)} %copy-done.7) | copy-start | bytes 2506756
  45.6 23.6 %collective-permute-start.12 = (bf16[512,256]{1,0:T(8,128)(2,1)S(1)}, bf16[512,256]{1,0:T(8,128)(2,1)S(1)}, u32[]{:S(2)}, u32[]{:S(2)}) collective-permute-start(bf16[512,256]{1,0:T(8,128)(2,1)S(1)} %get-tuple-element.118), channel_id=1, source_target_pairs={{0,3},{1,2},{2,1},{3,0},{4,7},{5,6},{6,5},{7,4},{8,11},{9,10},{10,... | collective-permute-start | bytes 786440 | tf_op jit(solution)/shard_map/ppermute | solution.py:34
  62.6 0.9 copy-start.9
  63.5 5.2 %copy-start.10 = (bf16[192,2176]{1,0:T(8,128)(2,1)S(1)}, bf16[192,2176]{1,0:T(8,128)(2,1)}, u32[]{:S(2)}) copy-start(bf16[192,2176]{1,0:T(8,128)(2,1)} %copy-done.9) | copy-start | bytes 2506756
  63.5 8.4 %collective-permute-start.11 = (bf16[512,256]{1,0:T(8,128)(2,1)S(1)}, bf16[512,256]{1,0:T(8,128)(2,1)S(1)}, u32[]{:S(2)}, u32[]{:S(2)}) collective-permute-start(bf16[512,256]{1,0:T(8,128)(2,1)S(1)} %get-tuple-element.117), channel_id=1, source_target_pairs={{0,2},{1,3},{2,0},{3,1},{4,6},{5,7},{6,4},{7,5},{8,10},{9,11},{10,... | collective-permute-start | bytes 786440 | tf_op jit(solution)/shard_map/ppermute | solution.py:34
  64.9 0.9 copy-start.11
  65.8 2.8 %copy-start.12 = (bf16[192,2176]{1,0:T(8,128)(2,1)S(1)}, bf16[192,2176]{1,0:T(8,128)(2,1)}, u32[]{:S(2)}) copy-start(bf16[192,2176]{1,0:T(8,128)(2,1)} %copy-done.11) | copy-start | bytes 2506756
  65.9 8.0 %collective-permute-start.10 = (bf16[512,256]{1,0:T(8,128)(2,1)S(1)}, bf16[512,256]{1,0:T(8,128)(2,1)S(1)}, u32[]{:S(2)}, u32[]{:S(2)}) collective-permute-start(bf16[512,256]{1,0:T(8,128)(2,1)S(1)} %get-tuple-element.116), channel_id=1, source_target_pairs={{0,1},{1,0},{2,3},{3,2},{4,5},{5,4},{6,7},{7,6},{8,9},{9,8},{10,11... | collective-permute-start | bytes 786440 | tf_op jit(solution)/shard_map/ppermute | solution.py:34
  74.9 7.9 %collective-permute-start.15 = (bf16[768,2176]{1,0:T(8,128)(2,1)S(1)}, bf16[768,2176]{1,0:T(8,128)(2,1)S(1)}, u32[]{:S(2)}, u32[]{:S(2)}) collective-permute-start(bf16[768,2176]{1,0:T(8,128)(2,1)S(1)} %lay.2.refs_0_), channel_id=1, source_target_pairs={{0,4},{1,5},{2,6},{3,7},{4,0},{5,1},{6,2},{7,3},{8,12},{9,13},{10,... | collective-permute-start | bytes 10027016 | tf_op jit(solution)/shard_map/ppermute | solution.py:34
  74.9 29.9 %collective-permute-start.13 = (bf16[1024,512]{1,0:T(8,128)(2,1)}, bf16[1024,512]{1,0:T(8,128)(2,1)}, u32[]{:S(2)}, u32[]{:S(2)}) collective-permute-start(bf16[1024,512]{1,0:T(8,128)(2,1)} %collective-permute-done.5.refs_1_), channel_id=1, source_target_pairs={{8,16},{9,17},{10,18},{11,19},{12,20},{13,21},{14,22},{15,23},{16,... | collective-permute-start | bytes 3145736 | tf_op jit(solution)/shard_map/ppermute | solution.py:34
  78.4 26.5 %collective-permute-start.14 = (bf16[1024,512]{1,0:T(8,128)(2,1)}, bf16[1024,512]{1,0:T(8,128)(2,1)}, u32[]{:S(2)}, u32[]{:S(2)}) collective-permute-start(bf16[1024,512]{1,0:T(8,128)(2,1)} %collective-permute-done.6.refs_2_), channel_id=1, source_target_pairs={{8,0},{9,1},{10,2},{11,3},{12,4},{13,5},{14,6},{15,7},{16,8},{17,9... | collective-permute-start | bytes 3145736 | tf_op jit(solution)/shard_map/ppermute | solution.py:34
  82.7 1.7 copy-start.5
  84.4 20.4 %collective-permute-start.17 = (bf16[1024,256]{1,0:T(8,128)(2,1)}, bf16[1024,256]{1,0:T(8,128)(2,1)}, u32[]{:S(2)}, u32[]{:S(2)}) collective-permute-start(bf16[1024,256]{1,0:T(8,128)(2,1)} %bitcast.6.refs_0_), channel_id=1, source_target_pairs={{0,4},{1,5},{2,6},{3,7},{4,0},{5,1},{6,2},{7,3},{8,12},{9,13},{10,... | collective-permute-start | bytes 1572872 | tf_op jit(solution)/shard_map/ppermute | solution.py:34
  84.4 20.4 %collective-permute-start.18 = (bf16[1024,256]{1,0:T(8,128)(2,1)}, bf16[1024,256]{1,0:T(8,128)(2,1)}, u32[]{:S(2)}, u32[]{:S(2)}) collective-permute-start(bf16[1024,256]{1,0:T(8,128)(2,1)} %bitcast.7.refs_2_), channel_id=1, source_target_pairs={{0,4},{1,5},{2,6},{3,7},{4,0},{5,1},{6,2},{7,3},{8,12},{9,13},{10,... | collective-permute-start | bytes 1572872 | tf_op jit(solution)/shard_map/ppermute | solution.py:34
  84.9 1.9 %copy-start.6 = (bf16[768,2176]{1,0:T(8,128)(2,1)S(1)}, bf16[768,2176]{1,0:T(8,128)(2,1)}, u32[]{:S(2)}) copy-start(bf16[768,2176]{1,0:T(8,128)(2,1)} %copy-done.5) | copy-start | bytes 10027012
  86.9 3.7 %copy-start.2 = (bf16[2048,384]{1,0:T(8,128)(2,1)S(1)}, bf16[2048,384]{1,0:T(8,128)(2,1)}, u32[]{:S(2)}) copy-start(bf16[2048,384]{1,0:T(8,128)(2,1)} %pad_maximum_fusion.w_ref) | copy-start | bytes 4718596
  87.8 2.8 %copy-start.1 = (bf16[1536,2176]{1,0:T(8,128)(2,1)}, bf16[1536,2176]{1,0:T(8,128)(2,1)S(1)}, u32[]{:S(2)}) copy-start(bf16[1536,2176]{1,0:T(8,128)(2,1)S(1)} %lay.3.x_ref.refs_5_.refs_6_) | copy-start | bytes 20054020
  87.9 17.0 %collective-permute-start.16 = (bf16[16,2176]{1,0:T(8,128)(2,1)S(1)}, bf16[16,2176]{1,0:T(8,128)(2,1)S(1)}, u32[]{:S(2)}, u32[]{:S(2)}) collective-permute-start(bf16[16,2176]{1,0:T(8,128)(2,1)S(1)} %slice.12), channel_id=1, source_target_pairs={{0,8},{1,9},{2,10},{3,11},{4,12},{5,13},{6,14},{7,15},{8,16},{9,17... | collective-permute-start | bytes 208904 | tf_op jit(solution)/shard_map/ppermute | solution.py:34
  104.9 14.2 %collective-permute-start.19 = (bf16[1024,256]{1,0:T(8,128)(2,1)}, bf16[1024,256]{1,0:T(8,128)(2,1)S(1)}, u32[]{:S(2)}, u32[]{:S(2)}) collective-permute-start(bf16[1024,256]{1,0:T(8,128)(2,1)} %bitcast.6.refs_0_), channel_id=1, source_target_pairs={{0,8},{1,9},{2,10},{3,11},{4,12},{5,13},{6,14},{7,15},{8,16},{9,17... | collective-permute-start | bytes 1572872 | tf_op jit(solution)/shard_map/ppermute | solution.py:34
  119.1 11.0 %collective-permute-start.22 = (bf16[144,256]{1,0:T(8,128)(2,1)S(1)}, bf16[144,256]{1,0:T(8,128)(2,1)S(1)}, u32[]{:S(2)}, u32[]{:S(2)}) collective-permute-start(bf16[144,256]{1,0:T(8,128)(2,1)S(1)} %get-tuple-element.162), channel_id=1, source_target_pairs={{0,8},{1,9},{2,10},{3,11},{4,12},{5,13},{6,14},{7,15},{8,16},{9,17... | collective-permute-start | bytes 221192 | tf_op jit(solution)/shard_map/ppermute | solution.py:34
  122.6 7.5 %collective-permute-start.23 = (bf16[144,256]{1,0:T(8,128)(2,1)S(1)}, bf16[144,256]{1,0:T(8,128)(2,1)S(1)}, u32[]{:S(2)}, u32[]{:S(2)}) collective-permute-start(bf16[144,256]{1,0:T(8,128)(2,1)S(1)} %get-tuple-element.162), channel_id=1, source_target_pairs={{0,16},{1,17},{2,18},{3,19},{4,20},{5,21},{6,22},{7,23},{8,24},{9,... | collective-permute-start | bytes 221192 | tf_op jit(solution)/shard_map/ppermute | solution.py:34
  123.9 6.2 %collective-permute-start.24 = (bf16[144,256]{1,0:T(8,128)(2,1)S(1)}, bf16[144,256]{1,0:T(8,128)(2,1)S(1)}, u32[]{:S(2)}, u32[]{:S(2)}) collective-permute-start(bf16[144,256]{1,0:T(8,128)(2,1)S(1)} %get-tuple-element.162), channel_id=1, source_target_pairs={{0,24},{1,25},{2,26},{3,27},{4,28},{5,29},{6,30},{7,31}} | collective-permute-start | bytes 221192 | tf_op jit(solution)/shard_map/ppermute | solution.py:34
  124.6 15.5 %collective-permute-start.21 = (bf16[1024,256]{1,0:T(8,128)(2,1)}, bf16[1024,256]{1,0:T(8,128)(2,1)S(1)}, u32[]{:S(2)}, u32[]{:S(2)}) collective-permute-start(bf16[1024,256]{1,0:T(8,128)(2,1)} %bitcast.7.refs_2_), channel_id=1, source_target_pairs={{8,0},{9,1},{10,2},{11,3},{12,4},{13,5},{14,6},{15,7},{16,8},{17,9... | collective-permute-start | bytes 1572872 | tf_op jit(solution)/shard_map/ppermute | solution.py:34
  128.0 14.8 %collective-permute-start.20 = (bf16[1024,256]{1,0:T(8,128)(2,1)S(1)}, bf16[1024,256]{1,0:T(8,128)(2,1)}, u32[]{:S(2)}, u32[]{:S(2)}) collective-permute-start(bf16[1024,256]{1,0:T(8,128)(2,1)S(1)} %collective-permute-done.19.refs_0_), channel_id=1, source_target_pairs={{8,16},{9,17},{10,18},{11,19},{12,20},{13,21},{14,22},{15,23},{16,... | collective-permute-start | bytes 1572872 | tf_op jit(solution)/shard_map/ppermute | solution.py:34
  133.2 9.6 %collective-permute-start.25 = (bf16[1024,256]{1,0:T(8,128)(2,1)S(1)}, bf16[1024,256]{1,0:T(8,128)(2,1)S(1)}, u32[]{:S(2)}, u32[]{:S(2)}) collective-permute-start(bf16[1024,256]{1,0:T(8,128)(2,1)S(1)} %collective-permute-done.19.refs_0_), channel_id=1, source_target_pairs={{0,4},{1,5},{2,6},{3,7},{4,0},{5,1},{6,2},{7,3},{8,12},{9,13},{10,... | collective-permute-start | bytes 1572872 | tf_op jit(solution)/shard_map/ppermute | solution.py:34
  133.3 2.5 %collective-permute-start.26 = (bf16[768,256]{1,0:T(8,128)(2,1)S(1)}, bf16[768,256]{1,0:T(8,128)(2,1)S(1)}, u32[]{:S(2)}, u32[]{:S(2)}) collective-permute-start(bf16[768,256]{1,0:T(8,128)(2,1)S(1)} %get-tuple-element.167), channel_id=1, source_target_pairs={{0,4},{1,5},{2,6},{3,7},{4,0},{5,1},{6,2},{7,3},{8,12},{9,13},{10,... | collective-permute-start | bytes 1179656 | tf_op jit(solution)/shard_map/ppermute | solution.py:34
  139.2 12.2 %collective-permute-start.27 = (bf16[192,1024]{1,0:T(8,128)(2,1)S(1)}, bf16[192,1024]{1,0:T(8,128)(2,1)S(1)}, u32[]{:S(2)}, u32[]{:S(2)}) collective-permute-start(bf16[192,1024]{1,0:T(8,128)(2,1)S(1)} %get-tuple-element.175), channel_id=1, source_target_pairs={{0,1},{1,0},{2,3},{3,2},{4,5},{5,4},{6,7},{7,6},{8,9},{9,8},{10,11... | collective-permute-start | bytes 1179656 | tf_op jit(solution)/shard_map/ppermute | solution.py:34
  144.0 2.9 %collective-permute-start.30 = (bf16[512,256]{1,0:T(8,128)(2,1)S(1)}, bf16[512,256]{1,0:T(8,128)(2,1)S(1)}, u32[]{:S(2)}, u32[]{:S(2)}) collective-permute-start(bf16[512,256]{1,0:T(8,128)(2,1)S(1)} %get-tuple-element.185), channel_id=1, source_target_pairs={{0,4},{1,5},{2,6},{3,7},{4,0},{5,1},{6,2},{7,3},{8,12},{9,13},{10,... | collective-permute-start | bytes 786440 | tf_op jit(solution)/shard_map/ppermute | solution.py:34
  144.1 2.8 %collective-permute-start.31 = (bf16[512,256]{1,0:T(8,128)(2,1)S(1)}, bf16[512,256]{1,0:T(8,128)(2,1)S(1)}, u32[]{:S(2)}, u32[]{:S(2)}) collective-permute-start(bf16[512,256]{1,0:T(8,128)(2,1)S(1)} %get-tuple-element.186), channel_id=1, source_target_pairs={{0,4},{1,5},{2,6},{3,7},{4,0},{5,1},{6,2},{7,3},{8,12},{9,13},{10,... | collective-permute-start | bytes 786440 | tf_op jit(solution)/shard_map/ppermute | solution.py:34
  144.6 20.4 %collective-permute-start.28 = (bf16[192,1024]{1,0:T(8,128)(2,1)S(1)}, bf16[192,1024]{1,0:T(8,128)(2,1)S(1)}, u32[]{:S(2)}, u32[]{:S(2)}) collective-permute-start(bf16[192,1024]{1,0:T(8,128)(2,1)S(1)} %get-tuple-element.176), channel_id=1, source_target_pairs={{0,2},{1,3},{2,0},{3,1},{4,6},{5,7},{6,4},{7,5},{8,10},{9,11},{10,... | collective-permute-start | bytes 1179656 | tf_op jit(solution)/shard_map/ppermute | solution.py:34
  145.3 19.7 %collective-permute-start.29 = (bf16[192,1024]{1,0:T(8,128)(2,1)S(1)}, bf16[192,1024]{1,0:T(8,128)(2,1)S(1)}, u32[]{:S(2)}, u32[]{:S(2)}) collective-permute-start(bf16[192,1024]{1,0:T(8,128)(2,1)S(1)} %get-tuple-element.177), channel_id=1, source_target_pairs={{0,3},{1,2},{2,1},{3,0},{4,7},{5,6},{6,5},{7,4},{8,11},{9,10},{10,... | collective-permute-start | bytes 1179656 | tf_op jit(solution)/shard_map/ppermute | solution.py:34
  149.3 18.8 %collective-permute-start.32 = (bf16[192,1024]{1,0:T(8,128)(2,1)S(1)}, bf16[192,1024]{1,0:T(8,128)(2,1)S(1)}, u32[]{:S(2)}, u32[]{:S(2)}) collective-permute-start(bf16[192,1024]{1,0:T(8,128)(2,1)S(1)} %get-tuple-element.182), channel_id=1, source_target_pairs={{0,1},{1,0},{2,3},{3,2},{4,5},{5,4},{6,7},{7,6},{8,9},{9,8},{10,11... | collective-permute-start | bytes 1179656 | tf_op jit(solution)/shard_map/ppermute | solution.py:34
  150.6 30.3 %collective-permute-start.33 = (bf16[192,1024]{1,0:T(8,128)(2,1)S(1)}, bf16[192,1024]{1,0:T(8,128)(2,1)S(1)}, u32[]{:S(2)}, u32[]{:S(2)}) collective-permute-start(bf16[192,1024]{1,0:T(8,128)(2,1)S(1)} %get-tuple-element.183), channel_id=1, source_target_pairs={{0,2},{1,3},{2,0},{3,1},{4,6},{5,7},{6,4},{7,5},{8,10},{9,11},{10,... | collective-permute-start | bytes 1179656 | tf_op jit(solution)/shard_map/ppermute | solution.py:34
  151.4 29.6 %collective-permute-start.34 = (bf16[192,1024]{1,0:T(8,128)(2,1)S(1)}, bf16[192,1024]{1,0:T(8,128)(2,1)S(1)}, u32[]{:S(2)}, u32[]{:S(2)}) collective-permute-start(bf16[192,1024]{1,0:T(8,128)(2,1)S(1)} %get-tuple-element.184), channel_id=1, source_target_pairs={{0,3},{1,2},{2,1},{3,0},{4,7},{5,6},{6,5},{7,4},{8,11},{9,10},{10,... | collective-permute-start | bytes 1179656 | tf_op jit(solution)/shard_map/ppermute | solution.py:34
